TPU v7x, 128 devices: a whole 4x4x4 slice. The times are simulated.
128 devices in a mesh: tm: 32 (over x, z, core), band: 4 (over y).
Axes of the slice: x: 4, y: 4, z: 4, core: 2. Of those that a mesh axis runs over, the one named last changes fastest.
Arguments:
- frames_in: bfloat16 [64, 32, 256, 128], P('tm', 'band'), may hold values from -6 to 6
- clip_id: int32 [64], replicated, may hold values from 0 to 15, never falling along the last dimension, each value on 1 to 16 neighbouring positions
- conv_weight: bfloat16 [3, 3, 3, 128, 128], replicated, may hold values from -0.109375 to 0.109375
- conv_bias: float32 [128], replicated, may hold values from -3 to 3
- norm_gain: float32 [128], replicated, may hold values from 0.1 to 1.9
- norm_shift: float32 [128], replicated, may hold values from -3 to 3
- down_weight: bfloat16 [3, 3, 3, 128, 256], replicated, may hold values from -0.109375 to 0.109375
- out_gain: float32 [256], replicated, may hold values from 0.1 to 1.9
- out_shift: float32 [256], replicated, may hold values from -3 to 3
Outputs:
- encoded: bfloat16 [64, 16, 128, 256], P('tm', 'band')
Inputs may be any that keep to these rules, and one draw needn't show every extreme that they name: `clip_id`: clip numbers never fall along the frames; every clip covers 1 to 16 consecutive frames and one covers exactly 16.
All inputs are finite; a program needn't handle non-finite values.
Results may differ from a plain program's by a relative error of at most 0.011.
Values may be sent and summed in bfloat16 or wider, within the bound.
No kernel may reach another device: no remote copies, remote signals or barrier semaphores. Data moves between devices by JAX's collectives and lax.ppermute only.
A program may use at most 64 MiB of HBM per device.

v0:
```python
import functools
import jax
import jax.numpy as jnp
from jax import lax
from jax.experimental import pallas as pl
from jax.experimental.pallas import tpu as pltpu
from jax.sharding import PartitionSpec as P

GROUPS = 32
EPS = 1e-06
F32 = jnp.float32
BF16 = jnp.bfloat16
VMEM = pl.BlockSpec(memory_space=pltpu.VMEM)
cat = jnp.concatenate


def iota(shape, dim):
    return lax.broadcasted_iota(jnp.int32, shape, dim)


def exact_dot(rows, zero_one):
    n = rows.shape[0]
    high = rows.astype(BF16)
    rest = rows - high.astype(F32)
    middle = rest.astype(BF16)
    low = (rest - middle.astype(F32)).astype(BF16)
    parts = cat([high.astype(F32), middle.astype(F32), low.astype(F32)], axis=0)
    spare = -parts.shape[0] % 16
    if spare:
        parts = cat([parts, jnp.zeros((spare, parts.shape[1]), F32)], axis=0)
    found = jnp.dot(parts.astype(BF16), zero_one.astype(BF16), preferred_element_type=F32)
    return found[:n] + found[n : 2 * n] + found[2 * n : 3 * n]


def pack_row(sums):
    channels = sums[0].shape[1]
    size = channels // GROUPS
    gather = iota((channels, 128), 0) // size == iota((channels, 128), 1) % GROUPS
    grouped = exact_dot(cat(sums, axis=0), gather.astype(F32))
    place = iota((4, 128), 1) // GROUPS == iota((4, 128), 0)
    return jnp.sum(jnp.where(place, grouped, 0.0), axis=0, keepdims=True)


def frame_sums(lines):
    deep = 64
    channels = lines[0].shape[1]
    one, two = jnp.zeros((deep, channels), F32), jnp.zeros((deep, channels), F32)
    for v in lines:
        for a in range(0, v.shape[0], deep):
            part = v[a : a + deep]
            one, two = one + part, two + part * part
    return [jnp.sum(one, axis=0, keepdims=True), jnp.sum(two, axis=0, keepdims=True)]


def scale_and_shift(rows, info_ref, gain, offset, cells, bands):
    channels = gain.shape[1]
    size = channels // GROUPS
    frame = 2 * (iota(rows.shape, 0) // bands) + iota(rows.shape, 1) // 64
    lane, channel = iota((128, 2 * channels), 0) % 64, iota((128, 2 * channels), 1)
    spread = lane == GROUPS * (channel // channels) + channel % channels // size
    totals = []
    for n in range(2):
        begin, end = info_ref[n : n + 1, :], info_ref[4 + n : 5 + n, :]
        inside = jnp.where((frame >= begin) & (frame < end), rows, 0.0)
        totals.append(jnp.sum(inside, axis=0, keepdims=True))
    sums = exact_dot(cat(totals, axis=0), spread.astype(F32))
    found = []
    for n in range(2):
        frames = (info_ref[4 + n : 5 + n, :] - info_ref[n : n + 1, :]).astype(F32)
        per = 1.0 / (cat([frames] * (channels // 128), axis=1) * cells)
        mean = sums[n : n + 1, :channels] * per
        inv_std = lax.rsqrt(sums[n : n + 1, channels:] * per - mean * mean + EPS)
        scale = inv_std * gain
        found.append((scale, offset - mean * scale))
    return found


def sums_kernel(x_ref, row_ref):
    sums = []
    for f in range(x_ref.shape[0]):
        sums += frame_sums([x_ref[f, r].astype(F32) for r in range(x_ref.shape[1])])
    row_ref[...] = jnp.broadcast_to(pack_row(sums)[None], row_ref.shape)


def setup_kernel(
    clip_ref, weight_ref, bias_ref, gain_ref, offset_ref, out_gain_ref, out_offset_ref,
    weights_ref, info_ref, vectors_ref,
):
    channels = bias_ref.shape[1]
    zero = jnp.zeros((channels, channels), BF16)
    for tap in range(9):
        w0, w1, w2 = (weight_ref[tap, dx] for dx in range(3))
        weights_ref[tap, 0:channels] = cat([w1, w0, zero, w2], axis=1)
        weights_ref[tap, channels : 2 * channels] = cat([w2, w1, w0, zero], axis=1)
    ids = clip_ref[...].astype(F32)
    lane = iota(ids.shape, 1)
    first = lax.axis_index("tm") * 2
    begins, ends = [], []
    for n in range(4):
        at = jnp.minimum(first + n, ids.shape[1] - 1)
        mine = jnp.sum(jnp.where(lane == at, ids, 0.0), axis=1, keepdims=True)
        begins.append(jnp.sum(jnp.where(ids < mine, 1.0, 0.0), axis=1, keepdims=True))
        ends.append(jnp.sum(jnp.where(ids <= mine, 1.0, 0.0), axis=1, keepdims=True))
    table = cat([jnp.broadcast_to(v, (1, 128)) for v in begins + ends], axis=0)
    info_ref[...] = table.astype(jnp.int32)
    blank = jnp.zeros((1, channels), F32)
    vectors_ref[...] = cat(
        [cat([ref[...], blank], axis=1) for ref in (bias_ref, gain_ref, offset_ref)]
        + [out_gain_ref[...], out_offset_ref[...], jnp.zeros((3, 2 * channels), F32)],
        axis=0,
    )


def edges_kernel(before_ref, x_ref, top_ref, bottom_ref):
    rows = x_ref.shape[1]
    for f in range(4):
        source = before_ref if f < 2 else x_ref
        top_ref[f] = source[f % 2, 0:2]
        bottom_ref[f, 0] = source[f % 2, rows - 1]


def activate(value, slot, scale, shift, hidden_at, own_at=None, keep=None):
    cols, channels = value.shape
    slot[...] = value.astype(F32)
    for side in range(2):
        lanes = pl.ds(side * channels, channels)
        part = slot[pl.ds(side, cols // 2, 2), :]
        if own_at is not None:
            own_at[:, lanes] = part.astype(BF16)
        u = part * scale + shift
        h = u + u * jnp.tanh(u)
        if keep is not None:
            h = h * keep
        hidden_at[:, lanes] = h.astype(BF16)


def convolve(line, weights_ref, outputs):
    weights = weights_ref[...].reshape(-1, weights_ref.shape[2])
    window = cat(
        [
            cat([line(sources[k], r + dy) for sources, r in outputs], axis=0)
            for k in range(3)
            for dy in (-1, 0, 1)
        ],
        axis=1,
    )
    found = jnp.dot(window, weights, preferred_element_type=F32)
    wide = found.shape[1] // 2
    channels = wide // 2
    size = found.shape[0]
    half = size // len(outputs)
    column = iota((size, channels), 0) % half
    from_left = jnp.where(column == 0, 0.0, pltpu.roll(found[:, wide : wide + channels], 1, 0))
    from_right = jnp.where(column == half - 1, 0.0, pltpu.roll(found[:, wide + channels :], size - 1, 0))
    total = found[:, :wide] + cat([from_left, from_right], axis=1)
    return [total[n * half : (n + 1) * half] for n in range(len(outputs))]


def strided(lines, down_ref, k):
    wide = down_ref.shape[1]
    channels = down_ref.shape[0] // 27
    windows = [lines(dy) for dy in range(3)]
    half = windows[0].shape[1]
    windows = [w.reshape(-1, wide) for w in windows]
    places = [(k * 9 + dy * 3) * channels for dy in range(3)]
    both = cat([down_ref[at : at + 2 * channels] for at in places], axis=0)
    next_even = cat([down_ref[at + 2 * channels : at + 3 * channels] for at in places], axis=0)
    total = jnp.dot(cat(windows, axis=1), both, preferred_element_type=F32)
    shifted = jnp.dot(
        cat([w[:, :channels] for w in windows], axis=1), next_even, preferred_element_type=F32
    )
    size = total.shape[0]
    column = iota(shifted.shape, 0) % half
    shifted = jnp.where(column == half - 1, 0.0, pltpu.roll(shifted, size - 1, 0))
    return (total + shifted).reshape(-1, half, wide)


def hand_on(line, outputs, info_ref, first, down_ref, partial_ref):
    begins = [info_ref[2, 0], info_ref[3, 0]]
    source = (begins[0] > first).astype(jnp.int32)
    takes = [(b <= first + 1).astype(F32) for b in begins]

    def both(dy):
        return jnp.stack([line(f, 2 * i + dy) for f in (source, 1) for i in outputs])

    def second(dy):
        return jnp.stack([line(1, 2 * i + dy) for i in outputs])

    n = len(outputs)
    older = strided(both, down_ref, 0)
    newer = strided(second, down_ref, 1)
    partial_ref[0] = ((older[:n] + newer) * takes[0]).astype(BF16)
    partial_ref[1] = (older[n:] * takes[1]).astype(BF16)


def frame_sources(info_ref, first):
    return [
        [jnp.maximum(first + f - 2 + k, info_ref[f, 0]) - (first - 2) for k in range(3)] for f in range(2)
    ]


def inner_kernel(
    bands, cells, rows_ref, info_ref, vectors_ref, x_ref, before_ref, weights_ref, down_ref,
    hidden_ref, stats_ref, residual_ref, partial_ref, own, slots,
):
    frames, rows, cols, channels = x_ref.shape
    first = lax.axis_index("tm") * frames
    bias, gain, offset = (vectors_ref[n : n + 1, :channels] for n in range(3))
    stats = scale_and_shift(rows_ref[...], info_ref, gain, offset, cells, bands)
    stats = [(0.5 * scale, 0.5 * shift) for scale, shift in stats]
    stats_ref[...] = cat([v for pair in stats for v in pair] + [jnp.zeros((4, channels), F32)], axis=0)
    for frame in range(4):
        scale, shift = stats[1 if frame == 3 else 0]
        for r in range(rows):
            activate(
                (before_ref if frame < 2 else x_ref)[frame % 2, r],
                slots.at[r],
                scale,
                shift,
                hidden_ref.at[frame, r],
                own.at[frame - 2, r - 1] if frame >= 2 and 0 < r < rows - 1 else None,
            )
    sources = frame_sources(info_ref, first)
    outputs = [(f, r) for f in range(frames) for r in range(1, rows - 1)]
    found = convolve(
        lambda source, r: hidden_ref[source, r], weights_ref, [(sources[f], r) for f, r in outputs]
    )
    bias = cat([bias, bias], axis=1)
    for (f, r), total in zip(outputs, found):
        residual_ref[f, r - 1] = (total + own[f, r - 1].astype(F32) + bias).astype(BF16)
    hand_on(lambda f, r: residual_ref[f, r - 1], (1, 2), info_ref, first, down_ref, partial_ref)


def edge_kernel(
    bands, info_ref, vectors_ref, stats_ref, x_ref, hidden_ref, above_ref, below_ref, inner_ref,
    weights_ref, down_ref, residual_ref, partial_ref, rim, own, slots,
):
    frames, rows, cols, channels = x_ref.shape
    first = lax.axis_index("tm") * frames
    band = lax.axis_index("band")
    keep_above = (band > 0).astype(F32)
    keep_below = (band < bands - 1).astype(F32)
    for frame in range(4):
        n = 2 if frame == 3 else 0
        scale, shift = stats_ref[n : n + 1, :], stats_ref[n + 1 : n + 2, :]
        owned = own.at[frame - 2, 2] if frame >= 2 else None
        activate(above_ref[frame, 0], slots.at[0], scale, shift, rim.at[frame, 0], None, keep_above)
        activate(below_ref[frame, 0], slots.at[1], scale, shift, rim.at[frame, 1], owned, keep_below)
        activate(below_ref[frame, 1], slots.at[2], scale, shift, rim.at[frame, 2], None, keep_below)
    for f in range(frames):
        for n, r in enumerate((0, rows - 1)):
            slots[3 + n] = x_ref[f, r].astype(F32)
            for side in range(2):
                own[f, n, :, pl.ds(side * channels, channels)] = slots[
                    3 + n, pl.ds(side, cols // 2, 2), :
                ].astype(BF16)

    def line(source, r):
        if r < 0:
            return rim[source, 0]
        return hidden_ref[source, r] if r < rows else rim[source, 1 + r - rows]

    sources = frame_sources(info_ref, first)
    outputs = [(f, r) for f in range(frames) for r in (0, rows - 1, rows)]
    found = convolve(line, weights_ref, [(sources[f], r) for f, r in outputs])
    bias = vectors_ref[0:1, :channels]
    bias = cat([bias, bias], axis=1)
    for n, total in enumerate(found):
        f, place = n // 3, n % 3
        value = total + own[f, place].astype(F32) + bias
        if place == 2:
            value = value * keep_below
        residual_ref[f, place] = value.astype(BF16)
    hand_on(
        lambda f, r: residual_line(inner_ref, residual_ref, rows, f, r),
        (0, rows // 2 - 1), info_ref, first, down_ref, partial_ref,
    )


def residual_line(inner_ref, edge_ref, rows, f, r):
    if 0 < r < rows - 1:
        return inner_ref[f, r - 1]
    return edge_ref[f, 0 if r == 0 else r - rows + 2]


def local_kernel(rows, info_ref, inner_ref, edge_ref, down_ref, out_ref):
    first = lax.axis_index("tm") * 2
    begins = [info_ref[0, 0], info_ref[1, 0]]

    def lines(*picked):
        return lambda dy: jnp.stack(
            [residual_line(inner_ref, edge_ref, rows, f, 2 * i + dy) for f in picked for i in range(rows // 2)]
        )

    base = strided(lines(0, 1), down_ref, 2)
    out_ref[0] = base[: rows // 2]
    out_ref[1] = base[rows // 2 :] + strided(lines((begins[1] > first).astype(jnp.int32)), down_ref, 1)

    @pl.when(begins[0] == first)
    def _():
        out_ref[0] += strided(lines(0), down_ref, 0) + strided(lines(0), down_ref, 1)

    @pl.when(begins[1] >= first)
    def _():
        out_ref[1] += strided(lines(begins[1] - first), down_ref, 0)


def join_kernel(local_ref, inner_ref, edge_ref, reduced_ref, row_ref):
    frames, lines, half, channels = local_ref.shape
    sums = []
    for f in range(frames):
        values = []
        for i in range(lines):
            sent = inner_ref[f, i - 1] if 0 < i < lines - 1 else edge_ref[f, min(i, 1)]
            v = (local_ref[f, i] + sent.astype(F32)).astype(BF16)
            reduced_ref[f, i] = v
            values.append(v.astype(F32))
        sums += frame_sums(values)
    row_ref[...] = jnp.broadcast_to(pack_row(sums)[None], row_ref.shape)


def out_kernel(bands, cells, rows_ref, info_ref, vectors_ref, reduced_ref, out_ref):
    frames, lines = reduced_ref.shape[:2]
    stats = scale_and_shift(
        rows_ref[...], info_ref, vectors_ref[3:4, :], vectors_ref[4:5, :], cells, bands
    )
    for f in range(frames):
        scale, shift = stats[f]
        for i in range(lines):
            out_ref[f, i] = (reduced_ref[f, i].astype(F32) * scale + shift).astype(BF16)


def call(kernel, out_shape, in_specs, scratch=(), megabytes=4, flops=0, moved=0):
    return pl.pallas_call(
        kernel,
        out_shape=out_shape,
        in_specs=in_specs,
        out_specs=jax.tree.map(lambda _: VMEM, out_shape),
        scratch_shapes=list(scratch),
        compiler_params=pltpu.CompilerParams(vmem_limit_bytes=megabytes << 20),
        cost_estimate=pl.CostEstimate(flops=flops, bytes_accessed=moved, transcendentals=0),
    )


def passed_on(array, axis, by):
    peers = lax.axis_size(axis)
    pairs = [(i, i + by) for i in range(peers) if 0 <= i + by < peers]
    return lax.ppermute(array, axis, pairs)


def on_device(
    frames_in, clip_id, conv_weight, conv_bias, norm_gain, norm_shift, down_weight, out_gain, out_shift
):
    frames, rows, cols, channels = frames_in.shape
    wide = down_weight.shape[-1]
    bands = lax.axis_size("band")
    devices, half, lines = lax.axis_size("tm") * bands, cols // 2, rows // 2
    shape = jax.ShapeDtypeStruct
    everyone = shape((devices, 1, 128), F32)

    def exchange(row):
        return lax.all_to_all(row, ("tm", "band"), 0, 0, tiled=True).reshape(devices, 128)

    before = passed_on(frames_in, "tm", 1)
    row = call(sums_kernel, everyone, [VMEM], flops=1 << 33, moved=1 << 20)(frames_in)
    weights, info, vectors = call(
        setup_kernel,
        (
            shape((9, 2 * channels, 4 * channels), BF16),
            shape((8, 128), jnp.int32),
            shape((8, wide), F32),
        ),
        [VMEM] * 7,
        megabytes=8,
        flops=1 << 32,
        moved=1 << 22,
    )(
        clip_id.reshape(1, -1), conv_weight.reshape(9, 3, channels, channels), conv_bias.reshape(1, -1),
        norm_gain.reshape(1, -1), norm_shift.reshape(1, -1), out_gain.reshape(1, -1), out_shift.reshape(1, -1),
    )
    down = down_weight.reshape(-1, wide)
    sums = exchange(row)
    top, bottom = call(
        edges_kernel,
        (shape((4, 2, cols, channels), BF16), shape((4, 1, cols, channels), BF16)),
        [VMEM] * 2,
        flops=1 << 33,
        moved=1 << 20,
        megabytes=8,
    )(before, frames_in)
    below, above = passed_on(top, "band", -1), passed_on(bottom, "band", 1)
    hidden, stats, inner, inner_partial = call(
        functools.partial(inner_kernel, bands, float(bands * rows * cols * (channels // GROUPS))),
        (
            shape((4, rows, half, 2 * channels), BF16),
            shape((8, channels), F32),
            shape((frames, rows - 2, half, 2 * channels), BF16),
            shape((frames, lines - 2, half, wide), BF16),
        ),
        [VMEM] * 7,
        scratch=[
            pltpu.VMEM((frames, rows - 2, half, 2 * channels), BF16),
            pltpu.VMEM((rows, cols, channels), F32),
        ],
        megabytes=24,
        flops=5 << 30,
        moved=1 << 23,
    )(sums, info, vectors, frames_in, before, weights, down)
    inner_arrived = passed_on(inner_partial, "tm", 1)
    edge, edge_partial = call(
        functools.partial(edge_kernel, bands),
        (
            shape((frames, 3, half, 2 * channels), BF16),
            shape((frames, 2, half, wide), BF16),
        ),
        [VMEM] * 10,
        scratch=[
            pltpu.VMEM((4, 3, half, 2 * channels), BF16),
            pltpu.VMEM((frames, 3, half, 2 * channels), BF16),
            pltpu.VMEM((5, cols, channels), F32),
        ],
        megabytes=24,
        flops=2 << 30,
        moved=1 << 22,
    )(info, vectors, stats, frames_in, hidden, above, below, inner, weights, down)
    edge_arrived = passed_on(edge_partial, "tm", 1)
    local = call(
        functools.partial(local_kernel, rows),
        shape((frames, lines, half, wide), F32),
        [VMEM] * 4,
        megabytes=16,
        flops=1 << 31,
        moved=1 << 22,
    )(info, inner, edge, down)
    reduced, row = call(
        join_kernel,
        (shape((frames, lines, half, wide), BF16), everyone),
        [VMEM] * 3,
        megabytes=8,
        moved=1 << 21,
    )(local, inner_arrived, edge_arrived)
    return call(
        functools.partial(out_kernel, bands, float(bands * lines * half * (wide // GROUPS))),
        shape((frames, lines, half, wide), BF16),
        [VMEM] * 4,
        megabytes=8,
        moved=1 << 20,
    )(exchange(row), info, vectors, reduced)


def solution(mesh):
    return jax.shard_map(
        on_device,
        mesh=mesh,
        in_specs=(P("tm", "band", None, None), P(), P(), P(), P(), P(), P(), P(), P()),
        out_specs=P("tm", "band", None, None),
        check_vma=False,
    )
```

profile of v0, /device:TPU:1, one launch (start us, length us, event | category | flops | bytes accessed | tf_op | source)
XLA Modules:
  0.0 70.9 jit_solution(10583641014472576675)
XLA Ops:
  0.0 4.9 %collective-permute-start = (bf16[2,8,256,128]{3,2,1,0:T(8,128)(2,1)}, bf16[2,8,256,128]{3,2,1,0:T(8,128)(2,1)S(1)}, u32[]{:S(2)}, u32[]{:S(2)}) collective-permute-start(bf16[2,8,256,128]{3,2,1,0:T(8,128)(2,1)} %x_ref.7), channel_id=1, source_target_pairs={{0,4},{4,8},{8,12},{12,16},{16,20},{20,24},{24,28},{28,32},{32,36}... | collective-permute-start | bytes 3145736 | tf_op jit(solution)/shard_map/ppermute | solution.py:348
  4.9 0.0 copy-start.1
  4.9 1.2 %copy-done.1 = bf16[2,8,256,128]{3,2,1,0:T(8,128)(2,1)S(1)} copy-done((bf16[2,8,256,128]{3,2,1,0:T(8,128)(2,1)S(1)}, bf16[2,8,256,128]{3,2,1,0:T(8,128)(2,1)}, u32[]{:S(2)}) %copy-start.1) | copy-done | bytes 1048600
  6.2 0.0 copy-start.2
  6.2 1.0 %shard_map.92 = f32[128,1,128]{2,1,0:T(1,128)} custom-call(bf16[2,8,256,128]{3,2,1,0:T(8,128)(2,1)S(1)} %copy-done.1), custom_call_target="tpu_custom_call" | custom-call | flops 8589934592 | bytes 1048576 | tf_op jit(solution)/shard_map/pallas_call | solution.py:365
  7.1 9.7 %all-to-all-start = ((f32[128,1,128]{2,1,0:T(1,128)}), f32[128,1,128]{2,1,0:T(1,128)S(1)}, u32[]{:S(2)}, u32[]{:S(2)}) async-start(f32[128,1,128]{2,1,0:T(1,128)} %shard_map.92), calls=%async_computation | async-start | bytes 131072 | tf_op jit(solution)/shard_map/all_to_all | solution.py:362
  16.8 0.0 copy-start.5
  16.8 0.0 copy-start.6
  16.8 0.0 copy-start.7
  16.8 0.0 copy-start.8
  16.8 0.0 copy-start.9
  16.9 0.0 copy-start.10
  16.9 0.0 copy-start.11
  16.9 0.1 collective-permute-done.before_ref
  17.0 0.0 copy-done.2
  17.0 0.0 copy-start.3
  17.0 0.9 %shard_map.94 = (bf16[4,2,256,128]{3,2,1,0:T(8,128)(2,1)}, bf16[4,1,256,128]{3,2,1,0:T(8,128)(2,1)}) custom-call(bf16[2,8,256,128]{3,2,1,0:T(8,128)(2,1)S(1)} %collective-permute-done.before_ref, bf16[2,8,256,128]{3,2,1,0:T(8,128)(2,1)S(1)} %copy-done.2), custom_call_target="tpu_custom_call" | custom-call | flops 8589934592 | bytes 1048576 | tf_op jit(solution)/shard_map/pallas_call | solution.py:383
  17.9 0.3 copy-done.3
  18.2 1.3 %collective-permute-start.2 = (bf16[4,2,256,128]{3,2,1,0:T(8,128)(2,1)}, bf16[4,2,256,128]{3,2,1,0:T(8,128)(2,1)}, u32[]{:S(2)}, u32[]{:S(2)}) collective-permute-start(bf16[4,2,256,128]{3,2,1,0:T(8,128)(2,1)} %get-tuple-element.25), channel_id=1, source_target_pairs={{1,0},{2,1},{3,2},{5,4},{6,5},{7,6},{9,8},{10,9},{11,10},{13,12},{... | collective-permute-start | bytes 1572872 | tf_op jit(solution)/shard_map/ppermute | solution.py:348
  19.5 0.0 copy-done.5
  19.5 0.0 copy-done.6
  19.5 0.0 copy-done.7
  19.5 0.0 copy-done.8
  19.6 0.0 copy-done.9
  19.6 0.0 copy-done.10
  19.6 0.0 copy-done.11
  19.6 0.2 shard_map.91
  19.8 4.7 %collective-permute-start.1 = (bf16[4,1,256,128]{3,2,1,0:T(8,128)(2,1)}, bf16[4,1,256,128]{3,2,1,0:T(8,128)(2,1)}, u32[]{:S(2)}, u32[]{:S(2)}) collective-permute-start(bf16[4,1,256,128]{3,2,1,0:T(8,128)(2,1)} %get-tuple-element.24), channel_id=1, source_target_pairs={{0,1},{1,2},{2,3},{4,5},{5,6},{6,7},{8,9},{9,10},{10,11},{12,13},{... | collective-permute-start | bytes 786440 | tf_op jit(solution)/shard_map/ppermute | solution.py:348
  24.5 2.1 %all-to-all-done = f32[128,1,128]{2,1,0:T(1,128)S(1)} async-done(((f32[128,1,128]{2,1,0:T(1,128)}), f32[128,1,128]{2,1,0:T(1,128)S(1)}, u32[]{:S(2)}, u32[]{:S(2)}) %all-to-all-start) | async-done | bytes 65568 | tf_op jit(solution)/shard_map/all_to_all | solution.py:362
  26.7 0.0 copy-start
  26.7 1.5 %copy-done = bf16[3,3,3,128,256]{4,3,2,1,0:T(8,128)(2,1)S(1)} copy-done((bf16[3,3,3,128,256]{4,3,2,1,0:T(8,128)(2,1)S(1)}, bf16[3,3,3,128,256]{4,3,2,1,0:T(8,128)(2,1)}, u32[]{:S(2)}) %copy-start) | copy-done | bytes 1769496
  28.1 0.0 copy-start.4
  28.2 1.2 %copy-done.4 = bf16[2,8,256,128]{3,2,1,0:T(8,128)(2,1)S(1)} copy-done((bf16[2,8,256,128]{3,2,1,0:T(8,128)(2,1)S(1)}, bf16[2,8,256,128]{3,2,1,0:T(8,128)(2,1)}, u32[]{:S(2)}) %copy-start.4) | copy-done | bytes 1048600
  29.4 6.0 %shard_map.93 = (bf16[4,8,128,256]{3,2,1,0:T(8,128)(2,1)S(1)}, f32[8,128]{1,0:T(8,128)S(1)}, bf16[2,6,128,256]{3,2,1,0:T(8,128)(2,1)S(1)}, bf16[2,2,128,256]{3,2,1,0:T(8,128)(2,1)S(1)}) custom-call(f32[128,128]{1,0:T(8,128)S(1)} %bitcast.14, s32[8,128]{1,0:T(8,128)S(1)} %get-tuple-element.18.info_ref, f32[8,256]{1,0:T(8,128)S(1)} %get-tuple-element.19.vectors_ref, ...), custom_call_target="tpu_custom_call" | custom-call | flops 5368709120 | bytes 8388608 | tf_op jit(solution)/shard_map/pallas_call | solution.py:392
  35.4 2.7 %collective-permute-start.3 = (bf16[2,2,128,256]{3,2,1,0:T(8,128)(2,1)S(1)}, bf16[2,2,128,256]{3,2,1,0:T(8,128)(2,1)S(1)}, u32[]{:S(2)}, u32[]{:S(2)}) collective-permute-start(bf16[2,2,128,256]{3,2,1,0:T(8,128)(2,1)S(1)} %get-tuple-element.27), channel_id=1, source_target_pairs={{0,4},{4,8},{8,12},{12,16},{16,20},{20,24},{24,28},{28,32},{32,36}... | collective-permute-start | bytes 786440 | tf_op jit(solution)/shard_map/ppermute | solution.py:348
  38.1 0.0 collective-permute-done.1.above_ref
  38.1 0.0 collective-permute-done.2.below_ref
  38.1 4.5 %shard_map.95 = (bf16[2,3,128,256]{3,2,1,0:T(8,128)(2,1)S(1)}, bf16[2,2,128,256]{3,2,1,0:T(8,128)(2,1)S(1)}) custom-call(s32[8,128]{1,0:T(8,128)S(1)} %get-tuple-element.18.info_ref, f32[8,256]{1,0:T(8,128)S(1)} %get-tuple-element.19.vectors_ref, f32[8,128]{1,0:T(8,128)S(1)} %get-tuple-element.22.stats_ref, bf16[2,8,256,128]{3,2,1,0:T(8,128)(2,1)S(1)} %copy-done.2, ...), custom_call_target="tpu_custom_call" | custom-call | flops 2147483648 | bytes 4194304 | tf_op jit(solution)/shard_map/pallas_call | solution.py:410
  42.6 1.9 %collective-permute-start.4 = (bf16[2,2,128,256]{3,2,1,0:T(8,128)(2,1)S(1)}, bf16[2,2,128,256]{3,2,1,0:T(8,128)(2,1)S(1)}, u32[]{:S(2)}, u32[]{:S(2)}) collective-permute-start(bf16[2,2,128,256]{3,2,1,0:T(8,128)(2,1)S(1)} %get-tuple-element.28), channel_id=1, source_target_pairs={{0,4},{4,8},{8,12},{12,16},{16,20},{20,24},{24,28},{28,32},{32,36}... | collective-permute-start | bytes 786440 | tf_op jit(solution)/shard_map/ppermute | solution.py:348
  44.6 2.6 %shard_map.96.local_ref = f32[2,4,128,256]{3,2,1,0:T(8,128)S(1)} custom-call(s32[8,128]{1,0:T(8,128)S(1)} %get-tuple-element.18.info_ref, bf16[2,6,128,256]{3,2,1,0:T(8,128)(2,1)S(1)} %get-tuple-element.21.inner_ref, bf16[2,3,128,256]{3,2,1,0:T(8,128)(2,1)S(1)} %get-tuple-element.26.edge_ref, bf16[3456,256]{1,0:T(8,128)(2,1)S(1)} %bitcast.12), custom_call_target="tpu_custom_call" | custom-call | flops 2147483648 | bytes 4194304 | tf_op jit(solution)/shard_map/pallas_call | solution.py:427
  47.2 0.0 collective-permute-done.3.inner_ref
  47.2 0.7 collective-permute-done.4.edge_ref
  47.9 0.4 shard_map.97
  48.3 21.5 %all_to_all.10 = f32[128,1,128]{2,1,0:T(1,128)S(1)} all-to-all(f32[128,1,128]{2,1,0:T(1,128)S(1)} %get-tuple-element.29), channel_id=1, replica_groups=mesh['tm'=32,'band'=4] {'tm','band'}, dimensions={0} | all-to-all | bytes 131072 | tf_op jit(solution)/shard_map/all_to_all | solution.py:362
  69.8 1.1 %shard_map.98 = bf16[2,4,128,256]{3,2,1,0:T(8,128)(2,1)} custom-call(f32[128,128]{1,0:T(8,128)S(1)} %bitcast.13, s32[8,128]{1,0:T(8,128)S(1)} %get-tuple-element.18.info_ref, f32[8,256]{1,0:T(8,128)S(1)} %get-tuple-element.19.vectors_ref, bf16[2,4,128,256]{3,2,1,0:T(8,128)(2,1)S(1)} %get-tuple-element.30.reduced_ref), custom_call_target="tpu_custom_call" | custom-call | bytes 1048576 | tf_op jit(solution)/shard_map/pallas_call | solution.py:442
Async XLA Ops:
  0.0 17.0 %collective-permute-start = (bf16[2,8,256,128]{3,2,1,0:T(8,128)(2,1)}, bf16[2,8,256,128]{3,2,1,0:T(8,128)(2,1)S(1)}, u32[]{:S(2)}, u32[]{:S(2)}) collective-permute-start(bf16[2,8,256,128]{3,2,1,0:T(8,128)(2,1)} %x_ref.7), channel_id=1, source_target_pairs={{0,4},{4,8},{8,12},{12,16},{16,20},{20,24},{24,28},{28,32},{32,36}... | collective-permute-start | bytes 3145736 | tf_op jit(solution)/shard_map/ppermute | solution.py:348
  4.9 1.2 %copy-start.1 = (bf16[2,8,256,128]{3,2,1,0:T(8,128)(2,1)S(1)}, bf16[2,8,256,128]{3,2,1,0:T(8,128)(2,1)}, u32[]{:S(2)}) copy-start(bf16[2,8,256,128]{3,2,1,0:T(8,128)(2,1)} %x_ref.7) | copy-start | bytes 3145732
  6.2 10.8 %copy-start.2 = (bf16[2,8,256,128]{3,2,1,0:T(8,128)(2,1)S(1)}, bf16[2,8,256,128]{3,2,1,0:T(8,128)(2,1)}, u32[]{:S(2)}) copy-start(bf16[2,8,256,128]{3,2,1,0:T(8,128)(2,1)} %x_ref.7) | copy-start | bytes 3145732
  7.1 19.5 %all-to-all-start = ((f32[128,1,128]{2,1,0:T(1,128)}), f32[128,1,128]{2,1,0:T(1,128)S(1)}, u32[]{:S(2)}, u32[]{:S(2)}) async-start(f32[128,1,128]{2,1,0:T(1,128)} %shard_map.92), calls=%async_computation | async-start | bytes 131072 | tf_op jit(solution)/shard_map/all_to_all | solution.py:362
  16.8 2.7 %copy-start.5 = (bf16[3,3,3,128,128]{4,3,2,1,0:T(8,128)(2,1)S(1)}, bf16[3,3,3,128,128]{4,3,2,1,0:T(8,128)(2,1)}, u32[]{:S(2)}) copy-start(bf16[3,3,3,128,128]{4,3,2,1,0:T(8,128)(2,1)} %param.11) | copy-start | bytes 2654212
  16.8 2.7 %copy-start.6 = (f32[256]{0:T(256)S(1)}, f32[256]{0:T(256)}, u32[]{:S(2)}) copy-start(f32[256]{0:T(256)} %param.16) | copy-start | bytes 3076
  16.8 2.7 %copy-start.7 = (f32[256]{0:T(256)S(1)}, f32[256]{0:T(256)}, u32[]{:S(2)}) copy-start(f32[256]{0:T(256)} %param.17) | copy-start | bytes 3076
  16.8 2.7 %copy-start.8 = (s32[64]{0:T(128)S(1)}, s32[64]{0:T(128)}, u32[]{:S(2)}) copy-start(s32[64]{0:T(128)} %param.10) | copy-start | bytes 772
  16.8 2.7 %copy-start.9 = (f32[128]{0:T(128)S(1)}, f32[128]{0:T(128)}, u32[]{:S(2)}) copy-start(f32[128]{0:T(128)} %param.12) | copy-start | bytes 1540
  16.9 2.7 %copy-start.10 = (f32[128]{0:T(128)S(1)}, f32[128]{0:T(128)}, u32[]{:S(2)}) copy-start(f32[128]{0:T(128)} %param.13) | copy-start | bytes 1540
  16.9 2.7 %copy-start.11 = (f32[128]{0:T(128)S(1)}, f32[128]{0:T(128)}, u32[]{:S(2)}) copy-start(f32[128]{0:T(128)} %param.14) | copy-start | bytes 1540
  17.0 1.3 %copy-start.3 = (bf16[2,8,256,128]{3,2,1,0:T(8,128)(2,1)}, bf16[2,8,256,128]{3,2,1,0:T(8,128)(2,1)S(1)}, u32[]{:S(2)}) copy-start(bf16[2,8,256,128]{3,2,1,0:T(8,128)(2,1)S(1)} %collective-permute-done.before_ref) | copy-start | bytes 3145732
  18.2 19.9 %collective-permute-start.2 = (bf16[4,2,256,128]{3,2,1,0:T(8,128)(2,1)}, bf16[4,2,256,128]{3,2,1,0:T(8,128)(2,1)}, u32[]{:S(2)}, u32[]{:S(2)}) collective-permute-start(bf16[4,2,256,128]{3,2,1,0:T(8,128)(2,1)} %get-tuple-element.25), channel_id=1, source_target_pairs={{1,0},{2,1},{3,2},{5,4},{6,5},{7,6},{9,8},{10,9},{11,10},{13,12},{... | collective-permute-start | bytes 1572872 | tf_op jit(solution)/shard_map/ppermute | solution.py:348
  19.8 18.3 %collective-permute-start.1 = (bf16[4,1,256,128]{3,2,1,0:T(8,128)(2,1)}, bf16[4,1,256,128]{3,2,1,0:T(8,128)(2,1)}, u32[]{:S(2)}, u32[]{:S(2)}) collective-permute-start(bf16[4,1,256,128]{3,2,1,0:T(8,128)(2,1)} %get-tuple-element.24), channel_id=1, source_target_pairs={{0,1},{1,2},{2,3},{4,5},{5,6},{6,7},{8,9},{9,10},{10,11},{12,13},{... | collective-permute-start | bytes 786440 | tf_op jit(solution)/shard_map/ppermute | solution.py:348
  26.7 1.5 %copy-start = (bf16[3,3,3,128,256]{4,3,2,1,0:T(8,128)(2,1)S(1)}, bf16[3,3,3,128,256]{4,3,2,1,0:T(8,128)(2,1)}, u32[]{:S(2)}) copy-start(bf16[3,3,3,128,256]{4,3,2,1,0:T(8,128)(2,1)} %param.15) | copy-start | bytes 5308420
  28.1 1.2 %copy-start.4 = (bf16[2,8,256,128]{3,2,1,0:T(8,128)(2,1)S(1)}, bf16[2,8,256,128]{3,2,1,0:T(8,128)(2,1)}, u32[]{:S(2)}) copy-start(bf16[2,8,256,128]{3,2,1,0:T(8,128)(2,1)} %copy-done.3) | copy-start | bytes 3145732
  35.4 11.8 %collective-permute-start.3 = (bf16[2,2,128,256]{3,2,1,0:T(8,128)(2,1)S(1)}, bf16[2,2,128,256]{3,2,1,0:T(8,128)(2,1)S(1)}, u32[]{:S(2)}, u32[]{:S(2)}) collective-permute-start(bf16[2,2,128,256]{3,2,1,0:T(8,128)(2,1)S(1)} %get-tuple-element.27), channel_id=1, source_target_pairs={{0,4},{4,8},{8,12},{12,16},{16,20},{20,24},{24,28},{28,32},{32,36}... | collective-permute-start | bytes 786440 | tf_op jit(solution)/shard_map/ppermute | solution.py:348
  42.6 5.2 %collective-permute-start.4 = (bf16[2,2,128,256]{3,2,1,0:T(8,128)(2,1)S(1)}, bf16[2,2,128,256]{3,2,1,0:T(8,128)(2,1)S(1)}, u32[]{:S(2)}, u32[]{:S(2)}) collective-permute-start(bf16[2,2,128,256]{3,2,1,0:T(8,128)(2,1)S(1)} %get-tuple-element.28), channel_id=1, source_target_pairs={{0,4},{4,8},{8,12},{12,16},{16,20},{20,24},{24,28},{28,32},{32,36}... | collective-permute-start | bytes 786440 | tf_op jit(solution)/shard_map/ppermute | solution.py:348
where the time goes:
time: 71.3 us; the launch traced here: 70.9 us
  starting transfers between devices  25.2 us (35%)
  blocking collectives  21.5 us (30%)
  Pallas kernels  16.8 us (24%)
  local copies, waits for them, and re-layouts  4.31 us (6%)
  waiting for transfers between devices  2.92 us (4%)
    all_to_all x1, blocking collectives, exchange(): lax.all_to_all(row, ('tm', 'band'), 0, 0, tiled=True).reshape(devices, 128)  21.5 us
    ppermute x5, starting transfers between devices, passed_on(): return lax.ppermute(array, axis, pairs)  15.5 us
    all_to_all x1, starting transfers between devices, exchange(): lax.all_to_all(row, ('tm', 'band'), 0, 0, tiled=True).reshape(devices, 128)  9.65 us
    pallas_call x1, Pallas kernels, on_device(): call(functools.partial(inner_kernel, bands, float(bands * rows * cols * (...  6.05 us
    pallas_call x1, Pallas kernels, on_device(): call(functools.partial(edge_kernel, bands), (shape((frames, 3, half, 2 *...  4.5 us
    unnamed x24, local copies, waits for them, and re-layouts  4.31 us
    pallas_call x1, Pallas kernels, on_device(): call(functools.partial(local_kernel, rows), shape((frames, lines, half, w...  2.6 us
    all_to_all x1, waiting for transfers between devices, exchange(): lax.all_to_all(row, ('tm', 'band'), 0, 0, tiled=True).reshape(devices, 128)  2.15 us
  transfers between devices with their start and end apart: 6, of which 3 were waited for; matrix products, arithmetic and copies ran while one was open for 0% of the time, Pallas kernels for 22%

commit v1 on v0

v1 whole, which is shorter than its diff:
```python
import functools
import jax
import jax.numpy as jnp
from jax import lax
from jax.experimental import pallas as pl
from jax.experimental.pallas import tpu as pltpu
from jax.sharding import PartitionSpec as P

GROUPS = 32
EPS = 1e-06
F32 = jnp.float32
BF16 = jnp.bfloat16
VMEM = pl.BlockSpec(memory_space=pltpu.VMEM)
cat = jnp.concatenate


def iota(shape, dim):
    return lax.broadcasted_iota(jnp.int32, shape, dim)


def exact_dot(rows, zero_one):
    n = rows.shape[0]
    high = rows.astype(BF16)
    rest = rows - high.astype(F32)
    middle = rest.astype(BF16)
    low = (rest - middle.astype(F32)).astype(BF16)
    parts = cat([high.astype(F32), middle.astype(F32), low.astype(F32)], axis=0)
    spare = -parts.shape[0] % 16
    if spare:
        parts = cat([parts, jnp.zeros((spare, parts.shape[1]), F32)], axis=0)
    found = jnp.dot(parts.astype(BF16), zero_one.astype(BF16), preferred_element_type=F32)
    return found[:n] + found[n : 2 * n] + found[2 * n : 3 * n]


def pack_row(sums):
    channels = sums[0].shape[1]
    size = channels // GROUPS
    gather = iota((channels, 128), 0) // size == iota((channels, 128), 1) % GROUPS
    grouped = exact_dot(cat(sums, axis=0), gather.astype(F32))
    place = iota((4, 128), 1) // GROUPS == iota((4, 128), 0)
    return jnp.sum(jnp.where(place, grouped, 0.0), axis=0, keepdims=True)


def frame_sums(lines):
    deep = 64
    channels = lines[0].shape[1]
    one, two = jnp.zeros((deep, channels), F32), jnp.zeros((deep, channels), F32)
    for v in lines:
        for a in range(0, v.shape[0], deep):
            part = v[a : a + deep]
            one, two = one + part, two + part * part
    return [jnp.sum(one, axis=0, keepdims=True), jnp.sum(two, axis=0, keepdims=True)]


def scale_and_shift(rows, info_ref, gain, offset, cells, bands):
    channels = gain.shape[1]
    size = channels // GROUPS
    frame = 2 * (iota(rows.shape, 0) // bands) + iota(rows.shape, 1) // 64
    lane, channel = iota((128, 2 * channels), 0) % 64, iota((128, 2 * channels), 1)
    spread = lane == GROUPS * (channel // channels) + channel % channels // size
    totals = []
    for n in range(2):
        begin, end = info_ref[n : n + 1, :], info_ref[4 + n : 5 + n, :]
        inside = jnp.where((frame >= begin) & (frame < end), rows, 0.0)
        totals.append(jnp.sum(inside, axis=0, keepdims=True))
    sums = exact_dot(cat(totals, axis=0), spread.astype(F32))
    found = []
    for n in range(2):
        frames = (info_ref[4 + n : 5 + n, :] - info_ref[n : n + 1, :]).astype(F32)
        per = 1.0 / (cat([frames] * (channels // 128), axis=1) * cells)
        mean = sums[n : n + 1, :channels] * per
        inv_std = lax.rsqrt(sums[n : n + 1, channels:] * per - mean * mean + EPS)
        scale = inv_std * gain
        found.append((scale, offset - mean * scale))
    return found


def sums_kernel(x_ref, row_ref, top_ref, bottom_ref):
    frames, rows = x_ref.shape[:2]
    top_ref[...] = x_ref[:, 0:2]
    bottom_ref[...] = x_ref[:, rows - 1 : rows]
    sums = []
    for f in range(frames):
        sums += frame_sums([x_ref[f, r].astype(F32) for r in range(rows)])
    row_ref[...] = jnp.broadcast_to(pack_row(sums)[None], row_ref.shape)


def arrange(weight_ref, weights):
    channels = weight_ref.shape[2]
    zero = jnp.zeros((channels, channels), BF16)
    for tap in range(9):
        w0, w1, w2 = (weight_ref[tap, dx] for dx in range(3))
        weights[tap, 0:channels] = cat([w1, w0, zero, w2], axis=1)
        weights[tap, channels : 2 * channels] = cat([w2, w1, w0, zero], axis=1)


def clip_table(clip_ref, first):
    ids = clip_ref[...].astype(F32)
    lane = iota(ids.shape, 1)
    begins, ends = [], []
    for n in range(4):
        at = jnp.minimum(first + n, ids.shape[1] - 1)
        mine = jnp.sum(jnp.where(lane == at, ids, 0.0), axis=1, keepdims=True)
        begins.append(jnp.sum(jnp.where(ids < mine, 1.0, 0.0), axis=1, keepdims=True))
        ends.append(jnp.sum(jnp.where(ids <= mine, 1.0, 0.0), axis=1, keepdims=True))
    return cat([jnp.broadcast_to(v, (1, 128)) for v in begins + ends], axis=0).astype(jnp.int32)


def activated(value, scale, shift):
    u = value.astype(F32) * scale + shift
    return u + u * jnp.tanh(u)


def convolve(line, weights_ref, outputs):
    weights = weights_ref[...].reshape(-1, weights_ref.shape[2])
    window = cat(
        [
            cat([line(sources[k], r + dy) for sources, r in outputs], axis=0)
            for k in range(3)
            for dy in (-1, 0, 1)
        ],
        axis=1,
    )
    found = jnp.dot(window, weights, preferred_element_type=F32)
    wide = found.shape[1] // 2
    channels = wide // 2
    size = found.shape[0]
    half = size // len(outputs)
    column = iota((size, channels), 0) % half
    from_left = jnp.where(column == 0, 0.0, pltpu.roll(found[:, wide : wide + channels], 1, 0))
    from_right = jnp.where(column == half - 1, 0.0, pltpu.roll(found[:, wide + channels :], size - 1, 0))
    total = found[:, :wide] + cat([from_left, from_right], axis=1)
    return [total[n * half : (n + 1) * half] for n in range(len(outputs))]


def strided(lines, down_ref, k):
    wide = down_ref.shape[1]
    channels = down_ref.shape[0] // 27
    windows = [lines(dy) for dy in range(3)]
    half = windows[0].shape[1]
    windows = [w.reshape(-1, wide) for w in windows]
    places = [(k * 9 + dy * 3) * channels for dy in range(3)]
    both = cat([down_ref[at : at + 2 * channels] for at in places], axis=0)
    next_even = cat([down_ref[at + 2 * channels : at + 3 * channels] for at in places], axis=0)
    total = jnp.dot(cat(windows, axis=1), both, preferred_element_type=F32)
    shifted = jnp.dot(
        cat([w[:, :channels] for w in windows], axis=1), next_even, preferred_element_type=F32
    )
    size = total.shape[0]
    column = iota(shifted.shape, 0) % half
    shifted = jnp.where(column == half - 1, 0.0, pltpu.roll(shifted, size - 1, 0))
    return (total + shifted).reshape(-1, half, wide)


def hand_on(line, outputs, info_ref, first, down_ref, partial_ref):
    begins = [info_ref[2, 0], info_ref[3, 0]]
    source = (begins[0] > first).astype(jnp.int32)
    goes = lax.axis_index("tm") < lax.axis_size("tm") - 1
    takes = [(goes & (b <= first + 1)).astype(F32) for b in begins]

    def both(dy):
        return jnp.stack([line(f, 2 * i + dy) for f in (source, 1) for i in outputs])

    def second(dy):
        return jnp.stack([line(1, 2 * i + dy) for i in outputs])

    n = len(outputs)
    older = strided(both, down_ref, 0)
    newer = strided(second, down_ref, 1)
    partial_ref[0] = ((older[:n] + newer) * takes[0]).astype(BF16)
    partial_ref[1] = (older[n:] * takes[1]).astype(BF16)


def frame_sources(info_ref, first):
    return [
        [jnp.maximum(first + f - 2 + k, info_ref[f, 0]) - (first - 2) for k in range(3)] for f in range(2)
    ]


def conv_kernel(
    bands, cells, rows_ref, clip_ref, bias_ref, gain_ref, offset_ref, weight_ref, down_ref,
    x_ref, before_ref, above_ref, above_before_ref, below_ref, below_before_ref,
    residual_ref, partial_ref, info_ref, hidden, own, weights, slots,
):
    rows, cols, channels = x_ref.shape[1:]
    first = lax.axis_index("tm") * 2
    band = lax.axis_index("band")
    keep_above = (band > 0).astype(F32)
    keep_below = (band < bands - 1).astype(F32)
    info_ref[...] = clip_table(clip_ref, first)
    arrange(weight_ref, weights)
    bias = bias_ref[...]
    stats = scale_and_shift(rows_ref[...], info_ref, gain_ref[...], offset_ref[...], cells, bands)
    stats = [0.5 * v for pair in stats for v in pair]
    for frame in range(4):
        scale, shift = stats[2:] if frame == 3 else stats[:2]
        body, above, below = (
            (before_ref, above_before_ref, below_before_ref)
            if frame < 2
            else (x_ref, above_ref, below_ref)
        )
        f = frame % 2
        lines = [above.at[f, 0]] + [body.at[f, r] for r in range(rows)] + [below.at[f, r] for r in range(2)]
        for n, line in enumerate(lines):
            slot = slots.at[n]
            slot[...] = line[...].astype(F32)
            for side in range(2):
                lanes = pl.ds(side * channels, channels)
                value = slot[pl.ds(side, cols // 2, 2), :]
                if frame >= 2 and 1 <= n < rows + 2:
                    own[f, n - 1, :, lanes] = value.astype(BF16)
                value = activated(value, scale, shift)
                if n == 0:
                    value = value * keep_above
                if n > rows:
                    value = value * keep_below
                hidden[frame, n, :, lanes] = value.astype(BF16)
    sources = frame_sources(info_ref, first)
    bias = cat([bias, bias], axis=1)
    for f in range(2):
        found = convolve(
            lambda source, r: hidden[source, r + 1], weights, [(sources[f], r) for r in range(rows + 1)]
        )
        for r, total in enumerate(found):
            value = total + own[f, r].astype(F32) + bias
            if r == rows:
                value = value * keep_below
            residual_ref[f, r] = value.astype(BF16)
    hand_on(
        lambda f, r: residual_ref[f, r], range(rows // 2), info_ref, first, down_ref, partial_ref
    )


def local_kernel(info_ref, residual_ref, down_ref, out_ref):
    first = lax.axis_index("tm") * 2
    begins = [info_ref[0, 0], info_ref[1, 0]]
    count = out_ref.shape[1]

    def lines(*picked):
        return lambda dy: jnp.stack([residual_ref[f, 2 * i + dy] for f in picked for i in range(count)])

    base = strided(lines(0, 1), down_ref, 2)
    out_ref[0] = base[:count]
    out_ref[1] = base[count:] + strided(lines((begins[1] > first).astype(jnp.int32)), down_ref, 1)

    @pl.when(begins[0] == first)
    def _():
        out_ref[0] += strided(lines(0), down_ref, 0) + strided(lines(0), down_ref, 1)

    @pl.when(begins[1] >= first)
    def _():
        out_ref[1] += strided(lines(begins[1] - first), down_ref, 0)


def join_kernel(local_ref, sent_ref, reduced_ref, row_ref):
    frames, lines, half, channels = local_ref.shape
    sums = []
    for f in range(frames):
        values = []
        for i in range(lines):
            v = (local_ref[f, i] + sent_ref[f, i].astype(F32)).astype(BF16)
            reduced_ref[f, i] = v
            values.append(v.astype(F32))
        sums += frame_sums(values)
    row_ref[...] = jnp.broadcast_to(pack_row(sums)[None], row_ref.shape)


def out_kernel(bands, cells, rows_ref, info_ref, gain_ref, offset_ref, reduced_ref, out_ref):
    frames, lines = reduced_ref.shape[:2]
    stats = scale_and_shift(rows_ref[...], info_ref, gain_ref[...], offset_ref[...], cells, bands)
    for f in range(frames):
        scale, shift = stats[f]
        for i in range(lines):
            out_ref[f, i] = (reduced_ref[f, i].astype(F32) * scale + shift).astype(BF16)


def call(kernel, out_shape, in_specs, scratch=(), megabytes=4, flops=0, moved=0):
    return pl.pallas_call(
        kernel,
        out_shape=out_shape,
        in_specs=in_specs,
        out_specs=jax.tree.map(lambda _: VMEM, out_shape),
        scratch_shapes=list(scratch),
        compiler_params=pltpu.CompilerParams(vmem_limit_bytes=megabytes << 20),
        cost_estimate=pl.CostEstimate(flops=flops, bytes_accessed=moved, transcendentals=0),
    )


def passed_on(array, tm_by, band_by):
    tms, bands = lax.axis_size("tm"), lax.axis_size("band")
    pairs = [
        (i * bands + b, (i + tm_by) % tms * bands + (b + band_by) % bands)
        for i in range(tms)
        for b in range(bands)
    ]
    return lax.ppermute(array, ("tm", "band"), pairs)


def on_device(
    frames_in, clip_id, conv_weight, conv_bias, norm_gain, norm_shift, down_weight, out_gain, out_shift
):
    frames, rows, cols, channels = frames_in.shape
    wide = down_weight.shape[-1]
    bands = lax.axis_size("band")
    devices, half, lines = lax.axis_size("tm") * bands, cols // 2, rows // 2
    shape = jax.ShapeDtypeStruct
    everyone = shape((devices, 1, 128), F32)

    def exchange(row):
        return lax.all_to_all(row, ("tm", "band"), 0, 0, tiled=True).reshape(devices, 128)

    before = passed_on(frames_in, 1, 0)
    row, top, bottom = call(
        sums_kernel,
        (
            everyone,
            shape((frames, 2, cols, channels), BF16),
            shape((frames, 1, cols, channels), BF16),
        ),
        [VMEM],
        flops=1 << 33,
        moved=1 << 20,
    )(frames_in)
    below_before, below = passed_on(top, 1, -1), passed_on(top, 0, -1)
    above_before, above = passed_on(bottom, 1, 1), passed_on(bottom, 0, 1)
    sums = exchange(row)
    down = down_weight.reshape(-1, wide)
    pair = (half, 2 * channels)
    residual, partial, info = call(
        functools.partial(conv_kernel, bands, float(bands * rows * cols * (channels // GROUPS))),
        (
            shape((frames, rows + 1, *pair), BF16),
            shape((frames, lines, half, wide), BF16),
            shape((8, 128), jnp.int32),
        ),
        [VMEM] * 13,
        scratch=[
            pltpu.VMEM((4, rows + 3, *pair), BF16),
            pltpu.VMEM((frames, rows + 1, *pair), BF16),
            pltpu.VMEM((9, 2 * channels, 4 * channels), BF16),
            pltpu.VMEM((rows + 3, cols, channels), F32),
        ],
        megabytes=28,
        flops=5 << 30,
        moved=1 << 23,
    )(
        sums, clip_id.reshape(1, -1), conv_bias.reshape(1, -1), norm_gain.reshape(1, -1),
        norm_shift.reshape(1, -1), conv_weight.reshape(9, 3, channels, channels), down,
        frames_in, before, above, above_before, below, below_before,
    )
    arrived = passed_on(partial, 1, 0)
    local = call(
        local_kernel,
        shape((frames, lines, half, wide), F32),
        [VMEM] * 3,
        megabytes=16,
        flops=1 << 31,
        moved=1 << 22,
    )(info, residual, down)
    reduced, row = call(
        join_kernel,
        (shape((frames, lines, half, wide), BF16), everyone),
        [VMEM] * 2,
        megabytes=8,
        moved=1 << 21,
    )(local, arrived)
    return call(
        functools.partial(out_kernel, bands, float(bands * lines * half * (wide // GROUPS))),
        shape((frames, lines, half, wide), BF16),
        [VMEM] * 5,
        megabytes=8,
        moved=1 << 20,
    )(exchange(row), info, out_gain.reshape(1, -1), out_shift.reshape(1, -1), reduced)


def solution(mesh):
    return jax.shard_map(
        on_device,
        mesh=mesh,
        in_specs=(P("tm", "band", None, None), P(), P(), P(), P(), P(), P(), P(), P()),
        out_specs=P("tm", "band", None, None),
        check_vma=False,
    )
```

time: 71.3 us -> 64.7 us (0.907)
  starting transfers between devices: 25.2 us -> 9.95 us
  blocking collectives: 21.5 us -> 36 us
  Pallas kernels: 16.8 us -> 12.2 us
  local copies, waits for them, and re-layouts: 4.31 us -> 1.29 us
  waiting for transfers between devices: 2.92 us -> 4.91 us
    all_to_all x1 -> x2, blocking collectives: 21.5 us -> 36 us  [exchange(): lax.all_to_all(row, ('tm', 'band'), 0, 0, tiled=True).reshape(devices, 128)]
    all_to_all x1 -> x0, starting transfers between devices: 9.65 us -> none  [exchange(): lax.all_to_all(row, ('tm', 'band'), 0, 0, tiled=True).reshape(devices, 128)]
    ppermute x5 -> x6, starting transfers between devices: 15.5 us -> 9.95 us  [passed_on(): return lax.ppermute(array, ('tm', 'band'), pairs)]
    pallas_call x6 -> x3, Pallas kernels: 15.3 us -> 10.6 us  [the longest x1 9.04 us: on_device(): call(functools.partial(conv_kernel, bands, float(bands * rows * cols * (c...]
    ppermute x5 -> x6, waiting for transfers between devices: 0.77 us -> 4.91 us  [passed_on(): return lax.ppermute(array, ('tm', 'band'), pairs)]
    unnamed x24 -> x20, local copies, waits for them, and re-layouts: 4.31 us -> 1.29 us
    all_to_all x1 -> x0, waiting for transfers between devices: 2.15 us -> none  [exchange(): lax.all_to_all(row, ('tm', 'band'), 0, 0, tiled=True).reshape(devices, 128)]
  transfers between devices with their start and end apart: 6 -> 6, of which waited for: 3 -> 1; matrix products, arithmetic and copies ran while one was open for 0% -> 0% of each run, Pallas kernels for 22% -> 2%
where the time goes in v1:
time: 64.7 us; the launch traced here: 64.5 us
  blocking collectives  36 us (56%)
  Pallas kernels  12.2 us (19%)
  starting transfers between devices  9.95 us (15%)
  waiting for transfers between devices  4.91 us (8%)
  local copies, waits for them, and re-layouts  1.29 us (2%)
    all_to_all x2, blocking collectives, exchange(): lax.all_to_all(row, ('tm', 'band'), 0, 0, tiled=True).reshape(devices, 128)  36 us
    ppermute x6, starting transfers between devices, passed_on(): return lax.ppermute(array, ('tm', 'band'), pairs)  9.95 us
    pallas_call x1, Pallas kernels, on_device(): call(functools.partial(conv_kernel, bands, float(bands * rows * cols * (c...  9.04 us
    ppermute x6, waiting for transfers between devices, passed_on(): return lax.ppermute(array, ('tm', 'band'), pairs)  4.91 us
  transfers between devices with their start and end apart: 6, of which 1 were waited for; matrix products, arithmetic and copies ran while one was open for 0% of the time, Pallas kernels for 2%

profile of v1, /device:TPU:1, one launch (start us, length us, event | category | flops | bytes accessed | tf_op | source)
XLA Modules:
  0.0 64.5 jit_solution(7543826596982885333)
XLA Ops:
  0.0 0.0 copy-start.2
  0.0 3.0 %collective-permute-start = (bf16[2,8,256,128]{3,2,1,0:T(8,128)(2,1)}, bf16[2,8,256,128]{3,2,1,0:T(8,128)(2,1)S(1)}, u32[]{:S(2)}, u32[]{:S(2)}) collective-permute-start(bf16[2,8,256,128]{3,2,1,0:T(8,128)(2,1)} %x_ref.3), channel_id=1, source_target_pairs={{0,4},{1,5},{2,6},{3,7},{4,8},{5,9},{6,10},{7,11},{8,12},{9,13},{1... | collective-permute-start | bytes 3145736 | tf_op jit(solution)/shard_map/ppermute | solution.py:296
  3.0 0.0 copy-start.3
  3.0 1.3 %copy-done.3 = bf16[2,8,256,128]{3,2,1,0:T(8,128)(2,1)S(1)} copy-done((bf16[2,8,256,128]{3,2,1,0:T(8,128)(2,1)S(1)}, bf16[2,8,256,128]{3,2,1,0:T(8,128)(2,1)}, u32[]{:S(2)}) %copy-start.3) | copy-done | bytes 1048600
  4.3 0.0 copy-start.4
  4.3 0.0 copy-start.5
  4.3 0.0 copy-start.6
  4.3 0.0 copy-start.7
  4.3 0.0 copy-start.8
  4.3 0.0 copy-start.9
  4.3 0.4 shard_map.91
  4.7 2.6 %collective-permute-start.4 = (bf16[2,2,256,128]{3,2,1,0:T(8,128)(2,1)S(1)}, bf16[2,2,256,128]{3,2,1,0:T(8,128)(2,1)S(1)}, u32[]{:S(2)}, u32[]{:S(2)}) collective-permute-start(bf16[2,2,256,128]{3,2,1,0:T(8,128)(2,1)S(1)} %get-tuple-element.15), channel_id=1, source_target_pairs={{0,7},{1,4},{2,5},{3,6},{4,11},{5,8},{6,9},{7,10},{8,15},{9,12},{1... | collective-permute-start | bytes 786440 | tf_op jit(solution)/shard_map/ppermute | solution.py:296
  7.3 0.5 collective-permute-start.3
  7.8 3.1 %collective-permute-start.2 = (bf16[2,1,256,128]{3,2,1,0:T(8,128)(2,1)S(1)}, bf16[2,1,256,128]{3,2,1,0:T(8,128)(2,1)S(1)}, u32[]{:S(2)}, u32[]{:S(2)}) collective-permute-start(bf16[2,1,256,128]{3,2,1,0:T(8,128)(2,1)S(1)} %get-tuple-element.14), channel_id=1, source_target_pairs={{0,5},{1,6},{2,7},{3,4},{4,9},{5,10},{6,11},{7,8},{8,13},{9,14},{1... | collective-permute-start | bytes 393224 | tf_op jit(solution)/shard_map/ppermute | solution.py:296
  10.9 0.0 collective-permute-start.1
  10.9 17.7 %all_to_all.10 = f32[128,1,128]{2,1,0:T(1,128)S(1)} all-to-all(f32[128,1,128]{2,1,0:T(1,128)S(1)} %get-tuple-element.13), channel_id=1, replica_groups=mesh['tm'=32,'band'=4] {'tm','band'}, dimensions={0} | all-to-all | bytes 131072 | tf_op jit(solution)/shard_map/all_to_all | solution.py:310
  28.6 0.0 collective-permute-done.2.above_before_ref
  28.6 0.0 collective-permute-done.1.above_ref
  28.6 0.0 collective-permute-done.4.below_before_ref
  28.6 0.0 collective-permute-done.3.below_ref
  28.7 0.0 collective-permute-done.before_ref
  28.7 0.0 copy-done.2
  28.7 0.0 copy-done.4
  28.7 0.0 copy-done.5
  28.7 0.0 copy-done.6
  28.7 0.0 copy-done.7
  28.7 0.0 copy-done.8
  28.7 0.0 copy-done.9
  28.7 9.0 %shard_map.92 = (bf16[2,9,128,256]{3,2,1,0:T(8,128)(2,1)S(1)}, bf16[2,4,128,256]{3,2,1,0:T(8,128)(2,1)S(1)}, s32[8,128]{1,0:T(8,128)S(1)}) custom-call(f32[128,128]{1,0:T(8,128)S(1)} %bitcast.11, s32[1,64]{1,0:T(1,128)S(1)} %bitcast.17, f32[1,128]{1,0:T(1,128)S(1)} %bitcast.18, f32[1,128]{1,0:T(1,128)S(1)} %bitcast.19, f32[1,128]{1,0:T(1,128)S(1)} %bitcast.20, ...), custom_call_target="tpu_custom_call" | custom-call | flops 5368709120 | bytes 8388608 | tf_op jit(solution)/shard_map/pallas_call | solution.py:329
  37.8 0.7 %collective-permute-start.5 = (bf16[2,4,128,256]{3,2,1,0:T(8,128)(2,1)S(1)}, bf16[2,4,128,256]{3,2,1,0:T(8,128)(2,1)S(1)}, u32[]{:S(2)}, u32[]{:S(2)}) collective-permute-start(bf16[2,4,128,256]{3,2,1,0:T(8,128)(2,1)S(1)} %get-tuple-element.18), channel_id=1, source_target_pairs={{0,4},{1,5},{2,6},{3,7},{4,8},{5,9},{6,10},{7,11},{8,12},{9,13},{1... | collective-permute-start | bytes 1572872 | tf_op jit(solution)/shard_map/ppermute | solution.py:296
  38.5 0.0 copy-start
  38.5 0.0 copy-start.1
  38.5 1.2 %shard_map.93.local_ref = f32[2,4,128,256]{3,2,1,0:T(8,128)S(1)} custom-call(s32[8,128]{1,0:T(8,128)S(1)} %get-tuple-element.16.info_ref, bf16[2,9,128,256]{3,2,1,0:T(8,128)(2,1)S(1)} %get-tuple-element.17.residual_ref, bf16[3456,256]{1,0:T(8,128)(2,1)S(1)} %bitcast.15), custom_call_target="tpu_custom_call" | custom-call | flops 2147483648 | bytes 4194304 | tf_op jit(solution)/shard_map/pallas_call | solution.py:352
  39.7 4.9 %collective-permute-done.5.sent_ref = bf16[2,4,128,256]{3,2,1,0:T(8,128)(2,1)S(1)} collective-permute-done((bf16[2,4,128,256]{3,2,1,0:T(8,128)(2,1)S(1)}, bf16[2,4,128,256]{3,2,1,0:T(8,128)(2,1)S(1)}, u32[]{:S(2)}, u32[]{:S(2)}) %collective-permute-start.5) | collective-permute-done | bytes 524320 | tf_op jit(solution)/shard_map/ppermute | solution.py:296
  44.6 0.4 shard_map.94
  45.1 18.3 %all_to_all.11 = f32[128,1,128]{2,1,0:T(1,128)S(1)} all-to-all(f32[128,1,128]{2,1,0:T(1,128)S(1)} %get-tuple-element.19), channel_id=1, replica_groups=mesh['tm'=32,'band'=4] {'tm','band'}, dimensions={0} | all-to-all | bytes 131072 | tf_op jit(solution)/shard_map/all_to_all | solution.py:310
  63.4 0.0 copy-done
  63.4 0.0 copy-done.1
  63.4 1.1 %shard_map.95 = bf16[2,4,128,256]{3,2,1,0:T(8,128)(2,1)} custom-call(f32[128,128]{1,0:T(8,128)S(1)} %bitcast.10, s32[8,128]{1,0:T(8,128)S(1)} %get-tuple-element.16.info_ref, f32[1,256]{1,0:T(1,128)S(1)} %bitcast.12, f32[1,256]{1,0:T(1,128)S(1)} %bitcast.13, bf16[2,4,128,256]{3,2,1,0:T(8,128)(2,1)S(1)} %get-tuple-element.20.reduced_ref), custom_call_target="tpu_custom_call" | custom-call | bytes 1048576 | tf_op jit(solution)/shard_map/pallas_call | solution.py:367
Async XLA Ops:
  0.0 28.7 %copy-start.2 = (bf16[3,3,3,128,256]{4,3,2,1,0:T(8,128)(2,1)S(1)}, bf16[3,3,3,128,256]{4,3,2,1,0:T(8,128)(2,1)}, u32[]{:S(2)}) copy-start(bf16[3,3,3,128,256]{4,3,2,1,0:T(8,128)(2,1)} %param.15) | copy-start | bytes 5308420
  0.0 28.7 %collective-permute-start = (bf16[2,8,256,128]{3,2,1,0:T(8,128)(2,1)}, bf16[2,8,256,128]{3,2,1,0:T(8,128)(2,1)S(1)}, u32[]{:S(2)}, u32[]{:S(2)}) collective-permute-start(bf16[2,8,256,128]{3,2,1,0:T(8,128)(2,1)} %x_ref.3), channel_id=1, source_target_pairs={{0,4},{1,5},{2,6},{3,7},{4,8},{5,9},{6,10},{7,11},{8,12},{9,13},{1... | collective-permute-start | bytes 3145736 | tf_op jit(solution)/shard_map/ppermute | solution.py:296
  3.0 1.3 %copy-start.3 = (bf16[2,8,256,128]{3,2,1,0:T(8,128)(2,1)S(1)}, bf16[2,8,256,128]{3,2,1,0:T(8,128)(2,1)}, u32[]{:S(2)}) copy-start(bf16[2,8,256,128]{3,2,1,0:T(8,128)(2,1)} %x_ref.3) | copy-start | bytes 3145732
  4.3 24.4 %copy-start.4 = (bf16[2,8,256,128]{3,2,1,0:T(8,128)(2,1)S(1)}, bf16[2,8,256,128]{3,2,1,0:T(8,128)(2,1)}, u32[]{:S(2)}) copy-start(bf16[2,8,256,128]{3,2,1,0:T(8,128)(2,1)} %x_ref.3) | copy-start | bytes 3145732
  4.3 24.4 %copy-start.5 = (bf16[3,3,3,128,128]{4,3,2,1,0:T(8,128)(2,1)S(1)}, bf16[3,3,3,128,128]{4,3,2,1,0:T(8,128)(2,1)}, u32[]{:S(2)}) copy-start(bf16[3,3,3,128,128]{4,3,2,1,0:T(8,128)(2,1)} %param.11) | copy-start | bytes 2654212
  4.3 24.4 %copy-start.6 = (s32[64]{0:T(128)S(1)}, s32[64]{0:T(128)}, u32[]{:S(2)}) copy-start(s32[64]{0:T(128)} %param.10) | copy-start | bytes 772
  4.3 24.4 %copy-start.7 = (f32[128]{0:T(128)S(1)}, f32[128]{0:T(128)}, u32[]{:S(2)}) copy-start(f32[128]{0:T(128)} %param.12) | copy-start | bytes 1540
  4.3 24.4 %copy-start.8 = (f32[128]{0:T(128)S(1)}, f32[128]{0:T(128)}, u32[]{:S(2)}) copy-start(f32[128]{0:T(128)} %param.13) | copy-start | bytes 1540
  4.3 24.4 %copy-start.9 = (f32[128]{0:T(128)S(1)}, f32[128]{0:T(128)}, u32[]{:S(2)}) copy-start(f32[128]{0:T(128)} %param.14) | copy-start | bytes 1540
  4.7 23.9 %collective-permute-start.4 = (bf16[2,2,256,128]{3,2,1,0:T(8,128)(2,1)S(1)}, bf16[2,2,256,128]{3,2,1,0:T(8,128)(2,1)S(1)}, u32[]{:S(2)}, u32[]{:S(2)}) collective-permute-start(bf16[2,2,256,128]{3,2,1,0:T(8,128)(2,1)S(1)} %get-tuple-element.15), channel_id=1, source_target_pairs={{0,7},{1,4},{2,5},{3,6},{4,11},{5,8},{6,9},{7,10},{8,15},{9,12},{1... | collective-permute-start | bytes 786440 | tf_op jit(solution)/shard_map/ppermute | solution.py:296
  7.3 21.3 %collective-permute-start.3 = (bf16[2,2,256,128]{3,2,1,0:T(8,128)(2,1)S(1)}, bf16[2,2,256,128]{3,2,1,0:T(8,128)(2,1)S(1)}, u32[]{:S(2)}, u32[]{:S(2)}) collective-permute-start(bf16[2,2,256,128]{3,2,1,0:T(8,128)(2,1)S(1)} %get-tuple-element.15), channel_id=1, source_target_pairs={{0,3},{1,0},{2,1},{3,2},{4,7},{5,4},{6,5},{7,6},{8,11},{9,8},{10,9... | collective-permute-start | bytes 786440 | tf_op jit(solution)/shard_map/ppermute | solution.py:296
  7.8 20.9 %collective-permute-start.2 = (bf16[2,1,256,128]{3,2,1,0:T(8,128)(2,1)S(1)}, bf16[2,1,256,128]{3,2,1,0:T(8,128)(2,1)S(1)}, u32[]{:S(2)}, u32[]{:S(2)}) collective-permute-start(bf16[2,1,256,128]{3,2,1,0:T(8,128)(2,1)S(1)} %get-tuple-element.14), channel_id=1, source_target_pairs={{0,5},{1,6},{2,7},{3,4},{4,9},{5,10},{6,11},{7,8},{8,13},{9,14},{1... | collective-permute-start | bytes 393224 | tf_op jit(solution)/shard_map/ppermute | solution.py:296
  10.9 17.8 %collective-permute-start.1 = (bf16[2,1,256,128]{3,2,1,0:T(8,128)(2,1)S(1)}, bf16[2,1,256,128]{3,2,1,0:T(8,128)(2,1)S(1)}, u32[]{:S(2)}, u32[]{:S(2)}) collective-permute-start(bf16[2,1,256,128]{3,2,1,0:T(8,128)(2,1)S(1)} %get-tuple-element.14), channel_id=1, source_target_pairs={{0,1},{1,2},{2,3},{3,0},{4,5},{5,6},{6,7},{7,4},{8,9},{9,10},{10,1... | collective-permute-start | bytes 393224 | tf_op jit(solution)/shard_map/ppermute | solution.py:296
  37.8 6.9 %collective-permute-start.5 = (bf16[2,4,128,256]{3,2,1,0:T(8,128)(2,1)S(1)}, bf16[2,4,128,256]{3,2,1,0:T(8,128)(2,1)S(1)}, u32[]{:S(2)}, u32[]{:S(2)}) collective-permute-start(bf16[2,4,128,256]{3,2,1,0:T(8,128)(2,1)S(1)} %get-tuple-element.18), channel_id=1, source_target_pairs={{0,4},{1,5},{2,6},{3,7},{4,8},{5,9},{6,10},{7,11},{8,12},{9,13},{1... | collective-permute-start | bytes 1572872 | tf_op jit(solution)/shard_map/ppermute | solution.py:296
  38.5 24.9 %copy-start = (f32[256]{0:T(256)S(1)}, f32[256]{0:T(256)}, u32[]{:S(2)}) copy-start(f32[256]{0:T(256)} %param.16) | copy-start | bytes 3076
  38.5 24.9 %copy-start.1 = (f32[256]{0:T(256)S(1)}, f32[256]{0:T(256)}, u32[]{:S(2)}) copy-start(f32[256]{0:T(256)} %param.17) | copy-start | bytes 3076

commit v2 on v1

--- a/solution.py
+++ b/solution.py
@@ -155,8 +155,7 @@
 def hand_on(line, outputs, info_ref, first, down_ref, partial_ref):
     begins = [info_ref[2, 0], info_ref[3, 0]]
     source = (begins[0] > first).astype(jnp.int32)
-    goes = lax.axis_index("tm") < lax.axis_size("tm") - 1
-    takes = [(goes & (b <= first + 1)).astype(F32) for b in begins]
+    takes = [(b <= first + 1).astype(F32) for b in begins]
 
     def both(dy):
         return jnp.stack([line(f, 2 * i + dy) for f in (source, 1) for i in outputs])
@@ -177,17 +176,28 @@
     ]
 
 
-def conv_kernel(
-    bands, cells, rows_ref, clip_ref, bias_ref, gain_ref, offset_ref, weight_ref, down_ref,
+def conv_first_kernel(which, bands, cells, clip_ref, *refs):
+    ins, (residual_ref, partial_ref, info_ref), scratch = refs[:12], refs[12:15], refs[15:]
+    info_ref[...] = clip_table(clip_ref, lax.axis_index("tm") * 2)
+    conv_kernel(which, bands, cells, info_ref, *ins, residual_ref, partial_ref, *scratch)
+
+
+def conv_kernel(which, bands, cells, *refs):
+    @pl.when(lax.axis_index("tm") % 2 == which)
+    def _():
+        convolve_frames(bands, cells, *refs)
+
+
+def convolve_frames(
+    bands, cells, info_ref, rows_ref, bias_ref, gain_ref, offset_ref, weight_ref, down_ref,
     x_ref, before_ref, above_ref, above_before_ref, below_ref, below_before_ref,
-    residual_ref, partial_ref, info_ref, hidden, own, weights, slots,
+    residual_ref, partial_ref, hidden, own, weights, slots,
 ):
     rows, cols, channels = x_ref.shape[1:]
     first = lax.axis_index("tm") * 2
     band = lax.axis_index("band")
     keep_above = (band > 0).astype(F32)
     keep_below = (band < bands - 1).astype(F32)
-    info_ref[...] = clip_table(clip_ref, first)
     arrange(weight_ref, weights)
     bias = bias_ref[...]
     stats = scale_and_shift(rows_ref[...], info_ref, gain_ref[...], offset_ref[...], cells, bands)
@@ -231,7 +241,15 @@
     )
 
 
-def local_kernel(info_ref, residual_ref, down_ref, out_ref):
+def local_kernel(info_ref, first_core_ref, second_core_ref, down_ref, out_ref):
+    for which, residual_ref in enumerate((first_core_ref, second_core_ref)):
+
+        @pl.when(lax.axis_index("tm") % 2 == which)
+        def _(residual_ref=residual_ref):
+            local_part(info_ref, residual_ref, down_ref, out_ref)
+
+
+def local_part(info_ref, residual_ref, down_ref, out_ref):
     first = lax.axis_index("tm") * 2
     begins = [info_ref[0, 0], info_ref[1, 0]]
     count = out_ref.shape[1]
@@ -252,13 +270,14 @@
         out_ref[1] += strided(lines(begins[1] - first), down_ref, 0)
 
 
-def join_kernel(local_ref, sent_ref, reduced_ref, row_ref):
+def join_kernel(local_ref, between_ref, within_ref, reduced_ref, row_ref):
     frames, lines, half, channels = local_ref.shape
     sums = []
     for f in range(frames):
         values = []
         for i in range(lines):
-            v = (local_ref[f, i] + sent_ref[f, i].astype(F32)).astype(BF16)
+            sent = between_ref[f, i].astype(F32) + within_ref[f, i].astype(F32)
+            v = (local_ref[f, i] + sent).astype(BF16)
             reduced_ref[f, i] = v
             values.append(v.astype(F32))
         sums += frame_sums(values)
@@ -294,6 +313,14 @@
         for b in range(bands)
     ]
     return lax.ppermute(array, ("tm", "band"), pairs)
+
+
+def between_chips(array):
+    return lax.ppermute(array, "tm", [(i, i + 1) for i in range(1, lax.axis_size("tm") - 1, 2)])
+
+
+def within_chips(array):
+    return lax.ppermute(array, "tm", [(i, i + 1) for i in range(0, lax.axis_size("tm"), 2)])
 
 
 def on_device(
@@ -326,44 +353,48 @@
     sums = exchange(row)
     down = down_weight.reshape(-1, wide)
     pair = (half, 2 * channels)
-    residual, partial, info = call(
-        functools.partial(conv_kernel, bands, float(bands * rows * cols * (channels // GROUPS))),
-        (
-            shape((frames, rows + 1, *pair), BF16),
-            shape((frames, lines, half, wide), BF16),
-            shape((8, 128), jnp.int32),
-        ),
-        [VMEM] * 13,
-        scratch=[
-            pltpu.VMEM((4, rows + 3, *pair), BF16),
-            pltpu.VMEM((frames, rows + 1, *pair), BF16),
-            pltpu.VMEM((9, 2 * channels, 4 * channels), BF16),
-            pltpu.VMEM((rows + 3, cols, channels), F32),
-        ],
-        megabytes=28,
-        flops=5 << 30,
-        moved=1 << 23,
-    )(
-        sums, clip_id.reshape(1, -1), conv_bias.reshape(1, -1), norm_gain.reshape(1, -1),
-        norm_shift.reshape(1, -1), conv_weight.reshape(9, 3, channels, channels), down,
-        frames_in, before, above, above_before, below, below_before,
-    )
-    arrived = passed_on(partial, 1, 0)
+    def conv(kernel, which, info, *more):
+        cells = float(bands * rows * cols * (channels // GROUPS))
+        return call(
+            functools.partial(kernel, which, bands, cells),
+            (shape((frames, rows + 1, *pair), BF16), shape((frames, lines, half, wide), BF16), *more),
+            [VMEM] * 13,
+            scratch=[
+                pltpu.VMEM((4, rows + 3, *pair), BF16),
+                pltpu.VMEM((frames, rows + 1, *pair), BF16),
+                pltpu.VMEM((9, 2 * channels, 4 * channels), BF16),
+                pltpu.VMEM((rows + 3, cols, channels), F32),
+            ],
+            megabytes=24,
+            flops=5 << 30,
+            moved=1 << 23,
+        )(
+            info, sums, conv_bias.reshape(1, -1), norm_gain.reshape(1, -1),
+            norm_shift.reshape(1, -1), conv_weight.reshape(9, 3, channels, channels), down,
+            frames_in, before, above, above_before, below, below_before,
+        )
+
+    second_core, partial, info = conv(
+        conv_first_kernel, 1, clip_id.reshape(1, -1), shape((8, 128), jnp.int32)
+    )
+    between = between_chips(partial)
+    first_core, partial = conv(conv_kernel, 0, info)
+    within = within_chips(partial)
     local = call(
         local_kernel,
         shape((frames, lines, half, wide), F32),
-        [VMEM] * 3,
-        megabytes=16,
+        [VMEM] * 4,
+        megabytes=12,
         flops=1 << 31,
         moved=1 << 22,
-    )(info, residual, down)
+    )(info, first_core, second_core, down)
     reduced, row = call(
         join_kernel,
         (shape((frames, lines, half, wide), BF16), everyone),
-        [VMEM] * 2,
+        [VMEM] * 3,
         megabytes=8,
         moved=1 << 21,
-    )(local, arrived)
+    )(local, between, within)
     return call(
         functools.partial(out_kernel, bands, float(bands * lines * half * (wide // GROUPS))),
         shape((frames, lines, half, wide), BF16),

time: 64.7 us -> 62.5 us (0.966)
  blocking collectives: 36 us -> 33.1 us
  waiting for transfers between devices: 4.91 us -> 2.8 us
  starting transfers between devices: 9.95 us -> 11.8 us
  Pallas kernels: 12.2 us -> 13.1 us
    ppermute x6 -> x5, waiting for transfers between devices: 4.91 us -> 0.01 us  [passed_on(): return lax.ppermute(array, ('tm', 'band'), pairs)]
    all_to_all x2, blocking collectives: 36 us -> 33.1 us  [exchange(): lax.all_to_all(row, ('tm', 'band'), 0, 0, tiled=True).reshape(devices, 128)]
    ppermute x0 -> x2, waiting for transfers between devices: none -> 2.79 us  [the longest x1 2.79 us: between_chips(): lax.ppermute(array, 'tm', [(i, i + 1) for i in range(1, lax.axis_size('tm...]
    ppermute x0 -> x2, starting transfers between devices: none -> 2.61 us  [the longest x1 1.32 us: between_chips(): lax.ppermute(array, 'tm', [(i, i + 1) for i in range(1, lax.axis_size('tm...]
    pallas_call x2 -> x3, Pallas kernels: 10.2 us -> 11.1 us  [the longest x2 9.31 us: conv(): call(functools.partial(kernel, which, bands, cells), (shape((frames, rows...]
    ppermute x6 -> x5, starting transfers between devices: 9.95 us -> 9.21 us  [passed_on(): return lax.ppermute(array, ('tm', 'band'), pairs)]
  transfers between devices with their start and end apart: 6 -> 7, of which waited for: 1 -> 1; matrix products, arithmetic and copies ran while one was open for 0% -> 0% of each run, Pallas kernels for 2% -> 4%
where the time goes in v2:
time: 62.5 us; the launch traced here: 62.3 us
  blocking collectives  33.1 us (53%)
  Pallas kernels  13.1 us (21%)
  starting transfers between devices  11.8 us (19%)
  waiting for transfers between devices  2.8 us (4%)
  local copies, waits for them, and re-layouts  1.3 us (2%)
    all_to_all x2, blocking collectives, exchange(): lax.all_to_all(row, ('tm', 'band'), 0, 0, tiled=True).reshape(devices, 128)  33.1 us
    pallas_call x2, Pallas kernels, conv(): call(functools.partial(kernel, which, bands, cells), (shape((frames, rows...  9.31 us
    ppermute x5, starting transfers between devices, passed_on(): return lax.ppermute(array, ('tm', 'band'), pairs)  9.21 us
    ppermute x1, waiting for transfers between devices, between_chips(): lax.ppermute(array, 'tm', [(i, i + 1) for i in range(1, lax.axis_size('tm...  2.79 us
    pallas_call x1, Pallas kernels, on_device(): call(local_kernel, shape((frames, lines, half, wide), F32), [VMEM] * 4, m...  1.74 us
    ppermute x1, starting transfers between devices, between_chips(): lax.ppermute(array, 'tm', [(i, i + 1) for i in range(1, lax.axis_size('tm...  1.32 us
    unnamed x20, local copies, waits for them, and re-layouts  1.3 us
    ppermute x1, starting transfers between devices, within_chips(): lax.ppermute(array, 'tm', [(i, i + 1) for i in range(0, lax.axis_size('tm...  1.29 us
  transfers between devices with their start and end apart: 7, of which 1 were waited for; matrix products, arithmetic and copies ran while one was open for 0% of the time, Pallas kernels for 4%

profile of v2, /device:TPU:1, one launch (start us, length us, event | category | flops | bytes accessed | tf_op | source)
XLA Modules:
  0.0 62.3 jit_solution(11110562766864631934)
XLA Ops:
  0.0 0.0 copy-start.2
  0.0 3.0 %collective-permute-start = (bf16[2,8,256,128]{3,2,1,0:T(8,128)(2,1)}, bf16[2,8,256,128]{3,2,1,0:T(8,128)(2,1)S(1)}, u32[]{:S(2)}, u32[]{:S(2)}) collective-permute-start(bf16[2,8,256,128]{3,2,1,0:T(8,128)(2,1)} %refs_7_.1), channel_id=1, source_target_pairs={{0,4},{1,5},{2,6},{3,7},{4,8},{5,9},{6,10},{7,11},{8,12},{9,13},{1... | collective-permute-start | bytes 3145736 | tf_op jit(solution)/shard_map/ppermute | solution.py:315
  3.0 0.0 copy-start.3
  3.0 1.3 %copy-done.3 = bf16[2,8,256,128]{3,2,1,0:T(8,128)(2,1)S(1)} copy-done((bf16[2,8,256,128]{3,2,1,0:T(8,128)(2,1)S(1)}, bf16[2,8,256,128]{3,2,1,0:T(8,128)(2,1)}, u32[]{:S(2)}) %copy-start.3) | copy-done | bytes 1048600
  4.3 0.0 copy-start.4
  4.3 0.0 copy-start.5
  4.3 0.0 copy-start.6
  4.3 0.0 copy-start.7
  4.3 0.0 copy-start.8
  4.3 0.0 copy-start.9
  4.3 0.4 shard_map.91
  4.7 2.6 %collective-permute-start.4 = (bf16[2,2,256,128]{3,2,1,0:T(8,128)(2,1)S(1)}, bf16[2,2,256,128]{3,2,1,0:T(8,128)(2,1)S(1)}, u32[]{:S(2)}, u32[]{:S(2)}) collective-permute-start(bf16[2,2,256,128]{3,2,1,0:T(8,128)(2,1)S(1)} %get-tuple-element.17), channel_id=1, source_target_pairs={{0,7},{1,4},{2,5},{3,6},{4,11},{5,8},{6,9},{7,10},{8,15},{9,12},{1... | collective-permute-start | bytes 786440 | tf_op jit(solution)/shard_map/ppermute | solution.py:315
  7.3 0.5 collective-permute-start.3
  7.8 3.1 %collective-permute-start.2 = (bf16[2,1,256,128]{3,2,1,0:T(8,128)(2,1)S(1)}, bf16[2,1,256,128]{3,2,1,0:T(8,128)(2,1)S(1)}, u32[]{:S(2)}, u32[]{:S(2)}) collective-permute-start(bf16[2,1,256,128]{3,2,1,0:T(8,128)(2,1)S(1)} %get-tuple-element.16), channel_id=1, source_target_pairs={{0,5},{1,6},{2,7},{3,4},{4,9},{5,10},{6,11},{7,8},{8,13},{9,14},{1... | collective-permute-start | bytes 393224 | tf_op jit(solution)/shard_map/ppermute | solution.py:315
  10.9 0.0 collective-permute-start.1
  10.9 17.7 %all_to_all.10 = f32[128,1,128]{2,1,0:T(1,128)S(1)} all-to-all(f32[128,1,128]{2,1,0:T(1,128)S(1)} %get-tuple-element.15), channel_id=1, replica_groups=mesh['tm'=32,'band'=4] {'tm','band'}, dimensions={0} | all-to-all | bytes 131072 | tf_op jit(solution)/shard_map/all_to_all | solution.py:337
  28.6 0.0 collective-permute-done.2.refs_9_.refs_10_
  28.6 0.0 collective-permute-done.1.refs_8_.refs_9_
  28.6 0.0 collective-permute-done.4.refs_11_.refs_12_
  28.6 0.0 collective-permute-done.3.refs_10_.refs_11_
  28.7 0.0 collective-permute-done.refs_7_.refs_8_
  28.7 0.0 copy-done.2
  28.7 0.0 copy-done.4
  28.7 0.0 copy-done.5
  28.7 0.0 copy-done.6
  28.7 0.0 copy-done.7
  28.7 0.0 copy-done.8
  28.7 0.0 copy-done.9
  28.7 9.1 %shard_map.92 = (bf16[2,9,128,256]{3,2,1,0:T(8,128)(2,1)S(1)}, bf16[2,4,128,256]{3,2,1,0:T(8,128)(2,1)S(1)}, s32[8,128]{1,0:T(8,128)S(1)}) custom-call(s32[1,64]{1,0:T(1,128)S(1)} %bitcast.20, f32[128,128]{1,0:T(8,128)S(1)} %bitcast.11, f32[1,128]{1,0:T(1,128)S(1)} %bitcast.21, f32[1,128]{1,0:T(1,128)S(1)} %bitcast.23, f32[1,128]{1,0:T(1,128)S(1)} %bitcast.25, ...), custom_call_target="tpu_custom_call" | custom-call | flops 5368709120 | bytes 8388608 | tf_op jit(solution)/shard_map/pallas_call | solution.py:358
  37.9 1.3 %collective-permute-start.5 = (bf16[2,4,128,256]{3,2,1,0:T(8,128)(2,1)S(1)}, bf16[2,4,128,256]{3,2,1,0:T(8,128)(2,1)S(1)}, u32[]{:S(2)}, u32[]{:S(2)}) collective-permute-start(bf16[2,4,128,256]{3,2,1,0:T(8,128)(2,1)S(1)} %get-tuple-element.21), channel_id=1, source_target_pairs={{4,8},{12,16},{20,24},{28,32},{36,40},{44,48},{52,56},{60,64},{68,... | collective-permute-start | bytes 1572872 | tf_op jit(solution)/shard_map/ppermute | solution.py:319
  39.2 0.2 shard_map.93
  39.4 1.3 %collective-permute-start.6 = (bf16[2,4,128,256]{3,2,1,0:T(8,128)(2,1)S(1)}, bf16[2,4,128,256]{3,2,1,0:T(8,128)(2,1)S(1)}, u32[]{:S(2)}, u32[]{:S(2)}) collective-permute-start(bf16[2,4,128,256]{3,2,1,0:T(8,128)(2,1)S(1)} %get-tuple-element.22), channel_id=1, source_target_pairs={{0,4},{8,12},{16,20},{24,28},{32,36},{40,44},{48,52},{56,60},{64,6... | collective-permute-start | bytes 1572872 | tf_op jit(solution)/shard_map/ppermute | solution.py:323
  40.7 1.7 %shard_map.94.local_ref = f32[2,4,128,256]{3,2,1,0:T(8,128)S(1)} custom-call(s32[8,128]{1,0:T(8,128)S(1)} %get-tuple-element.18.refs_0_.info_ref, bf16[2,9,128,256]{3,2,1,0:T(8,128)(2,1)S(1)} %get-tuple-element.19.first_core_ref, bf16[2,9,128,256]{3,2,1,0:T(8,128)(2,1)S(1)} %get-tuple-element.20.second_core_ref, bf16[3456,256]{1,0:T(8,128)(2,1)S(1)} %bitcast.17), custom_call_target="tpu_custom_call" | custom-call | flops 2147483648 | bytes 4194304 | tf_op jit(solution)/shard_map/pallas_call | solution.py:383
  42.4 0.0 copy-start
  42.5 0.0 copy-start.1
  42.5 2.8 %collective-permute-done.5.between_ref = bf16[2,4,128,256]{3,2,1,0:T(8,128)(2,1)S(1)} collective-permute-done((bf16[2,4,128,256]{3,2,1,0:T(8,128)(2,1)S(1)}, bf16[2,4,128,256]{3,2,1,0:T(8,128)(2,1)S(1)}, u32[]{:S(2)}, u32[]{:S(2)}) %collective-permute-start.5) | collective-permute-done | bytes 524320 | tf_op jit(solution)/shard_map/ppermute | solution.py:319
  45.3 0.0 collective-permute-done.6.within_ref
  45.3 0.5 shard_map.95
  45.8 15.4 %all_to_all.11 = f32[128,1,128]{2,1,0:T(1,128)S(1)} all-to-all(f32[128,1,128]{2,1,0:T(1,128)S(1)} %get-tuple-element.23), channel_id=1, replica_groups=mesh['tm'=32,'band'=4] {'tm','band'}, dimensions={0} | all-to-all | bytes 131072 | tf_op jit(solution)/shard_map/all_to_all | solution.py:337
  61.2 0.0 copy-done
  61.2 0.0 copy-done.1
  61.2 1.1 %shard_map.96 = bf16[2,4,128,256]{3,2,1,0:T(8,128)(2,1)} custom-call(f32[128,128]{1,0:T(8,128)S(1)} %bitcast.10, s32[8,128]{1,0:T(8,128)S(1)} %get-tuple-element.18.refs_0_.info_ref, f32[1,256]{1,0:T(1,128)S(1)} %bitcast.13, f32[1,256]{1,0:T(1,128)S(1)} %bitcast.14, bf16[2,4,128,256]{3,2,1,0:T(8,128)(2,1)S(1)} %get-tuple-element.24.reduced_ref), custom_call_target="tpu_custom_call" | custom-call | bytes 1048576 | tf_op jit(solution)/shard_map/pallas_call | solution.py:398
Async XLA Ops:
  0.0 28.7 %copy-start.2 = (bf16[3,3,3,128,256]{4,3,2,1,0:T(8,128)(2,1)S(1)}, bf16[3,3,3,128,256]{4,3,2,1,0:T(8,128)(2,1)}, u32[]{:S(2)}) copy-start(bf16[3,3,3,128,256]{4,3,2,1,0:T(8,128)(2,1)} %param.15) | copy-start | bytes 5308420
  0.0 28.7 %collective-permute-start = (bf16[2,8,256,128]{3,2,1,0:T(8,128)(2,1)}, bf16[2,8,256,128]{3,2,1,0:T(8,128)(2,1)S(1)}, u32[]{:S(2)}, u32[]{:S(2)}) collective-permute-start(bf16[2,8,256,128]{3,2,1,0:T(8,128)(2,1)} %refs_7_.1), channel_id=1, source_target_pairs={{0,4},{1,5},{2,6},{3,7},{4,8},{5,9},{6,10},{7,11},{8,12},{9,13},{1... | collective-permute-start | bytes 3145736 | tf_op jit(solution)/shard_map/ppermute | solution.py:315
  3.0 1.3 %copy-start.3 = (bf16[2,8,256,128]{3,2,1,0:T(8,128)(2,1)S(1)}, bf16[2,8,256,128]{3,2,1,0:T(8,128)(2,1)}, u32[]{:S(2)}) copy-start(bf16[2,8,256,128]{3,2,1,0:T(8,128)(2,1)} %refs_7_.1) | copy-start | bytes 3145732
  4.3 24.4 %copy-start.4 = (bf16[2,8,256,128]{3,2,1,0:T(8,128)(2,1)S(1)}, bf16[2,8,256,128]{3,2,1,0:T(8,128)(2,1)}, u32[]{:S(2)}) copy-start(bf16[2,8,256,128]{3,2,1,0:T(8,128)(2,1)} %refs_7_.1) | copy-start | bytes 3145732
  4.3 24.4 %copy-start.5 = (bf16[3,3,3,128,128]{4,3,2,1,0:T(8,128)(2,1)S(1)}, bf16[3,3,3,128,128]{4,3,2,1,0:T(8,128)(2,1)}, u32[]{:S(2)}) copy-start(bf16[3,3,3,128,128]{4,3,2,1,0:T(8,128)(2,1)} %param.11) | copy-start | bytes 2654212
  4.3 24.4 %copy-start.6 = (s32[64]{0:T(128)S(1)}, s32[64]{0:T(128)}, u32[]{:S(2)}) copy-start(s32[64]{0:T(128)} %param.10) | copy-start | bytes 772
  4.3 24.4 %copy-start.7 = (f32[128]{0:T(128)S(1)}, f32[128]{0:T(128)}, u32[]{:S(2)}) copy-start(f32[128]{0:T(128)} %param.12) | copy-start | bytes 1540
  4.3 24.4 %copy-start.8 = (f32[128]{0:T(128)S(1)}, f32[128]{0:T(128)}, u32[]{:S(2)}) copy-start(f32[128]{0:T(128)} %param.13) | copy-start | bytes 1540
  4.3 24.4 %copy-start.9 = (f32[128]{0:T(128)S(1)}, f32[128]{0:T(128)}, u32[]{:S(2)}) copy-start(f32[128]{0:T(128)} %param.14) | copy-start | bytes 1540
  4.7 23.9 %collective-permute-start.4 = (bf16[2,2,256,128]{3,2,1,0:T(8,128)(2,1)S(1)}, bf16[2,2,256,128]{3,2,1,0:T(8,128)(2,1)S(1)}, u32[]{:S(2)}, u32[]{:S(2)}) collective-permute-start(bf16[2,2,256,128]{3,2,1,0:T(8,128)(2,1)S(1)} %get-tuple-element.17), channel_id=1, source_target_pairs={{0,7},{1,4},{2,5},{3,6},{4,11},{5,8},{6,9},{7,10},{8,15},{9,12},{1... | collective-permute-start | bytes 786440 | tf_op jit(solution)/shard_map/ppermute | solution.py:315
  7.3 21.3 %collective-permute-start.3 = (bf16[2,2,256,128]{3,2,1,0:T(8,128)(2,1)S(1)}, bf16[2,2,256,128]{3,2,1,0:T(8,128)(2,1)S(1)}, u32[]{:S(2)}, u32[]{:S(2)}) collective-permute-start(bf16[2,2,256,128]{3,2,1,0:T(8,128)(2,1)S(1)} %get-tuple-element.17), channel_id=1, source_target_pairs={{0,3},{1,0},{2,1},{3,2},{4,7},{5,4},{6,5},{7,6},{8,11},{9,8},{10,9... | collective-permute-start | bytes 786440 | tf_op jit(solution)/shard_map/ppermute | solution.py:315
  7.8 20.9 %collective-permute-start.2 = (bf16[2,1,256,128]{3,2,1,0:T(8,128)(2,1)S(1)}, bf16[2,1,256,128]{3,2,1,0:T(8,128)(2,1)S(1)}, u32[]{:S(2)}, u32[]{:S(2)}) collective-permute-start(bf16[2,1,256,128]{3,2,1,0:T(8,128)(2,1)S(1)} %get-tuple-element.16), channel_id=1, source_target_pairs={{0,5},{1,6},{2,7},{3,4},{4,9},{5,10},{6,11},{7,8},{8,13},{9,14},{1... | collective-permute-start | bytes 393224 | tf_op jit(solution)/shard_map/ppermute | solution.py:315
  10.9 17.8 %collective-permute-start.1 = (bf16[2,1,256,128]{3,2,1,0:T(8,128)(2,1)S(1)}, bf16[2,1,256,128]{3,2,1,0:T(8,128)(2,1)S(1)}, u32[]{:S(2)}, u32[]{:S(2)}) collective-permute-start(bf16[2,1,256,128]{3,2,1,0:T(8,128)(2,1)S(1)} %get-tuple-element.16), channel_id=1, source_target_pairs={{0,1},{1,2},{2,3},{3,0},{4,5},{5,6},{6,7},{7,4},{8,9},{9,10},{10,1... | collective-permute-start | bytes 393224 | tf_op jit(solution)/shard_map/ppermute | solution.py:315
  37.9 7.4 %collective-permute-start.5 = (bf16[2,4,128,256]{3,2,1,0:T(8,128)(2,1)S(1)}, bf16[2,4,128,256]{3,2,1,0:T(8,128)(2,1)S(1)}, u32[]{:S(2)}, u32[]{:S(2)}) collective-permute-start(bf16[2,4,128,256]{3,2,1,0:T(8,128)(2,1)S(1)} %get-tuple-element.21), channel_id=1, source_target_pairs={{4,8},{12,16},{20,24},{28,32},{36,40},{44,48},{52,56},{60,64},{68,... | collective-permute-start | bytes 1572872 | tf_op jit(solution)/shard_map/ppermute | solution.py:319
  39.4 5.9 %collective-permute-start.6 = (bf16[2,4,128,256]{3,2,1,0:T(8,128)(2,1)S(1)}, bf16[2,4,128,256]{3,2,1,0:T(8,128)(2,1)S(1)}, u32[]{:S(2)}, u32[]{:S(2)}) collective-permute-start(bf16[2,4,128,256]{3,2,1,0:T(8,128)(2,1)S(1)} %get-tuple-element.22), channel_id=1, source_target_pairs={{0,4},{8,12},{16,20},{24,28},{32,36},{40,44},{48,52},{56,60},{64,6... | collective-permute-start | bytes 1572872 | tf_op jit(solution)/shard_map/ppermute | solution.py:323
  42.4 18.7 %copy-start = (f32[256]{0:T(256)S(1)}, f32[256]{0:T(256)}, u32[]{:S(2)}) copy-start(f32[256]{0:T(256)} %param.16) | copy-start | bytes 3076
  42.5 18.7 %copy-start.1 = (f32[256]{0:T(256)S(1)}, f32[256]{0:T(256)}, u32[]{:S(2)}) copy-start(f32[256]{0:T(256)} %param.17) | copy-start | bytes 3076

commit v3 on v2

--- a/solution.py
+++ b/solution.py
@@ -75,10 +75,9 @@
     return found
 
 
-def sums_kernel(x_ref, row_ref, top_ref, bottom_ref):
+def sums_kernel(x_ref, row_ref, top_ref):
     frames, rows = x_ref.shape[:2]
     top_ref[...] = x_ref[:, 0:2]
-    bottom_ref[...] = x_ref[:, rows - 1 : rows]
     sums = []
     for f in range(frames):
         sums += frame_sums([x_ref[f, r].astype(F32) for r in range(rows)])
@@ -115,7 +114,7 @@
     weights = weights_ref[...].reshape(-1, weights_ref.shape[2])
     window = cat(
         [
-            cat([line(sources[k], r + dy) for sources, r in outputs], axis=0)
+            cat([line(sources[k], r, dy) for sources, r in outputs], axis=0)
             for k in range(3)
             for dy in (-1, 0, 1)
         ],
@@ -133,41 +132,45 @@
     return [total[n * half : (n + 1) * half] for n in range(len(outputs))]
 
 
-def strided(lines, down_ref, k):
-    wide = down_ref.shape[1]
+def from_right(value, half):
+    column = iota(value.shape, 0) % half
+    return jnp.where(column == half - 1, 0.0, pltpu.roll(value, value.shape[0] - 1, 0))
+
+
+def tap_weights(down_ref, k, dy):
     channels = down_ref.shape[0] // 27
-    windows = [lines(dy) for dy in range(3)]
-    half = windows[0].shape[1]
-    windows = [w.reshape(-1, wide) for w in windows]
-    places = [(k * 9 + dy * 3) * channels for dy in range(3)]
-    both = cat([down_ref[at : at + 2 * channels] for at in places], axis=0)
-    next_even = cat([down_ref[at + 2 * channels : at + 3 * channels] for at in places], axis=0)
-    total = jnp.dot(cat(windows, axis=1), both, preferred_element_type=F32)
-    shifted = jnp.dot(
-        cat([w[:, :channels] for w in windows], axis=1), next_even, preferred_element_type=F32
-    )
-    size = total.shape[0]
-    column = iota(shifted.shape, 0) % half
-    shifted = jnp.where(column == half - 1, 0.0, pltpu.roll(shifted, size - 1, 0))
-    return (total + shifted).reshape(-1, half, wide)
-
-
-def hand_on(line, outputs, info_ref, first, down_ref, partial_ref):
+    at = (k * 9 + dy * 3) * channels
+    return down_ref[at : at + 2 * channels], down_ref[at + 2 * channels : at + 3 * channels]
+
+
+def strided(residual_ref, frames, down_ref, k):
+    rows, half, wide = residual_ref.shape[1] - 1, *residual_ref.shape[2:]
+    channels = wide // 2
+
+    def lines(picked):
+        return cat([residual_ref[f, r - 1] for f in frames for r in picked], axis=0)
+
+    zero, one = lines(range(2, rows, 2)), lines(range(1, rows, 2))
+    two = lines([*range(2, rows, 2), rows + 1])
+    (both_0, next_0), (both_1, next_1), (both_2, next_2) = (tap_weights(down_ref, k, dy) for dy in range(3))
+    dot = functools.partial(jnp.dot, preferred_element_type=F32)
+    total = dot(cat([one, two], axis=1), cat([both_1, both_2], axis=0))
+    evens = cat([one[:, :channels], two[:, :channels]], axis=1)
+    total = total + from_right(dot(evens, cat([next_1, next_2], axis=0)), half)
+    upper = dot(zero, both_0) + from_right(dot(zero[:, :channels], next_0), half)
+    total = total.reshape(len(frames), rows // 2, half, -1)
+    upper = upper.reshape(len(frames), rows // 2 - 1, half, -1)
+    return cat([total[:, :1], total[:, 1:] + upper], axis=1)
+
+
+def hand_on(residual_ref, info_ref, first, down_ref, partial_ref):
     begins = [info_ref[2, 0], info_ref[3, 0]]
     source = (begins[0] > first).astype(jnp.int32)
     takes = [(b <= first + 1).astype(F32) for b in begins]
-
-    def both(dy):
-        return jnp.stack([line(f, 2 * i + dy) for f in (source, 1) for i in outputs])
-
-    def second(dy):
-        return jnp.stack([line(1, 2 * i + dy) for i in outputs])
-
-    n = len(outputs)
-    older = strided(both, down_ref, 0)
-    newer = strided(second, down_ref, 1)
-    partial_ref[0] = ((older[:n] + newer) * takes[0]).astype(BF16)
-    partial_ref[1] = (older[n:] * takes[1]).astype(BF16)
+    older = strided(residual_ref, (source, 1), down_ref, 0)
+    newer = strided(residual_ref, (1,), down_ref, 1)
+    partial_ref[0] = ((older[0] + newer[0]) * takes[0]).astype(BF16)
+    partial_ref[1] = (older[1] * takes[1]).astype(BF16)
 
 
 def frame_sources(info_ref, first):
@@ -176,75 +179,89 @@
     ]
 
 
-def conv_first_kernel(which, bands, cells, clip_ref, *refs):
-    ins, (residual_ref, partial_ref, info_ref), scratch = refs[:12], refs[12:15], refs[15:]
-    info_ref[...] = clip_table(clip_ref, lax.axis_index("tm") * 2)
-    conv_kernel(which, bands, cells, info_ref, *ins, residual_ref, partial_ref, *scratch)
-
-
-def conv_kernel(which, bands, cells, *refs):
-    @pl.when(lax.axis_index("tm") % 2 == which)
-    def _():
-        convolve_frames(bands, cells, *refs)
+def on_core(which):
+    return pl.when(lax.axis_index("tm") % 2 == which)
+
+
+def second_core_kernel(bands, cells, down_ref, clip_ref, *refs):
+    ins, (residual_ref, edge_ref, partial_ref, info_ref), scratch = refs[:9], refs[9:13], refs[13:]
+    first = lax.axis_index("tm") * 2
+    info_ref[...] = clip_table(clip_ref, first)
+
+    @on_core(1)
+    def _():
+        convolve_frames(bands, cells, info_ref, *ins, residual_ref, edge_ref, *scratch)
+        hand_on(residual_ref, info_ref, first, down_ref, partial_ref)
+
+
+def first_core_kernel(bands, cells, other_edge_ref, info_ref, *refs):
+    ins, (residual_ref, edge_ref), scratch = refs[:9], refs[9:11], refs[11:]
+
+    @on_core(0)
+    def _():
+        convolve_frames(bands, cells, info_ref, *ins, residual_ref, edge_ref, *scratch)
+
+    @on_core(1)
+    def _():
+        edge_ref[...] = other_edge_ref[...]
 
 
 def convolve_frames(
-    bands, cells, info_ref, rows_ref, bias_ref, gain_ref, offset_ref, weight_ref, down_ref,
-    x_ref, before_ref, above_ref, above_before_ref, below_ref, below_before_ref,
-    residual_ref, partial_ref, hidden, own, weights, slots,
+    bands, cells, info_ref, rows_ref, bias_ref, gain_ref, offset_ref, weight_ref,
+    x_ref, before_ref, below_ref, below_before_ref,
+    residual_ref, edge_ref, hidden, own, weights, slots,
 ):
     rows, cols, channels = x_ref.shape[1:]
     first = lax.axis_index("tm") * 2
-    band = lax.axis_index("band")
-    keep_above = (band > 0).astype(F32)
-    keep_below = (band < bands - 1).astype(F32)
+    keep = (lax.axis_index("band") < bands - 1).astype(F32)
     arrange(weight_ref, weights)
     bias = bias_ref[...]
     stats = scale_and_shift(rows_ref[...], info_ref, gain_ref[...], offset_ref[...], cells, bands)
     stats = [0.5 * v for pair in stats for v in pair]
     for frame in range(4):
         scale, shift = stats[2:] if frame == 3 else stats[:2]
-        body, above, below = (
-            (before_ref, above_before_ref, below_before_ref)
-            if frame < 2
-            else (x_ref, above_ref, below_ref)
-        )
+        body, below = (before_ref, below_before_ref) if frame < 2 else (x_ref, below_ref)
         f = frame % 2
-        lines = [above.at[f, 0]] + [body.at[f, r] for r in range(rows)] + [below.at[f, r] for r in range(2)]
+        lines = [body.at[f, r] for r in range(rows)] + [below.at[f, r] for r in range(2)]
         for n, line in enumerate(lines):
             slot = slots.at[n]
             slot[...] = line[...].astype(F32)
             for side in range(2):
                 lanes = pl.ds(side * channels, channels)
                 value = slot[pl.ds(side, cols // 2, 2), :]
-                if frame >= 2 and 1 <= n < rows + 2:
+                if frame >= 2 and 1 <= n <= rows:
                     own[f, n - 1, :, lanes] = value.astype(BF16)
                 value = activated(value, scale, shift)
-                if n == 0:
-                    value = value * keep_above
-                if n > rows:
-                    value = value * keep_below
                 hidden[frame, n, :, lanes] = value.astype(BF16)
+                if n in (rows - 1, rows):
+                    hidden[frame, n + 3, :, lanes] = (value * keep).astype(BF16)
+
+    def line(source, r, dy):
+        across = (r, dy) in ((rows - 1, 1), (rows, -1))
+        return hidden[source, r + dy + (3 if across else 0)]
+
     sources = frame_sources(info_ref, first)
     bias = cat([bias, bias], axis=1)
     for f in range(2):
-        found = convolve(
-            lambda source, r: hidden[source, r + 1], weights, [(sources[f], r) for r in range(rows + 1)]
-        )
-        for r, total in enumerate(found):
-            value = total + own[f, r].astype(F32) + bias
-            if r == rows:
-                value = value * keep_below
-            residual_ref[f, r] = value.astype(BF16)
-    hand_on(
-        lambda f, r: residual_ref[f, r], range(rows // 2), info_ref, first, down_ref, partial_ref
-    )
+        found = convolve(line, weights, [(sources[f], r) for r in range(1, rows + 1)])
+        for n, total in enumerate(found):
+            value = total + own[f, n].astype(F32) + bias
+            residual_ref[f, n] = value.astype(BF16)
+            if n == rows - 1:
+                residual_ref[f, rows] = (value * keep).astype(BF16)
+                edge_ref[f] = value.astype(BF16)
+
+
+def hand_on_kernel(info_ref, residual_ref, down_ref, partial_ref):
+    @on_core(0)
+    def _():
+        hand_on(residual_ref, info_ref, lax.axis_index("tm") * 2, down_ref, partial_ref)
 
 
 def local_kernel(info_ref, first_core_ref, second_core_ref, down_ref, out_ref):
     for which, residual_ref in enumerate((first_core_ref, second_core_ref)):
 
-        @pl.when(lax.axis_index("tm") % 2 == which)
+        @on_core(which)
         def _(residual_ref=residual_ref):
             local_part(info_ref, residual_ref, down_ref, out_ref)
 
@@ -252,32 +269,44 @@
 def local_part(info_ref, residual_ref, down_ref, out_ref):
     first = lax.axis_index("tm") * 2
     begins = [info_ref[0, 0], info_ref[1, 0]]
-    count = out_ref.shape[1]
-
-    def lines(*picked):
-        return lambda dy: jnp.stack([residual_ref[f, 2 * i + dy] for f in picked for i in range(count)])
-
-    base = strided(lines(0, 1), down_ref, 2)
-    out_ref[0] = base[:count]
-    out_ref[1] = base[count:] + strided(lines((begins[1] > first).astype(jnp.int32)), down_ref, 1)
+    base = strided(residual_ref, (0, 1), down_ref, 2)
+    out_ref[0] = base[0]
+    out_ref[1] = base[1] + strided(residual_ref, ((begins[1] > first).astype(jnp.int32),), down_ref, 1)[0]
 
     @pl.when(begins[0] == first)
     def _():
-        out_ref[0] += strided(lines(0), down_ref, 0) + strided(lines(0), down_ref, 1)
+        out_ref[0] += strided(residual_ref, (0,), down_ref, 0)[0] + strided(residual_ref, (0,), down_ref, 1)[0]
 
     @pl.when(begins[1] >= first)
     def _():
-        out_ref[1] += strided(lines(begins[1] - first), down_ref, 0)
-
-
-def join_kernel(local_ref, between_ref, within_ref, reduced_ref, row_ref):
-    frames, lines, half, channels = local_ref.shape
+        out_ref[1] += strided(residual_ref, (begins[1] - first,), down_ref, 0)[0]
+
+
+def row_zero_kernel(info_ref, edge_before_ref, edge_ref, down_ref, out_ref, four):
+    half, wide = edge_ref.shape[1:]
+    four[0:2] = edge_before_ref[...]
+    four[2:4] = edge_ref[...]
+    sources = frame_sources(info_ref, lax.axis_index("tm") * 2)
+    weights = [tap_weights(down_ref, k, 0) for k in range(3)]
+    lines = cat([cat([four[s] for s in sources[f]], axis=1) for f in range(2)], axis=0)
+    evens = cat([lines[:, k * wide : k * wide + wide // 2] for k in range(3)], axis=1)
+    total = jnp.dot(lines, cat([w[0] for w in weights], axis=0), preferred_element_type=F32)
+    shifted = jnp.dot(evens, cat([w[1] for w in weights], axis=0), preferred_element_type=F32)
+    out_ref[...] = (total + from_right(shifted, half)).reshape(out_ref.shape)
+
+
+def first_line_kernel(upper_ref, local_ref, between_ref, out_ref):
+    out_ref[...] = upper_ref[...] + local_ref[:, 0] + between_ref[:, 0].astype(F32)
+
+
+def join_kernel(first_line_ref, local_ref, between_ref, within_ref, reduced_ref, row_ref):
+    frames, lines = local_ref.shape[:2]
     sums = []
     for f in range(frames):
         values = []
         for i in range(lines):
-            sent = between_ref[f, i].astype(F32) + within_ref[f, i].astype(F32)
-            v = (local_ref[f, i] + sent).astype(BF16)
+            v = first_line_ref[f] if i == 0 else local_ref[f, i] + between_ref[f, i].astype(F32)
+            v = (v + within_ref[f, i].astype(F32)).astype(BF16)
             reduced_ref[f, i] = v
             values.append(v.astype(F32))
         sums += frame_sums(values)
@@ -337,48 +366,47 @@
         return lax.all_to_all(row, ("tm", "band"), 0, 0, tiled=True).reshape(devices, 128)
 
     before = passed_on(frames_in, 1, 0)
-    row, top, bottom = call(
+    row, top = call(
         sums_kernel,
-        (
-            everyone,
-            shape((frames, 2, cols, channels), BF16),
-            shape((frames, 1, cols, channels), BF16),
-        ),
+        (everyone, shape((frames, 2, cols, channels), BF16)),
         [VMEM],
         flops=1 << 33,
         moved=1 << 20,
     )(frames_in)
     below_before, below = passed_on(top, 1, -1), passed_on(top, 0, -1)
-    above_before, above = passed_on(bottom, 1, 1), passed_on(bottom, 0, 1)
     sums = exchange(row)
     down = down_weight.reshape(-1, wide)
     pair = (half, 2 * channels)
-    def conv(kernel, which, info, *more):
+    def conv(kernel, given, ranges, *made):
         cells = float(bands * rows * cols * (channels // GROUPS))
         return call(
-            functools.partial(kernel, which, bands, cells),
-            (shape((frames, rows + 1, *pair), BF16), shape((frames, lines, half, wide), BF16), *more),
-            [VMEM] * 13,
+            functools.partial(kernel, bands, cells),
+            (shape((frames, rows + 1, *pair), BF16), shape((frames, *pair), BF16), *made),
+            [VMEM] * 11,
             scratch=[
-                pltpu.VMEM((4, rows + 3, *pair), BF16),
-                pltpu.VMEM((frames, rows + 1, *pair), BF16),
+                pltpu.VMEM((4, rows + 4, *pair), BF16),
+                pltpu.VMEM((frames, rows, *pair), BF16),
                 pltpu.VMEM((9, 2 * channels, 4 * channels), BF16),
-                pltpu.VMEM((rows + 3, cols, channels), F32),
+                pltpu.VMEM((rows + 2, cols, channels), F32),
             ],
             megabytes=24,
             flops=5 << 30,
             moved=1 << 23,
         )(
-            info, sums, conv_bias.reshape(1, -1), norm_gain.reshape(1, -1),
-            norm_shift.reshape(1, -1), conv_weight.reshape(9, 3, channels, channels), down,
-            frames_in, before, above, above_before, below, below_before,
+            given, ranges, sums, conv_bias.reshape(1, -1), norm_gain.reshape(1, -1), norm_shift.reshape(1, -1),
+            conv_weight.reshape(9, 3, channels, channels), frames_in, before, below, below_before,
         )
 
-    second_core, partial, info = conv(
-        conv_first_kernel, 1, clip_id.reshape(1, -1), shape((8, 128), jnp.int32)
+    sent = shape((frames, lines, half, wide), BF16)
+    second_core, edge, partial, info = conv(
+        second_core_kernel, down, clip_id.reshape(1, -1), sent, shape((8, 128), jnp.int32)
     )
     between = between_chips(partial)
-    first_core, partial = conv(conv_kernel, 0, info)
+    first_core, edge = conv(first_core_kernel, edge, info)
+    edge, edge_before = passed_on(edge, 0, 1), passed_on(edge, 1, 1)
+    partial = call(hand_on_kernel, sent, [VMEM] * 3, megabytes=12, flops=1 << 30, moved=1 << 22)(
+        info, first_core, down
+    )
     within = within_chips(partial)
     local = call(
         local_kernel,
@@ -388,13 +416,18 @@
         flops=1 << 31,
         moved=1 << 22,
     )(info, first_core, second_core, down)
+    line = shape((frames, half, wide), F32)
+    upper = call(
+        row_zero_kernel, line, [VMEM] * 4, scratch=[pltpu.VMEM((4, *pair), BF16)], megabytes=6
+    )(info, edge_before, edge, down)
+    first_line = call(first_line_kernel, line, [VMEM] * 3, flops=1 << 32)(upper, local, between)
     reduced, row = call(
         join_kernel,
         (shape((frames, lines, half, wide), BF16), everyone),
-        [VMEM] * 3,
+        [VMEM] * 4,
         megabytes=8,
         moved=1 << 21,
-    )(local, between, within)
+    )(first_line, local, between, within)
     return call(
         functools.partial(out_kernel, bands, float(bands * lines * half * (wide // GROUPS))),
         shape((frames, lines, half, wide), BF16),

time: 62.5 us -> 60.9 us (0.974)
  starting transfers between devices: 11.8 us -> 9.12 us
  waiting for transfers between devices: 2.8 us -> 4.36 us
    ppermute x5, waiting for transfers between devices: 0.01 us -> 4.35 us  [passed_on(): return lax.ppermute(array, ('tm', 'band'), pairs)]
    ppermute x1, waiting for transfers between devices: 2.79 us -> 0.01 us  [between_chips(): lax.ppermute(array, 'tm', [(i, i + 1) for i in range(1, lax.axis_size('tm...]
    ppermute x5, starting transfers between devices: 9.21 us -> 6.51 us  [passed_on(): return lax.ppermute(array, ('tm', 'band'), pairs)]
    pallas_call x3 -> x6, Pallas kernels: 9.69 us -> 9.33 us  [the longest x2 8.56 us: conv(): call(functools.partial(kernel, bands, cells), (shape((frames, rows + 1, *...]
  transfers between devices with their start and end apart: 7 -> 7, of which waited for: 1 -> 2; matrix products, arithmetic and copies ran while one was open for 0% -> 0% of each run, Pallas kernels for 4% -> 4%
where the time goes in v3:
time: 60.9 us; the launch traced here: 60.7 us
  blocking collectives  33.2 us (55%)
  Pallas kernels  12.5 us (21%)
  starting transfers between devices  9.12 us (15%)
  waiting for transfers between devices  4.36 us (7%)
  local copies, waits for them, and re-layouts  1.3 us (2%)
    all_to_all x2, blocking collectives, exchange(): lax.all_to_all(row, ('tm', 'band'), 0, 0, tiled=True).reshape(devices, 128)  33.2 us
    pallas_call x2, Pallas kernels, conv(): call(functools.partial(kernel, bands, cells), (shape((frames, rows + 1, *...  8.56 us
    ppermute x5, starting transfers between devices, passed_on(): return lax.ppermute(array, ('tm', 'band'), pairs)  6.51 us
    ppermute x5, waiting for transfers between devices, passed_on(): return lax.ppermute(array, ('tm', 'band'), pairs)  4.35 us
    pallas_call x1, Pallas kernels, on_device(): call(local_kernel, shape((frames, lines, half, wide), F32), [VMEM] * 4, m...  1.64 us
    ppermute x1, starting transfers between devices, between_chips(): lax.ppermute(array, 'tm', [(i, i + 1) for i in range(1, lax.axis_size('tm...  1.32 us
    unnamed x20, local copies, waits for them, and re-layouts  1.3 us
    ppermute x1, starting transfers between devices, within_chips(): lax.ppermute(array, 'tm', [(i, i + 1) for i in range(0, lax.axis_size('tm...  1.28 us
  transfers between devices with their start and end apart: 7, of which 2 were waited for; matrix products, arithmetic and copies ran while one was open for 0% of the time, Pallas kernels for 4%

profile of v3, /device:TPU:1, one launch (start us, length us, event | category | flops | bytes accessed | tf_op | source)
XLA Modules:
  0.0 60.7 jit_solution(216529275011252767)
XLA Ops:
  0.0 0.0 copy-start
  0.0 3.0 %collective-permute-start = (bf16[2,8,256,128]{3,2,1,0:T(8,128)(2,1)}, bf16[2,8,256,128]{3,2,1,0:T(8,128)(2,1)S(1)}, u32[]{:S(2)}, u32[]{:S(2)}) collective-permute-start(bf16[2,8,256,128]{3,2,1,0:T(8,128)(2,1)} %refs_5_.3), channel_id=1, source_target_pairs={{0,4},{1,5},{2,6},{3,7},{4,8},{5,9},{6,10},{7,11},{8,12},{9,13},{1... | collective-permute-start | bytes 3145736 | tf_op jit(solution)/shard_map/ppermute | solution.py:344
  3.0 0.0 copy-start.3
  3.0 1.3 %copy-done.3 = bf16[2,8,256,128]{3,2,1,0:T(8,128)(2,1)S(1)} copy-done((bf16[2,8,256,128]{3,2,1,0:T(8,128)(2,1)S(1)}, bf16[2,8,256,128]{3,2,1,0:T(8,128)(2,1)}, u32[]{:S(2)}) %copy-start.3) | copy-done | bytes 1048600
  4.3 0.0 copy-start.4
  4.3 0.0 copy-start.5
  4.3 0.0 copy-start.6
  4.3 0.0 copy-start.7
  4.3 0.0 copy-start.8
  4.3 0.0 copy-start.9
  4.3 0.4 shard_map.91
  4.7 2.6 %collective-permute-start.2 = (bf16[2,2,256,128]{3,2,1,0:T(8,128)(2,1)S(1)}, bf16[2,2,256,128]{3,2,1,0:T(8,128)(2,1)S(1)}, u32[]{:S(2)}, u32[]{:S(2)}) collective-permute-start(bf16[2,2,256,128]{3,2,1,0:T(8,128)(2,1)S(1)} %get-tuple-element.16), channel_id=1, source_target_pairs={{0,7},{1,4},{2,5},{3,6},{4,11},{5,8},{6,9},{7,10},{8,15},{9,12},{1... | collective-permute-start | bytes 786440 | tf_op jit(solution)/shard_map/ppermute | solution.py:344
  7.3 0.5 collective-permute-start.1
  7.8 18.2 %all_to_all.10 = f32[128,1,128]{2,1,0:T(1,128)S(1)} all-to-all(f32[128,1,128]{2,1,0:T(1,128)S(1)} %get-tuple-element.15), channel_id=1, replica_groups=mesh['tm'=32,'band'=4] {'tm','band'}, dimensions={0} | all-to-all | bytes 131072 | tf_op jit(solution)/shard_map/all_to_all | solution.py:366
  26.0 0.0 collective-permute-done.2.refs_8_
  26.0 0.0 collective-permute-done.1.refs_7_
  26.0 0.0 collective-permute-done.refs_6_
  26.0 0.0 copy-done
  26.0 0.0 copy-done.4
  26.0 0.0 copy-done.5
  26.0 0.0 copy-done.6
  26.0 0.0 copy-done.7
  26.0 0.0 copy-done.8
  26.0 0.0 copy-done.9
  26.0 8.3 %shard_map.92 = (bf16[2,9,128,256]{3,2,1,0:T(8,128)(2,1)S(1)}, bf16[2,128,256]{2,1,0:T(8,128)(2,1)S(1)}, bf16[2,4,128,256]{3,2,1,0:T(8,128)(2,1)S(1)}, s32[8,128]{1,0:T(8,128)S(1)}) custom-call(bf16[3456,256]{1,0:T(8,128)(2,1)S(1)} %bitcast.10, s32[1,64]{1,0:T(1,128)S(1)} %bitcast.21, f32[128,128]{1,0:T(8,128)S(1)} %bitcast.15, f32[1,128]{1,0:T(1,128)S(1)} %bitcast.22, ...), custom_call_target="tpu_custom_call" | custom-call | flops 5368709120 | bytes 8388608 | tf_op jit(solution)/shard_map/pallas_call | solution.py:382
  34.4 1.3 %collective-permute-start.5 = (bf16[2,4,128,256]{3,2,1,0:T(8,128)(2,1)S(1)}, bf16[2,4,128,256]{3,2,1,0:T(8,128)(2,1)S(1)}, u32[]{:S(2)}, u32[]{:S(2)}) collective-permute-start(bf16[2,4,128,256]{3,2,1,0:T(8,128)(2,1)S(1)} %get-tuple-element.22), channel_id=1, source_target_pairs={{4,8},{12,16},{20,24},{28,32},{36,40},{44,48},{52,56},{60,64},{68,... | collective-permute-start | bytes 1572872 | tf_op jit(solution)/shard_map/ppermute | solution.py:348
  35.7 0.2 shard_map.93
  35.9 0.4 collective-permute-start.4
  36.3 0.0 collective-permute-start.3
  36.4 1.3 %collective-permute-start.6 = (bf16[2,4,128,256]{3,2,1,0:T(8,128)(2,1)S(1)}, bf16[2,4,128,256]{3,2,1,0:T(8,128)(2,1)S(1)}, u32[]{:S(2)}, u32[]{:S(2)}) collective-permute-start(bf16[2,4,128,256]{3,2,1,0:T(8,128)(2,1)S(1)} %shard_map.97), channel_id=1, source_target_pairs={{0,4},{8,12},{16,20},{24,28},{32,36},{40,44},{48,52},{56,60},{64,6... | collective-permute-start | bytes 1572872 | tf_op jit(solution)/shard_map/ppermute | solution.py:352
  37.6 1.6 %shard_map.95.local_ref = f32[2,4,128,256]{3,2,1,0:T(8,128)S(1)} custom-call(s32[8,128]{1,0:T(8,128)S(1)} %get-tuple-element.17.info_ref, bf16[2,9,128,256]{3,2,1,0:T(8,128)(2,1)S(1)} %get-tuple-element.20.first_core_ref.residual_ref, bf16[2,9,128,256]{3,2,1,0:T(8,128)(2,1)S(1)} %get-tuple-element.21.second_core_ref, bf16[3456,256]{1,0:T(8,128)(2,1)S(1)} %bitcast.12), custom_call_target="tpu_custom_call" | custom-call | flops 2147483648 | bytes 4194304 | tf_op jit(solution)/shard_map/pallas_call | solution.py:411
  39.3 2.4 %collective-permute-done.4.edge_ref = bf16[2,128,256]{2,1,0:T(8,128)(2,1)S(1)} collective-permute-done((bf16[2,128,256]{2,1,0:T(8,128)(2,1)S(1)}, bf16[2,128,256]{2,1,0:T(8,128)(2,1)S(1)}, u32[]{:S(2)}, u32[]{:S(2)}) %collective-permute-start.4) | collective-permute-done | bytes 131104 | tf_op jit(solution)/shard_map/ppermute | solution.py:344
  41.7 1.9 %collective-permute-done.3.edge_before_ref = bf16[2,128,256]{2,1,0:T(8,128)(2,1)S(1)} collective-permute-done((bf16[2,128,256]{2,1,0:T(8,128)(2,1)S(1)}, bf16[2,128,256]{2,1,0:T(8,128)(2,1)S(1)}, u32[]{:S(2)}, u32[]{:S(2)}) %collective-permute-start.3) | collective-permute-done | bytes 131104 | tf_op jit(solution)/shard_map/ppermute | solution.py:344
  43.6 0.4 shard_map.94.upper_ref
  44.0 0.0 collective-permute-done.5.between_ref
  44.1 0.0 copy-start.1
  44.1 0.0 copy-start.2
  44.1 0.0 collective-permute-done.6.within_ref
  44.1 0.5 shard_map.98
  44.6 15.1 %all_to_all.11 = f32[128,1,128]{2,1,0:T(1,128)S(1)} all-to-all(f32[128,1,128]{2,1,0:T(1,128)S(1)} %get-tuple-element.23), channel_id=1, replica_groups=mesh['tm'=32,'band'=4] {'tm','band'}, dimensions={0} | all-to-all | bytes 131072 | tf_op jit(solution)/shard_map/all_to_all | solution.py:366
  59.6 0.0 copy-done.1
  59.6 0.0 copy-done.2
  59.6 1.1 %shard_map.99 = bf16[2,4,128,256]{3,2,1,0:T(8,128)(2,1)} custom-call(f32[128,128]{1,0:T(8,128)S(1)} %bitcast.14, s32[8,128]{1,0:T(8,128)S(1)} %get-tuple-element.17.info_ref, f32[1,256]{1,0:T(1,128)S(1)} %bitcast.17, f32[1,256]{1,0:T(1,128)S(1)} %bitcast.18, bf16[2,4,128,256]{3,2,1,0:T(8,128)(2,1)S(1)} %get-tuple-element.24.reduced_ref), custom_call_target="tpu_custom_call" | custom-call | bytes 1048576 | tf_op jit(solution)/shard_map/pallas_call | solution.py:431
  (2 shorter events, 0.0 us)
Async XLA Ops:
  0.0 26.0 %copy-start = (bf16[3,3,3,128,256]{4,3,2,1,0:T(8,128)(2,1)S(1)}, bf16[3,3,3,128,256]{4,3,2,1,0:T(8,128)(2,1)}, u32[]{:S(2)}) copy-start(bf16[3,3,3,128,256]{4,3,2,1,0:T(8,128)(2,1)} %param.15) | copy-start | bytes 5308420
  0.0 26.0 %collective-permute-start = (bf16[2,8,256,128]{3,2,1,0:T(8,128)(2,1)}, bf16[2,8,256,128]{3,2,1,0:T(8,128)(2,1)S(1)}, u32[]{:S(2)}, u32[]{:S(2)}) collective-permute-start(bf16[2,8,256,128]{3,2,1,0:T(8,128)(2,1)} %refs_5_.3), channel_id=1, source_target_pairs={{0,4},{1,5},{2,6},{3,7},{4,8},{5,9},{6,10},{7,11},{8,12},{9,13},{1... | collective-permute-start | bytes 3145736 | tf_op jit(solution)/shard_map/ppermute | solution.py:344
  3.0 1.3 %copy-start.3 = (bf16[2,8,256,128]{3,2,1,0:T(8,128)(2,1)S(1)}, bf16[2,8,256,128]{3,2,1,0:T(8,128)(2,1)}, u32[]{:S(2)}) copy-start(bf16[2,8,256,128]{3,2,1,0:T(8,128)(2,1)} %refs_5_.3) | copy-start | bytes 3145732
  4.3 21.7 %copy-start.4 = (bf16[2,8,256,128]{3,2,1,0:T(8,128)(2,1)S(1)}, bf16[2,8,256,128]{3,2,1,0:T(8,128)(2,1)}, u32[]{:S(2)}) copy-start(bf16[2,8,256,128]{3,2,1,0:T(8,128)(2,1)} %refs_5_.3) | copy-start | bytes 3145732
  4.3 21.7 %copy-start.5 = (bf16[3,3,3,128,128]{4,3,2,1,0:T(8,128)(2,1)S(1)}, bf16[3,3,3,128,128]{4,3,2,1,0:T(8,128)(2,1)}, u32[]{:S(2)}) copy-start(bf16[3,3,3,128,128]{4,3,2,1,0:T(8,128)(2,1)} %param.11) | copy-start | bytes 2654212
  4.3 21.7 %copy-start.6 = (s32[64]{0:T(128)S(1)}, s32[64]{0:T(128)}, u32[]{:S(2)}) copy-start(s32[64]{0:T(128)} %param.10) | copy-start | bytes 772
  4.3 21.7 %copy-start.7 = (f32[128]{0:T(128)S(1)}, f32[128]{0:T(128)}, u32[]{:S(2)}) copy-start(f32[128]{0:T(128)} %param.12) | copy-start | bytes 1540
  4.3 21.7 %copy-start.8 = (f32[128]{0:T(128)S(1)}, f32[128]{0:T(128)}, u32[]{:S(2)}) copy-start(f32[128]{0:T(128)} %param.13) | copy-start | bytes 1540
  4.3 21.7 %copy-start.9 = (f32[128]{0:T(128)S(1)}, f32[128]{0:T(128)}, u32[]{:S(2)}) copy-start(f32[128]{0:T(128)} %param.14) | copy-start | bytes 1540
  4.7 21.3 %collective-permute-start.2 = (bf16[2,2,256,128]{3,2,1,0:T(8,128)(2,1)S(1)}, bf16[2,2,256,128]{3,2,1,0:T(8,128)(2,1)S(1)}, u32[]{:S(2)}, u32[]{:S(2)}) collective-permute-start(bf16[2,2,256,128]{3,2,1,0:T(8,128)(2,1)S(1)} %get-tuple-element.16), channel_id=1, source_target_pairs={{0,7},{1,4},{2,5},{3,6},{4,11},{5,8},{6,9},{7,10},{8,15},{9,12},{1... | collective-permute-start | bytes 786440 | tf_op jit(solution)/shard_map/ppermute | solution.py:344
  7.3 18.6 %collective-permute-start.1 = (bf16[2,2,256,128]{3,2,1,0:T(8,128)(2,1)S(1)}, bf16[2,2,256,128]{3,2,1,0:T(8,128)(2,1)S(1)}, u32[]{:S(2)}, u32[]{:S(2)}) collective-permute-start(bf16[2,2,256,128]{3,2,1,0:T(8,128)(2,1)S(1)} %get-tuple-element.16), channel_id=1, source_target_pairs={{0,3},{1,0},{2,1},{3,2},{4,7},{5,4},{6,5},{7,6},{8,11},{9,8},{10,9... | collective-permute-start | bytes 786440 | tf_op jit(solution)/shard_map/ppermute | solution.py:344
  34.4 9.6 %collective-permute-start.5 = (bf16[2,4,128,256]{3,2,1,0:T(8,128)(2,1)S(1)}, bf16[2,4,128,256]{3,2,1,0:T(8,128)(2,1)S(1)}, u32[]{:S(2)}, u32[]{:S(2)}) collective-permute-start(bf16[2,4,128,256]{3,2,1,0:T(8,128)(2,1)S(1)} %get-tuple-element.22), channel_id=1, source_target_pairs={{4,8},{12,16},{20,24},{28,32},{36,40},{44,48},{52,56},{60,64},{68,... | collective-permute-start | bytes 1572872 | tf_op jit(solution)/shard_map/ppermute | solution.py:348
  35.9 5.8 %collective-permute-start.4 = (bf16[2,128,256]{2,1,0:T(8,128)(2,1)S(1)}, bf16[2,128,256]{2,1,0:T(8,128)(2,1)S(1)}, u32[]{:S(2)}, u32[]{:S(2)}) collective-permute-start(bf16[2,128,256]{2,1,0:T(8,128)(2,1)S(1)} %get-tuple-element.19), channel_id=1, source_target_pairs={{0,1},{1,2},{2,3},{3,0},{4,5},{5,6},{6,7},{7,4},{8,9},{9,10},{10,1... | collective-permute-start | bytes 393224 | tf_op jit(solution)/shard_map/ppermute | solution.py:344
  36.3 7.3 %collective-permute-start.3 = (bf16[2,128,256]{2,1,0:T(8,128)(2,1)S(1)}, bf16[2,128,256]{2,1,0:T(8,128)(2,1)S(1)}, u32[]{:S(2)}, u32[]{:S(2)}) collective-permute-start(bf16[2,128,256]{2,1,0:T(8,128)(2,1)S(1)} %get-tuple-element.19), channel_id=1, source_target_pairs={{0,5},{1,6},{2,7},{3,4},{4,9},{5,10},{6,11},{7,8},{8,13},{9,14},{1... | collective-permute-start | bytes 393224 | tf_op jit(solution)/shard_map/ppermute | solution.py:344
  36.4 7.7 %collective-permute-start.6 = (bf16[2,4,128,256]{3,2,1,0:T(8,128)(2,1)S(1)}, bf16[2,4,128,256]{3,2,1,0:T(8,128)(2,1)S(1)}, u32[]{:S(2)}, u32[]{:S(2)}) collective-permute-start(bf16[2,4,128,256]{3,2,1,0:T(8,128)(2,1)S(1)} %shard_map.97), channel_id=1, source_target_pairs={{0,4},{8,12},{16,20},{24,28},{32,36},{40,44},{48,52},{56,60},{64,6... | collective-permute-start | bytes 1572872 | tf_op jit(solution)/shard_map/ppermute | solution.py:352
  44.1 15.6 %copy-start.1 = (f32[256]{0:T(256)S(1)}, f32[256]{0:T(256)}, u32[]{:S(2)}) copy-start(f32[256]{0:T(256)} %param.16) | copy-start | bytes 3076
  44.1 15.6 %copy-start.2 = (f32[256]{0:T(256)S(1)}, f32[256]{0:T(256)}, u32[]{:S(2)}) copy-start(f32[256]{0:T(256)} %param.17) | copy-start | bytes 3076

commit v4 on v3

--- a/solution.py
+++ b/solution.py
@@ -32,11 +32,20 @@
     return found[:n] + found[n : 2 * n] + found[2 * n : 3 * n]
 
 
-def pack_row(sums):
+def group_matrix(channels):
+    size = channels // GROUPS
+    return (iota((channels, 128), 0) // size == iota((channels, 128), 1) % GROUPS).astype(F32)
+
+
+def matrix_kernel(out_ref):
+    out_ref[...] = group_matrix(out_ref.shape[0])
+
+
+def pack_row(sums, gather=None):
     channels = sums[0].shape[1]
-    size = channels // GROUPS
-    gather = iota((channels, 128), 0) // size == iota((channels, 128), 1) % GROUPS
-    grouped = exact_dot(cat(sums, axis=0), gather.astype(F32))
+    if gather is None:
+        gather = group_matrix(channels)
+    grouped = exact_dot(cat(sums, axis=0), gather)
     place = iota((4, 128), 1) // GROUPS == iota((4, 128), 0)
     return jnp.sum(jnp.where(place, grouped, 0.0), axis=0, keepdims=True)
 
@@ -75,13 +84,13 @@
     return found
 
 
-def sums_kernel(x_ref, row_ref, top_ref):
+def sums_kernel(x_ref, gather_ref, row_ref, top_ref):
     frames, rows = x_ref.shape[:2]
     top_ref[...] = x_ref[:, 0:2]
     sums = []
     for f in range(frames):
         sums += frame_sums([x_ref[f, r].astype(F32) for r in range(rows)])
-    row_ref[...] = jnp.broadcast_to(pack_row(sums)[None], row_ref.shape)
+    row_ref[...] = jnp.broadcast_to(pack_row(sums, gather_ref[...])[None], row_ref.shape)
 
 
 def arrange(weight_ref, weights):
@@ -366,13 +375,14 @@
         return lax.all_to_all(row, ("tm", "band"), 0, 0, tiled=True).reshape(devices, 128)
 
     before = passed_on(frames_in, 1, 0)
+    gather = call(matrix_kernel, shape((channels, 128), F32), [], flops=1 << 29)()
     row, top = call(
         sums_kernel,
         (everyone, shape((frames, 2, cols, channels), BF16)),
-        [VMEM],
+        [VMEM] * 2,
         flops=1 << 33,
         moved=1 << 20,
-    )(frames_in)
+    )(frames_in, gather)
     below_before, below = passed_on(top, 1, -1), passed_on(top, 0, -1)
     sums = exchange(row)
     down = down_weight.reshape(-1, wide)

time: 60.9 us -> 60.6 us (level)
  local copies, waits for them, and re-layouts: 1.3 us -> 0.05 us
  starting transfers between devices: 9.12 us -> 10.2 us
    unnamed x20 -> x18, local copies, waits for them, and re-layouts: 1.3 us -> 0.05 us
    ppermute x5, starting transfers between devices: 6.51 us -> 7.64 us  [passed_on(): return lax.ppermute(array, ('tm', 'band'), pairs)]
where the time goes in v4:
time: 60.6 us; the launch traced here: 60.4 us
  blocking collectives  33 us (54%)
  Pallas kernels  12.6 us (21%)
  starting transfers between devices  10.2 us (17%)
  waiting for transfers between devices  4.35 us (7%)
    all_to_all x2, blocking collectives, exchange(): lax.all_to_all(row, ('tm', 'band'), 0, 0, tiled=True).reshape(devices, 128)  33 us
    pallas_call x2, Pallas kernels, conv(): call(functools.partial(kernel, bands, cells), (shape((frames, rows + 1, *...  8.54 us
    ppermute x5, starting transfers between devices, passed_on(): return lax.ppermute(array, ('tm', 'band'), pairs)  7.64 us
    ppermute x5, waiting for transfers between devices, passed_on(): return lax.ppermute(array, ('tm', 'band'), pairs)  4.34 us
    pallas_call x1, Pallas kernels, on_device(): call(local_kernel, shape((frames, lines, half, wide), F32), [VMEM] * 4, m...  1.66 us
    ppermute x1, starting transfers between devices, between_chips(): lax.ppermute(array, 'tm', [(i, i + 1) for i in range(1, lax.axis_size('tm...  1.32 us
    ppermute x1, starting transfers between devices, within_chips(): lax.ppermute(array, 'tm', [(i, i + 1) for i in range(0, lax.axis_size('tm...  1.28 us
  transfers between devices with their start and end apart: 7, of which 2 were waited for; matrix products, arithmetic and copies ran while one was open for 0% of the time, Pallas kernels for 4%

profile of v4, /device:TPU:1, one launch (start us, length us, event | category | flops | bytes accessed | tf_op | source)
XLA Modules:
  0.0 60.4 jit_solution(9235181360532589802)
XLA Ops:
  0.0 0.0 copy-start.3
  0.0 3.0 %collective-permute-start = (bf16[2,8,256,128]{3,2,1,0:T(8,128)(2,1)}, bf16[2,8,256,128]{3,2,1,0:T(8,128)(2,1)S(1)}, u32[]{:S(2)}, u32[]{:S(2)}) collective-permute-start(bf16[2,8,256,128]{3,2,1,0:T(8,128)(2,1)} %refs_5_.3), channel_id=1, source_target_pairs={{0,4},{1,5},{2,6},{3,7},{4,8},{5,9},{6,10},{7,11},{8,12},{9,13},{1... | collective-permute-start | bytes 3145736 | tf_op jit(solution)/shard_map/ppermute | solution.py:353
  3.0 0.0 copy-done.3
  3.1 0.0 copy-start
  3.1 0.0 copy-start.4
  3.1 0.0 copy-start.5
  3.1 0.0 copy-start.6
  3.1 0.0 copy-start.7
  3.1 0.0 copy-start.8
  3.1 0.4 shard_map.92
  3.5 3.7 %collective-permute-start.2 = (bf16[2,2,256,128]{3,2,1,0:T(8,128)(2,1)S(1)}, bf16[2,2,256,128]{3,2,1,0:T(8,128)(2,1)S(1)}, u32[]{:S(2)}, u32[]{:S(2)}) collective-permute-start(bf16[2,2,256,128]{3,2,1,0:T(8,128)(2,1)S(1)} %get-tuple-element.16), channel_id=1, source_target_pairs={{0,7},{1,4},{2,5},{3,6},{4,11},{5,8},{6,9},{7,10},{8,15},{9,12},{1... | collective-permute-start | bytes 786440 | tf_op jit(solution)/shard_map/ppermute | solution.py:353
  7.2 0.5 collective-permute-start.1
  7.7 17.9 %all_to_all.10 = f32[128,1,128]{2,1,0:T(1,128)S(1)} all-to-all(f32[128,1,128]{2,1,0:T(1,128)S(1)} %get-tuple-element.15), channel_id=1, replica_groups=mesh['tm'=32,'band'=4] {'tm','band'}, dimensions={0} | all-to-all | bytes 131072 | tf_op jit(solution)/shard_map/all_to_all | solution.py:375
  25.6 0.0 collective-permute-done.2.refs_8_
  25.6 0.0 collective-permute-done.1.refs_7_
  25.6 0.0 collective-permute-done.refs_6_
  25.6 0.0 copy-done
  25.6 0.0 copy-done.4
  25.6 0.0 copy-done.5
  25.6 0.0 copy-done.6
  25.6 0.0 copy-done.7
  25.6 0.0 copy-done.8
  25.6 8.3 %shard_map.93 = (bf16[2,9,128,256]{3,2,1,0:T(8,128)(2,1)S(1)}, bf16[2,128,256]{2,1,0:T(8,128)(2,1)S(1)}, bf16[2,4,128,256]{3,2,1,0:T(8,128)(2,1)S(1)}, s32[8,128]{1,0:T(8,128)S(1)}) custom-call(bf16[3456,256]{1,0:T(8,128)(2,1)S(1)} %bitcast.10, s32[1,64]{1,0:T(1,128)S(1)} %bitcast.21, f32[128,128]{1,0:T(8,128)S(1)} %bitcast.15, f32[1,128]{1,0:T(1,128)S(1)} %bitcast.22, ...), custom_call_target="tpu_custom_call" | custom-call | flops 5368709120 | bytes 8388608 | tf_op jit(solution)/shard_map/pallas_call | solution.py:392
  34.0 1.3 %collective-permute-start.5 = (bf16[2,4,128,256]{3,2,1,0:T(8,128)(2,1)S(1)}, bf16[2,4,128,256]{3,2,1,0:T(8,128)(2,1)S(1)}, u32[]{:S(2)}, u32[]{:S(2)}) collective-permute-start(bf16[2,4,128,256]{3,2,1,0:T(8,128)(2,1)S(1)} %get-tuple-element.22), channel_id=1, source_target_pairs={{4,8},{12,16},{20,24},{28,32},{36,40},{44,48},{52,56},{60,64},{68,... | collective-permute-start | bytes 1572872 | tf_op jit(solution)/shard_map/ppermute | solution.py:357
  35.3 0.2 shard_map.94
  35.5 0.5 collective-permute-start.4
  36.0 0.0 collective-permute-start.3
  36.0 1.3 %collective-permute-start.6 = (bf16[2,4,128,256]{3,2,1,0:T(8,128)(2,1)S(1)}, bf16[2,4,128,256]{3,2,1,0:T(8,128)(2,1)S(1)}, u32[]{:S(2)}, u32[]{:S(2)}) collective-permute-start(bf16[2,4,128,256]{3,2,1,0:T(8,128)(2,1)S(1)} %shard_map.98), channel_id=1, source_target_pairs={{0,4},{8,12},{16,20},{24,28},{32,36},{40,44},{48,52},{56,60},{64,6... | collective-permute-start | bytes 1572872 | tf_op jit(solution)/shard_map/ppermute | solution.py:361
  37.3 1.7 %shard_map.96.local_ref = f32[2,4,128,256]{3,2,1,0:T(8,128)S(1)} custom-call(s32[8,128]{1,0:T(8,128)S(1)} %get-tuple-element.17.info_ref, bf16[2,9,128,256]{3,2,1,0:T(8,128)(2,1)S(1)} %get-tuple-element.20.first_core_ref.residual_ref, bf16[2,9,128,256]{3,2,1,0:T(8,128)(2,1)S(1)} %get-tuple-element.21.second_core_ref, bf16[3456,256]{1,0:T(8,128)(2,1)S(1)} %bitcast.12), custom_call_target="tpu_custom_call" | custom-call | flops 2147483648 | bytes 4194304 | tf_op jit(solution)/shard_map/pallas_call | solution.py:421
  38.9 2.7 %collective-permute-done.4.edge_ref = bf16[2,128,256]{2,1,0:T(8,128)(2,1)S(1)} collective-permute-done((bf16[2,128,256]{2,1,0:T(8,128)(2,1)S(1)}, bf16[2,128,256]{2,1,0:T(8,128)(2,1)S(1)}, u32[]{:S(2)}, u32[]{:S(2)}) %collective-permute-start.4) | collective-permute-done | bytes 131104 | tf_op jit(solution)/shard_map/ppermute | solution.py:353
  41.7 1.6 %collective-permute-done.3.edge_before_ref = bf16[2,128,256]{2,1,0:T(8,128)(2,1)S(1)} collective-permute-done((bf16[2,128,256]{2,1,0:T(8,128)(2,1)S(1)}, bf16[2,128,256]{2,1,0:T(8,128)(2,1)S(1)}, u32[]{:S(2)}, u32[]{:S(2)}) %collective-permute-start.3) | collective-permute-done | bytes 131104 | tf_op jit(solution)/shard_map/ppermute | solution.py:353
  43.3 0.4 shard_map.95.upper_ref
  43.6 0.0 collective-permute-done.5.between_ref
  43.7 0.0 copy-start.1
  43.7 0.0 copy-start.2
  43.7 0.0 collective-permute-done.6.within_ref
  43.7 0.5 shard_map.99
  44.2 15.1 %all_to_all.11 = f32[128,1,128]{2,1,0:T(1,128)S(1)} all-to-all(f32[128,1,128]{2,1,0:T(1,128)S(1)} %get-tuple-element.23), channel_id=1, replica_groups=mesh['tm'=32,'band'=4] {'tm','band'}, dimensions={0} | all-to-all | bytes 131072 | tf_op jit(solution)/shard_map/all_to_all | solution.py:375
  59.3 0.0 copy-done.1
  59.3 0.0 copy-done.2
  59.3 1.1 %shard_map.100 = bf16[2,4,128,256]{3,2,1,0:T(8,128)(2,1)} custom-call(f32[128,128]{1,0:T(8,128)S(1)} %bitcast.14, s32[8,128]{1,0:T(8,128)S(1)} %get-tuple-element.17.info_ref, f32[1,256]{1,0:T(1,128)S(1)} %bitcast.17, f32[1,256]{1,0:T(1,128)S(1)} %bitcast.18, bf16[2,4,128,256]{3,2,1,0:T(8,128)(2,1)S(1)} %get-tuple-element.24.reduced_ref), custom_call_target="tpu_custom_call" | custom-call | bytes 1048576 | tf_op jit(solution)/shard_map/pallas_call | solution.py:441
  (3 shorter events, 0.1 us)
Async XLA Ops:
  0.0 3.0 %copy-start.3 = (bf16[2,8,256,128]{3,2,1,0:T(8,128)(2,1)S(1)}, bf16[2,8,256,128]{3,2,1,0:T(8,128)(2,1)}, u32[]{:S(2)}) copy-start(bf16[2,8,256,128]{3,2,1,0:T(8,128)(2,1)} %refs_5_.3) | copy-start | bytes 3145732
  0.0 25.6 %collective-permute-start = (bf16[2,8,256,128]{3,2,1,0:T(8,128)(2,1)}, bf16[2,8,256,128]{3,2,1,0:T(8,128)(2,1)S(1)}, u32[]{:S(2)}, u32[]{:S(2)}) collective-permute-start(bf16[2,8,256,128]{3,2,1,0:T(8,128)(2,1)} %refs_5_.3), channel_id=1, source_target_pairs={{0,4},{1,5},{2,6},{3,7},{4,8},{5,9},{6,10},{7,11},{8,12},{9,13},{1... | collective-permute-start | bytes 3145736 | tf_op jit(solution)/shard_map/ppermute | solution.py:353
  3.1 22.5 %copy-start = (bf16[3,3,3,128,256]{4,3,2,1,0:T(8,128)(2,1)S(1)}, bf16[3,3,3,128,256]{4,3,2,1,0:T(8,128)(2,1)}, u32[]{:S(2)}) copy-start(bf16[3,3,3,128,256]{4,3,2,1,0:T(8,128)(2,1)} %param.15) | copy-start | bytes 5308420
  3.1 22.5 %copy-start.4 = (bf16[3,3,3,128,128]{4,3,2,1,0:T(8,128)(2,1)S(1)}, bf16[3,3,3,128,128]{4,3,2,1,0:T(8,128)(2,1)}, u32[]{:S(2)}) copy-start(bf16[3,3,3,128,128]{4,3,2,1,0:T(8,128)(2,1)} %param.11) | copy-start | bytes 2654212
  3.1 22.5 %copy-start.5 = (s32[64]{0:T(128)S(1)}, s32[64]{0:T(128)}, u32[]{:S(2)}) copy-start(s32[64]{0:T(128)} %param.10) | copy-start | bytes 772
  3.1 22.5 %copy-start.6 = (f32[128]{0:T(128)S(1)}, f32[128]{0:T(128)}, u32[]{:S(2)}) copy-start(f32[128]{0:T(128)} %param.12) | copy-start | bytes 1540
  3.1 22.5 %copy-start.7 = (f32[128]{0:T(128)S(1)}, f32[128]{0:T(128)}, u32[]{:S(2)}) copy-start(f32[128]{0:T(128)} %param.13) | copy-start | bytes 1540
  3.1 22.5 %copy-start.8 = (f32[128]{0:T(128)S(1)}, f32[128]{0:T(128)}, u32[]{:S(2)}) copy-start(f32[128]{0:T(128)} %param.14) | copy-start | bytes 1540
  3.5 22.1 %collective-permute-start.2 = (bf16[2,2,256,128]{3,2,1,0:T(8,128)(2,1)S(1)}, bf16[2,2,256,128]{3,2,1,0:T(8,128)(2,1)S(1)}, u32[]{:S(2)}, u32[]{:S(2)}) collective-permute-start(bf16[2,2,256,128]{3,2,1,0:T(8,128)(2,1)S(1)} %get-tuple-element.16), channel_id=1, source_target_pairs={{0,7},{1,4},{2,5},{3,6},{4,11},{5,8},{6,9},{7,10},{8,15},{9,12},{1... | collective-permute-start | bytes 786440 | tf_op jit(solution)/shard_map/ppermute | solution.py:353
  7.2 18.4 %collective-permute-start.1 = (bf16[2,2,256,128]{3,2,1,0:T(8,128)(2,1)S(1)}, bf16[2,2,256,128]{3,2,1,0:T(8,128)(2,1)S(1)}, u32[]{:S(2)}, u32[]{:S(2)}) collective-permute-start(bf16[2,2,256,128]{3,2,1,0:T(8,128)(2,1)S(1)} %get-tuple-element.16), channel_id=1, source_target_pairs={{0,3},{1,0},{2,1},{3,2},{4,7},{5,4},{6,5},{7,6},{8,11},{9,8},{10,9... | collective-permute-start | bytes 786440 | tf_op jit(solution)/shard_map/ppermute | solution.py:353
  34.0 9.7 %collective-permute-start.5 = (bf16[2,4,128,256]{3,2,1,0:T(8,128)(2,1)S(1)}, bf16[2,4,128,256]{3,2,1,0:T(8,128)(2,1)S(1)}, u32[]{:S(2)}, u32[]{:S(2)}) collective-permute-start(bf16[2,4,128,256]{3,2,1,0:T(8,128)(2,1)S(1)} %get-tuple-element.22), channel_id=1, source_target_pairs={{4,8},{12,16},{20,24},{28,32},{36,40},{44,48},{52,56},{60,64},{68,... | collective-permute-start | bytes 1572872 | tf_op jit(solution)/shard_map/ppermute | solution.py:357
  35.5 6.2 %collective-permute-start.4 = (bf16[2,128,256]{2,1,0:T(8,128)(2,1)S(1)}, bf16[2,128,256]{2,1,0:T(8,128)(2,1)S(1)}, u32[]{:S(2)}, u32[]{:S(2)}) collective-permute-start(bf16[2,128,256]{2,1,0:T(8,128)(2,1)S(1)} %get-tuple-element.19), channel_id=1, source_target_pairs={{0,1},{1,2},{2,3},{3,0},{4,5},{5,6},{6,7},{7,4},{8,9},{9,10},{10,1... | collective-permute-start | bytes 393224 | tf_op jit(solution)/shard_map/ppermute | solution.py:353
  36.0 7.3 %collective-permute-start.3 = (bf16[2,128,256]{2,1,0:T(8,128)(2,1)S(1)}, bf16[2,128,256]{2,1,0:T(8,128)(2,1)S(1)}, u32[]{:S(2)}, u32[]{:S(2)}) collective-permute-start(bf16[2,128,256]{2,1,0:T(8,128)(2,1)S(1)} %get-tuple-element.19), channel_id=1, source_target_pairs={{0,5},{1,6},{2,7},{3,4},{4,9},{5,10},{6,11},{7,8},{8,13},{9,14},{1... | collective-permute-start | bytes 393224 | tf_op jit(solution)/shard_map/ppermute | solution.py:353
  36.0 7.7 %collective-permute-start.6 = (bf16[2,4,128,256]{3,2,1,0:T(8,128)(2,1)S(1)}, bf16[2,4,128,256]{3,2,1,0:T(8,128)(2,1)S(1)}, u32[]{:S(2)}, u32[]{:S(2)}) collective-permute-start(bf16[2,4,128,256]{3,2,1,0:T(8,128)(2,1)S(1)} %shard_map.98), channel_id=1, source_target_pairs={{0,4},{8,12},{16,20},{24,28},{32,36},{40,44},{48,52},{56,60},{64,6... | collective-permute-start | bytes 1572872 | tf_op jit(solution)/shard_map/ppermute | solution.py:361
  43.7 15.6 %copy-start.1 = (f32[256]{0:T(256)S(1)}, f32[256]{0:T(256)}, u32[]{:S(2)}) copy-start(f32[256]{0:T(256)} %param.16) | copy-start | bytes 3076
  43.7 15.6 %copy-start.2 = (f32[256]{0:T(256)S(1)}, f32[256]{0:T(256)}, u32[]{:S(2)}) copy-start(f32[256]{0:T(256)} %param.17) | copy-start | bytes 3076

commit v5 on v4

--- a/solution.py
+++ b/solution.py
@@ -93,13 +93,19 @@
     row_ref[...] = jnp.broadcast_to(pack_row(sums, gather_ref[...])[None], row_ref.shape)
 
 
-def arrange(weight_ref, weights):
+def arrange(weight_ref, weights, pairs):
     channels = weight_ref.shape[2]
     zero = jnp.zeros((channels, channels), BF16)
     for tap in range(9):
         w0, w1, w2 = (weight_ref[tap, dx] for dx in range(3))
-        weights[tap, 0:channels] = cat([w1, w0, zero, w2], axis=1)
-        weights[tap, channels : 2 * channels] = cat([w2, w1, w0, zero], axis=1)
+        weights[tap, 0:channels] = cat([w1, w0], axis=1)
+        weights[tap, channels : 2 * channels] = cat([w2, w1], axis=1)
+    for side in range(2):
+        for k in range(3):
+            w0, w1, w2 = (weight_ref[k * 3 + dy, 2 * side] for dy in range(3))
+            for j, blocks in enumerate(((w0, zero), (w1, w0), (w2, w1), (zero, w2))):
+                at = (k * 4 + j) * channels
+                pairs[side, at : at + channels] = cat(blocks, axis=1)
 
 
 def clip_table(clip_ref, first):
@@ -119,26 +125,46 @@
     return u + u * jnp.tanh(u)
 
 
-def convolve(line, weights_ref, outputs):
-    weights = weights_ref[...].reshape(-1, weights_ref.shape[2])
-    window = cat(
-        [
-            cat([line(sources[k], r, dy) for sources, r in outputs], axis=0)
-            for k in range(3)
-            for dy in (-1, 0, 1)
-        ],
-        axis=1,
-    )
-    found = jnp.dot(window, weights, preferred_element_type=F32)
-    wide = found.shape[1] // 2
+def convolve(line, weight_ref, weights, pairs, sources, rows):
+    wide = weights.shape[2]
     channels = wide // 2
-    size = found.shape[0]
-    half = size // len(outputs)
-    column = iota((size, channels), 0) % half
-    from_left = jnp.where(column == 0, 0.0, pltpu.roll(found[:, wide : wide + channels], 1, 0))
-    from_right = jnp.where(column == half - 1, 0.0, pltpu.roll(found[:, wide + channels :], size - 1, 0))
-    total = found[:, :wide] + cat([from_left, from_right], axis=1)
-    return [total[n * half : (n + 1) * half] for n in range(len(outputs))]
+    taps = [(k, dy) for k in range(3) for dy in (-1, 0, 1)]
+    dot = functools.partial(jnp.dot, preferred_element_type=F32)
+
+    def window(picked, lanes):
+        return cat(
+            [cat([line(sources[k], r, dy)[:, lanes] for r in picked], axis=0) for k, dy in taps], axis=1
+        )
+
+    total = dot(window(range(1, rows + 1), slice(0, wide)), weights[...].reshape(-1, wide))
+    half = total.shape[0] // rows
+    firsts, singles = range(1, rows - 2, 2), (rows - 1, rows)
+    crossing = [[] for _ in range(rows)]
+    for side in range(2):
+        lanes = slice(channels, wide) if side == 0 else slice(0, channels)
+        four = cat(
+            [
+                cat([line(sources[k], r + j // 3, min(j, 2) - 1)[:, lanes] for r in firsts], axis=0)
+                for k in range(3)
+                for j in range(4)
+            ],
+            axis=1,
+        )
+        alone = cat([weight_ref[tap, 2 * side] for tap in range(9)], axis=0)
+        by_two, by_one = dot(four, pairs[side]), dot(window(singles, lanes), alone)
+        shift = from_left if side == 0 else from_right
+        by_two, by_one = shift(by_two, half), shift(by_one, half)
+        for n in range(rows - 2):
+            at = n // 2 * half
+            crossing[n].append(by_two[at : at + half, n % 2 * channels : (n % 2 + 1) * channels])
+        for n in range(2):
+            crossing[rows - 2 + n].append(by_one[n * half : (n + 1) * half])
+    return [total[n * half : (n + 1) * half] + cat(crossing[n], axis=1) for n in range(rows)]
+
+
+def from_left(value, half):
+    column = iota(value.shape, 0) % half
+    return jnp.where(column == 0, 0.0, pltpu.roll(value, 1, 0))
 
 
 def from_right(value, half):
@@ -218,12 +244,12 @@
 def convolve_frames(
     bands, cells, info_ref, rows_ref, bias_ref, gain_ref, offset_ref, weight_ref,
     x_ref, before_ref, below_ref, below_before_ref,
-    residual_ref, edge_ref, hidden, own, weights, slots,
+    residual_ref, edge_ref, hidden, own, weights, pairs, slots,
 ):
     rows, cols, channels = x_ref.shape[1:]
     first = lax.axis_index("tm") * 2
     keep = (lax.axis_index("band") < bands - 1).astype(F32)
-    arrange(weight_ref, weights)
+    arrange(weight_ref, weights, pairs)
     bias = bias_ref[...]
     stats = scale_and_shift(rows_ref[...], info_ref, gain_ref[...], offset_ref[...], cells, bands)
     stats = [0.5 * v for pair in stats for v in pair]
@@ -252,7 +278,7 @@
     sources = frame_sources(info_ref, first)
     bias = cat([bias, bias], axis=1)
     for f in range(2):
-        found = convolve(line, weights, [(sources[f], r) for r in range(1, rows + 1)])
+        found = convolve(line, weight_ref, weights, pairs, sources[f], rows)
         for n, total in enumerate(found):
             value = total + own[f, n].astype(F32) + bias
             residual_ref[f, n] = value.astype(BF16)
@@ -396,7 +422,8 @@
             scratch=[
                 pltpu.VMEM((4, rows + 4, *pair), BF16),
                 pltpu.VMEM((frames, rows, *pair), BF16),
-                pltpu.VMEM((9, 2 * channels, 4 * channels), BF16),
+                pltpu.VMEM((9, 2 * channels, 2 * channels), BF16),
+                pltpu.VMEM((2, 12 * channels, 2 * channels), BF16),
                 pltpu.VMEM((rows + 2, cols, channels), F32),
             ],
             megabytes=24,

time: 60.6 us -> 60.1 us (level)
  no operation moved by 1% of the time
where the time goes in v5:
time: 60.1 us; the launch traced here: 59.9 us
  blocking collectives  33 us (55%)
  Pallas kernels  12 us (20%)
  starting transfers between devices  10.2 us (17%)
  waiting for transfers between devices  4.37 us (7%)
    all_to_all x2, blocking collectives, exchange(): lax.all_to_all(row, ('tm', 'band'), 0, 0, tiled=True).reshape(devices, 128)  33 us
    pallas_call x2, Pallas kernels, conv(): call(functools.partial(kernel, bands, cells), (shape((frames, rows + 1, *...  8.05 us
    ppermute x5, starting transfers between devices, passed_on(): return lax.ppermute(array, ('tm', 'band'), pairs)  7.64 us
    ppermute x5, waiting for transfers between devices, passed_on(): return lax.ppermute(array, ('tm', 'band'), pairs)  4.36 us
    pallas_call x1, Pallas kernels, on_device(): call(local_kernel, shape((frames, lines, half, wide), F32), [VMEM] * 4, m...  1.64 us
    ppermute x1, starting transfers between devices, between_chips(): lax.ppermute(array, 'tm', [(i, i + 1) for i in range(1, lax.axis_size('tm...  1.32 us
    ppermute x1, starting transfers between devices, within_chips(): lax.ppermute(array, 'tm', [(i, i + 1) for i in range(0, lax.axis_size('tm...  1.28 us
  transfers between devices with their start and end apart: 7, of which 2 were waited for; matrix products, arithmetic and copies ran while one was open for 0% of the time, Pallas kernels for 4%

profile of v5, /device:TPU:1, one launch (start us, length us, event | category | flops | bytes accessed | tf_op | source)
XLA Modules:
  0.0 59.9 jit_solution(2633418009936089426)
XLA Ops:
  0.0 0.0 copy-start.3
  0.0 3.0 %collective-permute-start = (bf16[2,8,256,128]{3,2,1,0:T(8,128)(2,1)}, bf16[2,8,256,128]{3,2,1,0:T(8,128)(2,1)S(1)}, u32[]{:S(2)}, u32[]{:S(2)}) collective-permute-start(bf16[2,8,256,128]{3,2,1,0:T(8,128)(2,1)} %refs_5_.3), channel_id=1, source_target_pairs={{0,4},{1,5},{2,6},{3,7},{4,8},{5,9},{6,10},{7,11},{8,12},{9,13},{1... | collective-permute-start | bytes 3145736 | tf_op jit(solution)/shard_map/ppermute | solution.py:379
  3.0 0.0 copy-done.3
  3.1 0.0 copy-start
  3.1 0.0 copy-start.4
  3.1 0.0 copy-start.5
  3.1 0.0 copy-start.6
  3.1 0.0 copy-start.7
  3.1 0.0 copy-start.8
  3.1 0.4 shard_map.92
  3.5 3.7 %collective-permute-start.2 = (bf16[2,2,256,128]{3,2,1,0:T(8,128)(2,1)S(1)}, bf16[2,2,256,128]{3,2,1,0:T(8,128)(2,1)S(1)}, u32[]{:S(2)}, u32[]{:S(2)}) collective-permute-start(bf16[2,2,256,128]{3,2,1,0:T(8,128)(2,1)S(1)} %get-tuple-element.16), channel_id=1, source_target_pairs={{0,7},{1,4},{2,5},{3,6},{4,11},{5,8},{6,9},{7,10},{8,15},{9,12},{1... | collective-permute-start | bytes 786440 | tf_op jit(solution)/shard_map/ppermute | solution.py:379
  7.2 0.5 collective-permute-start.1
  7.7 17.9 %all_to_all.10 = f32[128,1,128]{2,1,0:T(1,128)S(1)} all-to-all(f32[128,1,128]{2,1,0:T(1,128)S(1)} %get-tuple-element.15), channel_id=1, replica_groups=mesh['tm'=32,'band'=4] {'tm','band'}, dimensions={0} | all-to-all | bytes 131072 | tf_op jit(solution)/shard_map/all_to_all | solution.py:401
  25.6 0.0 collective-permute-done.2.refs_8_
  25.6 0.0 collective-permute-done.1.refs_7_
  25.6 0.0 collective-permute-done.refs_6_
  25.6 0.0 copy-done
  25.6 0.0 copy-done.4
  25.6 0.0 copy-done.5
  25.6 0.0 copy-done.6
  25.6 0.0 copy-done.7
  25.6 0.0 copy-done.8
  25.6 7.8 %shard_map.93 = (bf16[2,9,128,256]{3,2,1,0:T(8,128)(2,1)S(1)}, bf16[2,128,256]{2,1,0:T(8,128)(2,1)S(1)}, bf16[2,4,128,256]{3,2,1,0:T(8,128)(2,1)S(1)}, s32[8,128]{1,0:T(8,128)S(1)}) custom-call(bf16[3456,256]{1,0:T(8,128)(2,1)S(1)} %bitcast.10, s32[1,64]{1,0:T(1,128)S(1)} %bitcast.21, f32[128,128]{1,0:T(8,128)S(1)} %bitcast.15, f32[1,128]{1,0:T(1,128)S(1)} %bitcast.22, ...), custom_call_target="tpu_custom_call" | custom-call | flops 5368709120 | bytes 8388608 | tf_op jit(solution)/shard_map/pallas_call | solution.py:418
  33.5 1.3 %collective-permute-start.5 = (bf16[2,4,128,256]{3,2,1,0:T(8,128)(2,1)S(1)}, bf16[2,4,128,256]{3,2,1,0:T(8,128)(2,1)S(1)}, u32[]{:S(2)}, u32[]{:S(2)}) collective-permute-start(bf16[2,4,128,256]{3,2,1,0:T(8,128)(2,1)S(1)} %get-tuple-element.22), channel_id=1, source_target_pairs={{4,8},{12,16},{20,24},{28,32},{36,40},{44,48},{52,56},{60,64},{68,... | collective-permute-start | bytes 1572872 | tf_op jit(solution)/shard_map/ppermute | solution.py:383
  34.8 0.2 shard_map.94
  35.0 0.5 collective-permute-start.4
  35.5 0.0 collective-permute-start.3
  35.5 1.3 %collective-permute-start.6 = (bf16[2,4,128,256]{3,2,1,0:T(8,128)(2,1)S(1)}, bf16[2,4,128,256]{3,2,1,0:T(8,128)(2,1)S(1)}, u32[]{:S(2)}, u32[]{:S(2)}) collective-permute-start(bf16[2,4,128,256]{3,2,1,0:T(8,128)(2,1)S(1)} %shard_map.98), channel_id=1, source_target_pairs={{0,4},{8,12},{16,20},{24,28},{32,36},{40,44},{48,52},{56,60},{64,6... | collective-permute-start | bytes 1572872 | tf_op jit(solution)/shard_map/ppermute | solution.py:387
  36.8 1.6 %shard_map.96.local_ref = f32[2,4,128,256]{3,2,1,0:T(8,128)S(1)} custom-call(s32[8,128]{1,0:T(8,128)S(1)} %get-tuple-element.17.info_ref, bf16[2,9,128,256]{3,2,1,0:T(8,128)(2,1)S(1)} %get-tuple-element.20.first_core_ref.residual_ref, bf16[2,9,128,256]{3,2,1,0:T(8,128)(2,1)S(1)} %get-tuple-element.21.second_core_ref, bf16[3456,256]{1,0:T(8,128)(2,1)S(1)} %bitcast.12), custom_call_target="tpu_custom_call" | custom-call | flops 2147483648 | bytes 4194304 | tf_op jit(solution)/shard_map/pallas_call | solution.py:448
  38.4 2.6 %collective-permute-done.4.edge_ref = bf16[2,128,256]{2,1,0:T(8,128)(2,1)S(1)} collective-permute-done((bf16[2,128,256]{2,1,0:T(8,128)(2,1)S(1)}, bf16[2,128,256]{2,1,0:T(8,128)(2,1)S(1)}, u32[]{:S(2)}, u32[]{:S(2)}) %collective-permute-start.4) | collective-permute-done | bytes 131104 | tf_op jit(solution)/shard_map/ppermute | solution.py:379
  41.0 1.8 %collective-permute-done.3.edge_before_ref = bf16[2,128,256]{2,1,0:T(8,128)(2,1)S(1)} collective-permute-done((bf16[2,128,256]{2,1,0:T(8,128)(2,1)S(1)}, bf16[2,128,256]{2,1,0:T(8,128)(2,1)S(1)}, u32[]{:S(2)}, u32[]{:S(2)}) %collective-permute-start.3) | collective-permute-done | bytes 131104 | tf_op jit(solution)/shard_map/ppermute | solution.py:379
  42.8 0.3 shard_map.95.upper_ref
  43.1 0.0 collective-permute-done.5.between_ref
  43.2 0.0 copy-start.1
  43.2 0.0 copy-start.2
  43.2 0.0 collective-permute-done.6.within_ref
  43.2 0.5 shard_map.99
  43.7 15.1 %all_to_all.11 = f32[128,1,128]{2,1,0:T(1,128)S(1)} all-to-all(f32[128,1,128]{2,1,0:T(1,128)S(1)} %get-tuple-element.23), channel_id=1, replica_groups=mesh['tm'=32,'band'=4] {'tm','band'}, dimensions={0} | all-to-all | bytes 131072 | tf_op jit(solution)/shard_map/all_to_all | solution.py:401
  58.8 0.0 copy-done.1
  58.8 0.0 copy-done.2
  58.8 1.1 %shard_map.100 = bf16[2,4,128,256]{3,2,1,0:T(8,128)(2,1)} custom-call(f32[128,128]{1,0:T(8,128)S(1)} %bitcast.14, s32[8,128]{1,0:T(8,128)S(1)} %get-tuple-element.17.info_ref, f32[1,256]{1,0:T(1,128)S(1)} %bitcast.17, f32[1,256]{1,0:T(1,128)S(1)} %bitcast.18, bf16[2,4,128,256]{3,2,1,0:T(8,128)(2,1)S(1)} %get-tuple-element.24.reduced_ref), custom_call_target="tpu_custom_call" | custom-call | bytes 1048576 | tf_op jit(solution)/shard_map/pallas_call | solution.py:468
  (3 shorter events, 0.1 us)
Async XLA Ops:
  0.0 3.0 %copy-start.3 = (bf16[2,8,256,128]{3,2,1,0:T(8,128)(2,1)S(1)}, bf16[2,8,256,128]{3,2,1,0:T(8,128)(2,1)}, u32[]{:S(2)}) copy-start(bf16[2,8,256,128]{3,2,1,0:T(8,128)(2,1)} %refs_5_.3) | copy-start | bytes 3145732
  0.0 25.6 %collective-permute-start = (bf16[2,8,256,128]{3,2,1,0:T(8,128)(2,1)}, bf16[2,8,256,128]{3,2,1,0:T(8,128)(2,1)S(1)}, u32[]{:S(2)}, u32[]{:S(2)}) collective-permute-start(bf16[2,8,256,128]{3,2,1,0:T(8,128)(2,1)} %refs_5_.3), channel_id=1, source_target_pairs={{0,4},{1,5},{2,6},{3,7},{4,8},{5,9},{6,10},{7,11},{8,12},{9,13},{1... | collective-permute-start | bytes 3145736 | tf_op jit(solution)/shard_map/ppermute | solution.py:379
  3.1 22.5 %copy-start = (bf16[3,3,3,128,256]{4,3,2,1,0:T(8,128)(2,1)S(1)}, bf16[3,3,3,128,256]{4,3,2,1,0:T(8,128)(2,1)}, u32[]{:S(2)}) copy-start(bf16[3,3,3,128,256]{4,3,2,1,0:T(8,128)(2,1)} %param.15) | copy-start | bytes 5308420
  3.1 22.5 %copy-start.4 = (bf16[3,3,3,128,128]{4,3,2,1,0:T(8,128)(2,1)S(1)}, bf16[3,3,3,128,128]{4,3,2,1,0:T(8,128)(2,1)}, u32[]{:S(2)}) copy-start(bf16[3,3,3,128,128]{4,3,2,1,0:T(8,128)(2,1)} %param.11) | copy-start | bytes 2654212
  3.1 22.5 %copy-start.5 = (s32[64]{0:T(128)S(1)}, s32[64]{0:T(128)}, u32[]{:S(2)}) copy-start(s32[64]{0:T(128)} %param.10) | copy-start | bytes 772
  3.1 22.5 %copy-start.6 = (f32[128]{0:T(128)S(1)}, f32[128]{0:T(128)}, u32[]{:S(2)}) copy-start(f32[128]{0:T(128)} %param.12) | copy-start | bytes 1540
  3.1 22.5 %copy-start.7 = (f32[128]{0:T(128)S(1)}, f32[128]{0:T(128)}, u32[]{:S(2)}) copy-start(f32[128]{0:T(128)} %param.13) | copy-start | bytes 1540
  3.1 22.5 %copy-start.8 = (f32[128]{0:T(128)S(1)}, f32[128]{0:T(128)}, u32[]{:S(2)}) copy-start(f32[128]{0:T(128)} %param.14) | copy-start | bytes 1540
  3.5 22.1 %collective-permute-start.2 = (bf16[2,2,256,128]{3,2,1,0:T(8,128)(2,1)S(1)}, bf16[2,2,256,128]{3,2,1,0:T(8,128)(2,1)S(1)}, u32[]{:S(2)}, u32[]{:S(2)}) collective-permute-start(bf16[2,2,256,128]{3,2,1,0:T(8,128)(2,1)S(1)} %get-tuple-element.16), channel_id=1, source_target_pairs={{0,7},{1,4},{2,5},{3,6},{4,11},{5,8},{6,9},{7,10},{8,15},{9,12},{1... | collective-permute-start | bytes 786440 | tf_op jit(solution)/shard_map/ppermute | solution.py:379
  7.2 18.4 %collective-permute-start.1 = (bf16[2,2,256,128]{3,2,1,0:T(8,128)(2,1)S(1)}, bf16[2,2,256,128]{3,2,1,0:T(8,128)(2,1)S(1)}, u32[]{:S(2)}, u32[]{:S(2)}) collective-permute-start(bf16[2,2,256,128]{3,2,1,0:T(8,128)(2,1)S(1)} %get-tuple-element.16), channel_id=1, source_target_pairs={{0,3},{1,0},{2,1},{3,2},{4,7},{5,4},{6,5},{7,6},{8,11},{9,8},{10,9... | collective-permute-start | bytes 786440 | tf_op jit(solution)/shard_map/ppermute | solution.py:379
  33.5 9.7 %collective-permute-start.5 = (bf16[2,4,128,256]{3,2,1,0:T(8,128)(2,1)S(1)}, bf16[2,4,128,256]{3,2,1,0:T(8,128)(2,1)S(1)}, u32[]{:S(2)}, u32[]{:S(2)}) collective-permute-start(bf16[2,4,128,256]{3,2,1,0:T(8,128)(2,1)S(1)} %get-tuple-element.22), channel_id=1, source_target_pairs={{4,8},{12,16},{20,24},{28,32},{36,40},{44,48},{52,56},{60,64},{68,... | collective-permute-start | bytes 1572872 | tf_op jit(solution)/shard_map/ppermute | solution.py:383
  35.0 6.0 %collective-permute-start.4 = (bf16[2,128,256]{2,1,0:T(8,128)(2,1)S(1)}, bf16[2,128,256]{2,1,0:T(8,128)(2,1)S(1)}, u32[]{:S(2)}, u32[]{:S(2)}) collective-permute-start(bf16[2,128,256]{2,1,0:T(8,128)(2,1)S(1)} %get-tuple-element.19), channel_id=1, source_target_pairs={{0,1},{1,2},{2,3},{3,0},{4,5},{5,6},{6,7},{7,4},{8,9},{9,10},{10,1... | collective-permute-start | bytes 393224 | tf_op jit(solution)/shard_map/ppermute | solution.py:379
  35.5 7.3 %collective-permute-start.3 = (bf16[2,128,256]{2,1,0:T(8,128)(2,1)S(1)}, bf16[2,128,256]{2,1,0:T(8,128)(2,1)S(1)}, u32[]{:S(2)}, u32[]{:S(2)}) collective-permute-start(bf16[2,128,256]{2,1,0:T(8,128)(2,1)S(1)} %get-tuple-element.19), channel_id=1, source_target_pairs={{0,5},{1,6},{2,7},{3,4},{4,9},{5,10},{6,11},{7,8},{8,13},{9,14},{1... | collective-permute-start | bytes 393224 | tf_op jit(solution)/shard_map/ppermute | solution.py:379
  35.5 7.7 %collective-permute-start.6 = (bf16[2,4,128,256]{3,2,1,0:T(8,128)(2,1)S(1)}, bf16[2,4,128,256]{3,2,1,0:T(8,128)(2,1)S(1)}, u32[]{:S(2)}, u32[]{:S(2)}) collective-permute-start(bf16[2,4,128,256]{3,2,1,0:T(8,128)(2,1)S(1)} %shard_map.98), channel_id=1, source_target_pairs={{0,4},{8,12},{16,20},{24,28},{32,36},{40,44},{48,52},{56,60},{64,6... | collective-permute-start | bytes 1572872 | tf_op jit(solution)/shard_map/ppermute | solution.py:387
  43.2 15.6 %copy-start.1 = (f32[256]{0:T(256)S(1)}, f32[256]{0:T(256)}, u32[]{:S(2)}) copy-start(f32[256]{0:T(256)} %param.16) | copy-start | bytes 3076
  43.2 15.6 %copy-start.2 = (f32[256]{0:T(256)S(1)}, f32[256]{0:T(256)}, u32[]{:S(2)}) copy-start(f32[256]{0:T(256)} %param.17) | copy-start | bytes 3076

commit v6 on v5

--- a/solution.py
+++ b/solution.py
@@ -317,7 +317,7 @@
         out_ref[1] += strided(residual_ref, (begins[1] - first,), down_ref, 0)[0]
 
 
-def row_zero_kernel(info_ref, edge_before_ref, edge_ref, down_ref, out_ref, four):
+def row_zero_kernel(info_ref, edge_ref, edge_before_ref, down_ref, out_ref, four):
     half, wide = edge_ref.shape[1:]
     four[0:2] = edge_before_ref[...]
     four[2:4] = edge_ref[...]
@@ -456,7 +456,7 @@
     line = shape((frames, half, wide), F32)
     upper = call(
         row_zero_kernel, line, [VMEM] * 4, scratch=[pltpu.VMEM((4, *pair), BF16)], megabytes=6
-    )(info, edge_before, edge, down)
+    )(info, edge, edge_before, down)
     first_line = call(first_line_kernel, line, [VMEM] * 3, flops=1 << 32)(upper, local, between)
     reduced, row = call(
         join_kernel,

time: 60.1 us -> 60.2 us (level)
  waiting for transfers between devices: 4.37 us -> 3.46 us
  Pallas kernels: 12 us -> 12.9 us
    ppermute x5, waiting for transfers between devices: 4.36 us -> 3.45 us  [passed_on(): return lax.ppermute(array, ('tm', 'band'), pairs)]
    pallas_call x1, Pallas kernels: 1.64 us -> 2.44 us  [on_device(): call(local_kernel, shape((frames, lines, half, wide), F32), [VMEM] * 4, m...]
  transfers between devices with their start and end apart: 7 -> 7, of which waited for: 2 -> 2; matrix products, arithmetic and copies ran while one was open for 0% -> 0% of each run, Pallas kernels for 4% -> 6%
where the time goes in v6:
time: 60.2 us; the launch traced here: 60 us
  blocking collectives  33.1 us (55%)
  Pallas kernels  12.9 us (21%)
  starting transfers between devices  10.3 us (17%)
  waiting for transfers between devices  3.46 us (6%)
    all_to_all x2, blocking collectives, exchange(): lax.all_to_all(row, ('tm', 'band'), 0, 0, tiled=True).reshape(devices, 128)  33.1 us
    pallas_call x2, Pallas kernels, conv(): call(functools.partial(kernel, bands, cells), (shape((frames, rows + 1, *...  8.05 us
    ppermute x5, starting transfers between devices, passed_on(): return lax.ppermute(array, ('tm', 'band'), pairs)  7.71 us
    ppermute x5, waiting for transfers between devices, passed_on(): return lax.ppermute(array, ('tm', 'band'), pairs)  3.45 us
    pallas_call x1, Pallas kernels, on_device(): call(local_kernel, shape((frames, lines, half, wide), F32), [VMEM] * 4, m...  2.44 us
    ppermute x1, starting transfers between devices, between_chips(): lax.ppermute(array, 'tm', [(i, i + 1) for i in range(1, lax.axis_size('tm...  1.32 us
    ppermute x1, starting transfers between devices, within_chips(): lax.ppermute(array, 'tm', [(i, i + 1) for i in range(0, lax.axis_size('tm...  1.28 us
  transfers between devices with their start and end apart: 7, of which 2 were waited for; matrix products, arithmetic and copies ran while one was open for 0% of the time, Pallas kernels for 6%

profile of v6, /device:TPU:1, one launch (start us, length us, event | category | flops | bytes accessed | tf_op | source)
XLA Modules:
  0.0 60.0 jit_solution(2206368530540112066)
XLA Ops:
  0.0 0.0 copy-start.3
  0.0 3.0 %collective-permute-start = (bf16[2,8,256,128]{3,2,1,0:T(8,128)(2,1)}, bf16[2,8,256,128]{3,2,1,0:T(8,128)(2,1)S(1)}, u32[]{:S(2)}, u32[]{:S(2)}) collective-permute-start(bf16[2,8,256,128]{3,2,1,0:T(8,128)(2,1)} %refs_5_.3), channel_id=1, source_target_pairs={{0,4},{1,5},{2,6},{3,7},{4,8},{5,9},{6,10},{7,11},{8,12},{9,13},{1... | collective-permute-start | bytes 3145736 | tf_op jit(solution)/shard_map/ppermute | solution.py:379
  3.0 0.0 copy-done.3
  3.1 0.0 copy-start
  3.1 0.0 copy-start.4
  3.1 0.0 copy-start.5
  3.1 0.0 copy-start.6
  3.1 0.0 copy-start.7
  3.1 0.0 copy-start.8
  3.1 0.4 shard_map.92
  3.5 3.7 %collective-permute-start.2 = (bf16[2,2,256,128]{3,2,1,0:T(8,128)(2,1)S(1)}, bf16[2,2,256,128]{3,2,1,0:T(8,128)(2,1)S(1)}, u32[]{:S(2)}, u32[]{:S(2)}) collective-permute-start(bf16[2,2,256,128]{3,2,1,0:T(8,128)(2,1)S(1)} %get-tuple-element.16), channel_id=1, source_target_pairs={{0,7},{1,4},{2,5},{3,6},{4,11},{5,8},{6,9},{7,10},{8,15},{9,12},{1... | collective-permute-start | bytes 786440 | tf_op jit(solution)/shard_map/ppermute | solution.py:379
  7.2 0.5 collective-permute-start.1
  7.7 17.9 %all_to_all.10 = f32[128,1,128]{2,1,0:T(1,128)S(1)} all-to-all(f32[128,1,128]{2,1,0:T(1,128)S(1)} %get-tuple-element.15), channel_id=1, replica_groups=mesh['tm'=32,'band'=4] {'tm','band'}, dimensions={0} | all-to-all | bytes 131072 | tf_op jit(solution)/shard_map/all_to_all | solution.py:401
  25.6 0.0 collective-permute-done.2.refs_8_
  25.6 0.0 collective-permute-done.1.refs_7_
  25.6 0.0 collective-permute-done.refs_6_
  25.6 0.0 copy-done
  25.6 0.0 copy-done.4
  25.6 0.0 copy-done.5
  25.6 0.0 copy-done.6
  25.6 0.0 copy-done.7
  25.6 0.0 copy-done.8
  25.6 7.8 %shard_map.93 = (bf16[2,9,128,256]{3,2,1,0:T(8,128)(2,1)S(1)}, bf16[2,128,256]{2,1,0:T(8,128)(2,1)S(1)}, bf16[2,4,128,256]{3,2,1,0:T(8,128)(2,1)S(1)}, s32[8,128]{1,0:T(8,128)S(1)}) custom-call(bf16[3456,256]{1,0:T(8,128)(2,1)S(1)} %bitcast.10, s32[1,64]{1,0:T(1,128)S(1)} %bitcast.21, f32[128,128]{1,0:T(8,128)S(1)} %bitcast.15, f32[1,128]{1,0:T(1,128)S(1)} %bitcast.22, ...), custom_call_target="tpu_custom_call" | custom-call | flops 5368709120 | bytes 8388608 | tf_op jit(solution)/shard_map/pallas_call | solution.py:418
  33.5 1.3 %collective-permute-start.5 = (bf16[2,4,128,256]{3,2,1,0:T(8,128)(2,1)S(1)}, bf16[2,4,128,256]{3,2,1,0:T(8,128)(2,1)S(1)}, u32[]{:S(2)}, u32[]{:S(2)}) collective-permute-start(bf16[2,4,128,256]{3,2,1,0:T(8,128)(2,1)S(1)} %get-tuple-element.22), channel_id=1, source_target_pairs={{4,8},{12,16},{20,24},{28,32},{36,40},{44,48},{52,56},{60,64},{68,... | collective-permute-start | bytes 1572872 | tf_op jit(solution)/shard_map/ppermute | solution.py:383
  34.8 0.2 shard_map.94
  35.0 0.1 collective-permute-start.4
  35.1 0.5 collective-permute-start.3
  35.6 1.3 %collective-permute-start.6 = (bf16[2,4,128,256]{3,2,1,0:T(8,128)(2,1)S(1)}, bf16[2,4,128,256]{3,2,1,0:T(8,128)(2,1)S(1)}, u32[]{:S(2)}, u32[]{:S(2)}) collective-permute-start(bf16[2,4,128,256]{3,2,1,0:T(8,128)(2,1)S(1)} %shard_map.98), channel_id=1, source_target_pairs={{0,4},{8,12},{16,20},{24,28},{32,36},{40,44},{48,52},{56,60},{64,6... | collective-permute-start | bytes 1572872 | tf_op jit(solution)/shard_map/ppermute | solution.py:387
  36.9 2.4 %shard_map.96.local_ref = f32[2,4,128,256]{3,2,1,0:T(8,128)S(1)} custom-call(s32[8,128]{1,0:T(8,128)S(1)} %get-tuple-element.17.info_ref, bf16[2,9,128,256]{3,2,1,0:T(8,128)(2,1)S(1)} %get-tuple-element.20.first_core_ref.residual_ref, bf16[2,9,128,256]{3,2,1,0:T(8,128)(2,1)S(1)} %get-tuple-element.21.second_core_ref, bf16[3456,256]{1,0:T(8,128)(2,1)S(1)} %bitcast.12), custom_call_target="tpu_custom_call" | custom-call | flops 2147483648 | bytes 4194304 | tf_op jit(solution)/shard_map/pallas_call | solution.py:448
  39.3 3.1 %collective-permute-done.4.edge_before_ref = bf16[2,128,256]{2,1,0:T(8,128)(2,1)S(1)} collective-permute-done((bf16[2,128,256]{2,1,0:T(8,128)(2,1)S(1)}, bf16[2,128,256]{2,1,0:T(8,128)(2,1)S(1)}, u32[]{:S(2)}, u32[]{:S(2)}) %collective-permute-start.4) | collective-permute-done | bytes 131104 | tf_op jit(solution)/shard_map/ppermute | solution.py:379
  42.4 0.3 collective-permute-done.3.edge_ref
  42.8 0.4 shard_map.95.upper_ref
  43.1 0.0 collective-permute-done.5.between_ref
  43.2 0.0 copy-start.1
  43.2 0.0 copy-start.2
  43.2 0.0 collective-permute-done.6.within_ref
  43.2 0.5 shard_map.99
  43.7 15.2 %all_to_all.11 = f32[128,1,128]{2,1,0:T(1,128)S(1)} all-to-all(f32[128,1,128]{2,1,0:T(1,128)S(1)} %get-tuple-element.23), channel_id=1, replica_groups=mesh['tm'=32,'band'=4] {'tm','band'}, dimensions={0} | all-to-all | bytes 131072 | tf_op jit(solution)/shard_map/all_to_all | solution.py:401
  58.9 0.0 copy-done.1
  58.9 0.0 copy-done.2
  58.9 1.1 %shard_map.100 = bf16[2,4,128,256]{3,2,1,0:T(8,128)(2,1)} custom-call(f32[128,128]{1,0:T(8,128)S(1)} %bitcast.14, s32[8,128]{1,0:T(8,128)S(1)} %get-tuple-element.17.info_ref, f32[1,256]{1,0:T(1,128)S(1)} %bitcast.17, f32[1,256]{1,0:T(1,128)S(1)} %bitcast.18, bf16[2,4,128,256]{3,2,1,0:T(8,128)(2,1)S(1)} %get-tuple-element.24.reduced_ref), custom_call_target="tpu_custom_call" | custom-call | bytes 1048576 | tf_op jit(solution)/shard_map/pallas_call | solution.py:468
  (3 shorter events, 0.1 us)
Async XLA Ops:
  0.0 3.0 %copy-start.3 = (bf16[2,8,256,128]{3,2,1,0:T(8,128)(2,1)S(1)}, bf16[2,8,256,128]{3,2,1,0:T(8,128)(2,1)}, u32[]{:S(2)}) copy-start(bf16[2,8,256,128]{3,2,1,0:T(8,128)(2,1)} %refs_5_.3) | copy-start | bytes 3145732
  0.0 25.6 %collective-permute-start = (bf16[2,8,256,128]{3,2,1,0:T(8,128)(2,1)}, bf16[2,8,256,128]{3,2,1,0:T(8,128)(2,1)S(1)}, u32[]{:S(2)}, u32[]{:S(2)}) collective-permute-start(bf16[2,8,256,128]{3,2,1,0:T(8,128)(2,1)} %refs_5_.3), channel_id=1, source_target_pairs={{0,4},{1,5},{2,6},{3,7},{4,8},{5,9},{6,10},{7,11},{8,12},{9,13},{1... | collective-permute-start | bytes 3145736 | tf_op jit(solution)/shard_map/ppermute | solution.py:379
  3.1 22.5 %copy-start = (bf16[3,3,3,128,256]{4,3,2,1,0:T(8,128)(2,1)S(1)}, bf16[3,3,3,128,256]{4,3,2,1,0:T(8,128)(2,1)}, u32[]{:S(2)}) copy-start(bf16[3,3,3,128,256]{4,3,2,1,0:T(8,128)(2,1)} %param.15) | copy-start | bytes 5308420
  3.1 22.5 %copy-start.4 = (bf16[3,3,3,128,128]{4,3,2,1,0:T(8,128)(2,1)S(1)}, bf16[3,3,3,128,128]{4,3,2,1,0:T(8,128)(2,1)}, u32[]{:S(2)}) copy-start(bf16[3,3,3,128,128]{4,3,2,1,0:T(8,128)(2,1)} %param.11) | copy-start | bytes 2654212
  3.1 22.5 %copy-start.5 = (s32[64]{0:T(128)S(1)}, s32[64]{0:T(128)}, u32[]{:S(2)}) copy-start(s32[64]{0:T(128)} %param.10) | copy-start | bytes 772
  3.1 22.5 %copy-start.6 = (f32[128]{0:T(128)S(1)}, f32[128]{0:T(128)}, u32[]{:S(2)}) copy-start(f32[128]{0:T(128)} %param.12) | copy-start | bytes 1540
  3.1 22.5 %copy-start.7 = (f32[128]{0:T(128)S(1)}, f32[128]{0:T(128)}, u32[]{:S(2)}) copy-start(f32[128]{0:T(128)} %param.13) | copy-start | bytes 1540
  3.1 22.5 %copy-start.8 = (f32[128]{0:T(128)S(1)}, f32[128]{0:T(128)}, u32[]{:S(2)}) copy-start(f32[128]{0:T(128)} %param.14) | copy-start | bytes 1540
  3.5 22.1 %collective-permute-start.2 = (bf16[2,2,256,128]{3,2,1,0:T(8,128)(2,1)S(1)}, bf16[2,2,256,128]{3,2,1,0:T(8,128)(2,1)S(1)}, u32[]{:S(2)}, u32[]{:S(2)}) collective-permute-start(bf16[2,2,256,128]{3,2,1,0:T(8,128)(2,1)S(1)} %get-tuple-element.16), channel_id=1, source_target_pairs={{0,7},{1,4},{2,5},{3,6},{4,11},{5,8},{6,9},{7,10},{8,15},{9,12},{1... | collective-permute-start | bytes 786440 | tf_op jit(solution)/shard_map/ppermute | solution.py:379
  7.2 18.4 %collective-permute-start.1 = (bf16[2,2,256,128]{3,2,1,0:T(8,128)(2,1)S(1)}, bf16[2,2,256,128]{3,2,1,0:T(8,128)(2,1)S(1)}, u32[]{:S(2)}, u32[]{:S(2)}) collective-permute-start(bf16[2,2,256,128]{3,2,1,0:T(8,128)(2,1)S(1)} %get-tuple-element.16), channel_id=1, source_target_pairs={{0,3},{1,0},{2,1},{3,2},{4,7},{5,4},{6,5},{7,6},{8,11},{9,8},{10,9... | collective-permute-start | bytes 786440 | tf_op jit(solution)/shard_map/ppermute | solution.py:379
  33.5 9.7 %collective-permute-start.5 = (bf16[2,4,128,256]{3,2,1,0:T(8,128)(2,1)S(1)}, bf16[2,4,128,256]{3,2,1,0:T(8,128)(2,1)S(1)}, u32[]{:S(2)}, u32[]{:S(2)}) collective-permute-start(bf16[2,4,128,256]{3,2,1,0:T(8,128)(2,1)S(1)} %get-tuple-element.22), channel_id=1, source_target_pairs={{4,8},{12,16},{20,24},{28,32},{36,40},{44,48},{52,56},{60,64},{68,... | collective-permute-start | bytes 1572872 | tf_op jit(solution)/shard_map/ppermute | solution.py:383
  35.0 7.4 %collective-permute-start.4 = (bf16[2,128,256]{2,1,0:T(8,128)(2,1)S(1)}, bf16[2,128,256]{2,1,0:T(8,128)(2,1)S(1)}, u32[]{:S(2)}, u32[]{:S(2)}) collective-permute-start(bf16[2,128,256]{2,1,0:T(8,128)(2,1)S(1)} %get-tuple-element.19), channel_id=1, source_target_pairs={{0,5},{1,6},{2,7},{3,4},{4,9},{5,10},{6,11},{7,8},{8,13},{9,14},{1... | collective-permute-start | bytes 393224 | tf_op jit(solution)/shard_map/ppermute | solution.py:379
  35.1 7.7 %collective-permute-start.3 = (bf16[2,128,256]{2,1,0:T(8,128)(2,1)S(1)}, bf16[2,128,256]{2,1,0:T(8,128)(2,1)S(1)}, u32[]{:S(2)}, u32[]{:S(2)}) collective-permute-start(bf16[2,128,256]{2,1,0:T(8,128)(2,1)S(1)} %get-tuple-element.19), channel_id=1, source_target_pairs={{0,1},{1,2},{2,3},{3,0},{4,5},{5,6},{6,7},{7,4},{8,9},{9,10},{10,1... | collective-permute-start | bytes 393224 | tf_op jit(solution)/shard_map/ppermute | solution.py:379
  35.6 7.6 %collective-permute-start.6 = (bf16[2,4,128,256]{3,2,1,0:T(8,128)(2,1)S(1)}, bf16[2,4,128,256]{3,2,1,0:T(8,128)(2,1)S(1)}, u32[]{:S(2)}, u32[]{:S(2)}) collective-permute-start(bf16[2,4,128,256]{3,2,1,0:T(8,128)(2,1)S(1)} %shard_map.98), channel_id=1, source_target_pairs={{0,4},{8,12},{16,20},{24,28},{32,36},{40,44},{48,52},{56,60},{64,6... | collective-permute-start | bytes 1572872 | tf_op jit(solution)/shard_map/ppermute | solution.py:387
  43.2 15.7 %copy-start.1 = (f32[256]{0:T(256)S(1)}, f32[256]{0:T(256)}, u32[]{:S(2)}) copy-start(f32[256]{0:T(256)} %param.16) | copy-start | bytes 3076
  43.2 15.7 %copy-start.2 = (f32[256]{0:T(256)S(1)}, f32[256]{0:T(256)}, u32[]{:S(2)}) copy-start(f32[256]{0:T(256)} %param.17) | copy-start | bytes 3076
